TPU v7x, 32 devices: a whole 2x2x4 slice. The times are simulated.
32 devices in a mesh: row: 4 (over y, core), col: 8 (over z, x).
Axes of the slice: x: 2, y: 2, z: 4, core: 2. Of those that a mesh axis runs over, the one named last changes fastest.
Arguments:
- features: float32 [128, 512, 128], P('row', 'col'), may hold values from -0.4 to 0.4
- step_size: float32 [128, 512, 128], P('row', 'col'), may hold values from 0.5 to 2
- write_weights: float32 [128, 512, 16], P('row', 'col'), may hold values from -6 to 6
- read_weights: float32 [128, 512, 16], P('row', 'col'), may hold values from -6 to 6
- decay_log: float32 [16, 128], replicated, may hold values from -7.6 to -3.5
- out_grad: float32 [128, 512, 128], P('row', 'col'), may hold values from -0.4 to 0.4
Outputs:
- grad_features: float32 [128, 512, 128], P('row', 'col')
- grad_step: float32 [128, 512, 128], P('row', 'col')
- grad_write: float32 [128, 512, 16], P('row', 'col')
- grad_read: float32 [128, 512, 16], P('row', 'col')
- grad_decay: float32 [16, 128], replicated
All inputs are finite; a program needn't handle non-finite values.
Results may differ from a plain program's by a relative error of at most 0.0002.
Values sent between devices are 32-bit elements; how exact they have to be, the bound alone decides.
No kernel may reach another device: no remote copies, remote signals or barrier semaphores. Data moves between devices by JAX's collectives and lax.ppermute only.
A program may use at most 320 MiB of HBM per device.

v0:
```python
import jax
import jax.numpy as jnp
from jax import lax
from jax.sharding import PartitionSpec as P


def carried_in(shard, axis, combine, identity, reverse):
    size, mine = (lax.axis_size(axis), lax.axis_index(axis))
    everything = jax.tree.map(lambda part: lax.all_gather(part, axis), shard)
    start = jax.tree.map(
        lambda part, zero: jnp.broadcast_to(jnp.asarray(zero, part.dtype), part.shape),
        shard,
        identity,
    )

    def lap(k, before):
        at = size - 1 - k if reverse else k
        reached = at > mine if reverse else at < mine
        new = combine(before, jax.tree.map(lambda part: part[at], everything))
        return jax.tree.map(lambda a, b: jnp.where(reached, a, b), new, before)

    return lax.fori_loop(0, size, lap, start)


def sweep_rows(decays, driving, backward):

    def advance(current, inputs):
        factor, source = inputs
        current = factor * current + source
        return (current, current)

    def retreat(passed, inputs):
        factor, source = inputs
        adjoint = source + passed
        return (factor * adjoint, adjoint)

    initial = jnp.zeros(decays.shape[1:], jnp.float32)
    if backward:
        closing, values = lax.scan(retreat, initial, (decays, driving), reverse=True)
    else:
        closing, values = lax.scan(advance, initial, (decays, driving))
    return (values, closing)


def sweep_cols(decays, driving, backward):
    length = decays.shape[1]

    def advance(index, running):
        current, values = running
        place = length - 1 - index if backward else index
        place = jnp.asarray(place).astype(jnp.int32)
        factor = lax.dynamic_index_in_dim(decays, place, 1, keepdims=False)
        source = lax.dynamic_index_in_dim(driving, place, 1, keepdims=False)
        if backward:
            value = source + current
            values = lax.dynamic_update_index_in_dim(values, value, place, 1)
            current = factor * value
        else:
            current = factor * current + source
            values = lax.dynamic_update_index_in_dim(values, current, place, 1)
        return (current, values)

    initial = jnp.zeros(decays.shape[:1] + decays.shape[2:], jnp.float32)
    closing, values = lax.fori_loop(0, length, advance, (initial, jnp.zeros_like(driving)))
    return (values, closing)


def link_parts(final_state, exponent_sum, decay_rate):

    def combine(earlier, subsequent):
        return (earlier[0] * subsequent[0], subsequent[0] * earlier[1] + subsequent[1])

    products = jnp.exp(exponent_sum[:, None, :] * decay_rate)
    element = (products, final_state)
    identity = (jnp.ones_like(products), jnp.zeros_like(final_state))
    return (element, identity, combine)


def shards(features, step_size, write_weights, read_weights, decay_log, out_grad):
    highest = lax.Precision.HIGHEST
    decay_rate = -jnp.exp(decay_log)
    decays = jnp.exp(step_size[:, :, None, :] * decay_rate)
    driving = step_size[:, :, None, :] * write_weights[:, :, :, None] * features[:, :, None, :]
    running_rows = jnp.cumsum(step_size, 0)
    running_cols = jnp.cumsum(step_size, 1)
    sum_rows = running_rows[-1]
    sum_cols = running_cols[:, -1]
    local_rows, leaving_rows = sweep_rows(decays, driving, False)
    element, identity, combine = link_parts(leaving_rows, sum_rows, decay_rate)
    from_above = carried_in(element, "row", combine, identity, False)[1]
    vertical = local_rows + jnp.exp(running_rows[:, :, None, :] * decay_rate) * from_above[None]
    vert_prev = jnp.concatenate([from_above[None], vertical[:-1]], 0)
    local_cols, leaving_cols = sweep_cols(decays, vertical, False)
    element, identity, combine = link_parts(leaving_cols, sum_cols, decay_rate)
    from_left = carried_in(element, "col", combine, identity, False)[1]
    states = local_cols + jnp.exp(running_cols[:, :, None, :] * decay_rate) * from_left[:, None]
    states_prev = jnp.concatenate([from_left[:, None], states[:, :-1]], 1)
    direct = read_weights[:, :, :, None] * out_grad[:, :, None, :]
    adjoint_local, outgoing_cols = sweep_cols(decays, direct, True)
    element, identity, combine = link_parts(outgoing_cols, sum_cols, decay_rate)
    from_right = carried_in(element, "col", combine, identity, True)[1]
    after_cols = sum_cols[:, None, :] - running_cols
    adjoint_h = (
        adjoint_local + jnp.exp(after_cols[:, :, None, :] * decay_rate) * from_right[:, None]
    )
    adjoint_vlocal, outgoing_rows = sweep_rows(decays, adjoint_h, True)
    element, identity, combine = link_parts(outgoing_rows, sum_rows, decay_rate)
    from_below = carried_in(element, "row", combine, identity, True)[1]
    after_rows = sum_rows[None] - running_rows
    adjoint_v = adjoint_vlocal + jnp.exp(after_rows[:, :, None, :] * decay_rate) * from_below[None]
    exponent_grad = (adjoint_h * states_prev + adjoint_v * vert_prev) * decays
    through = jnp.einsum("hwnd,hwn->hwd", adjoint_v, write_weights, precision=highest)
    grad_features = step_size * through
    grad_step = features * through + jnp.einsum(
        "hwnd,nd->hwd", exponent_grad, decay_rate, precision=highest
    )
    grad_write = jnp.einsum("hwnd,hwd->hwn", adjoint_v, step_size * features, precision=highest)
    grad_read = jnp.einsum("hwnd,hwd->hwn", states, out_grad, precision=highest)
    partial_sum = jnp.einsum("hwnd,hwd->nd", exponent_grad, step_size, precision=highest)
    grad_decay = lax.psum(partial_sum, ("row", "col")) * decay_rate
    return (grad_features, grad_step, grad_write, grad_read, grad_decay)


def solution(mesh):
    in_specs = (
        P("row", "col", None),
        P("row", "col", None),
        P("row", "col", None),
        P("row", "col", None),
        P(),
        P("row", "col", None),
    )
    out_specs = (
        P("row", "col", None),
        P("row", "col", None),
        P("row", "col", None),
        P("row", "col", None),
        P(),
    )
    return jax.shard_map(shards, mesh=mesh, in_specs=in_specs, out_specs=out_specs, check_vma=False)
```

profile of v0, /device:TPU:0, one launch (start us, length us, event | category | flops | bytes accessed | tf_op | source)
XLA Modules:
  0.0 915.2 jit_solution(12242600486648841948)
XLA Ops:
  13.7 9.3 %multiply_multiply_fusion = (f32[32,64,16,128]{3,2,0,1:T(8,128)}, f32[32,64,16,128]{3,2,0,1:T(8,128)S(1)}) fusion(f32[32,64,128]{2,0,1:T(8,128)S(1)} %copy.37, f32[32,64,16]{2,0,1:T(8,128)S(1)} %copy.36, f32[32,64,128]{2,0,1:T(8,128)S(1)} %copy.27, f32[16,128]{1,0:T(8,128)S(1)} %exponential_negate_fusion), kind=kLoop, calls=%fused_computation.34 | loop fusion | flops 12582912 | bytes 35790848 | tf_op jit(solution)/shard_map/mul | solution.py:83
  23.0 5.8 copy-done
  28.8 6.2 copy.32
  35.0 7.9 broadcast.59.clone3
  42.8 79.4 %while.128 = (s32[]{:T(128)}, f32[64,16,128]{2,1,0:T(8,128)S(1)}, f32[32,64,16,128]{3,2,0,1:T(8,128)}, f32[32,64,16,128]{3,2,1,0:T(8,128)}, f32[32,64,16,128]{3,2,0,1:T(8,128)}, /*index=5*/s32[]{:T(128)}, s32[]{:T(128)}) while((s32[]{:T(128)}, f32[64,16,128]{2,1,0:T(8,128)S(1)}, f32[32,64,16,128]{3,2,0,1:T(8,128)}, ...), condition=%wide.region_11.12_spmd.clone, body=%wide.region_10.11_spmd.clone.sunk | while | flops 393219 | bytes 2622039 | solution.py:41
  42.8 2.5 bitcast_dynamic-update-slice_fusion.10
  45.3 2.5 bitcast_dynamic-update-slice_fusion.10
  50.3 2.5 bitcast_dynamic-update-slice_fusion.10
  52.8 2.5 bitcast_dynamic-update-slice_fusion.10
  55.3 2.5 bitcast_dynamic-update-slice_fusion.10
  57.8 2.5 bitcast_dynamic-update-slice_fusion.10
  60.3 2.5 bitcast_dynamic-update-slice_fusion.10
  62.7 2.5 bitcast_dynamic-update-slice_fusion.10
  65.2 2.5 bitcast_dynamic-update-slice_fusion.10
  67.7 2.5 bitcast_dynamic-update-slice_fusion.10
  80.1 2.5 bitcast_dynamic-update-slice_fusion.10
  92.5 2.5 bitcast_dynamic-update-slice_fusion.10
  97.4 2.5 bitcast_dynamic-update-slice_fusion.10
  102.4 2.5 bitcast_dynamic-update-slice_fusion.10
  109.8 2.5 bitcast_dynamic-update-slice_fusion.10
  117.2 2.5 bitcast_dynamic-update-slice_fusion.10
  119.7 2.5 bitcast_dynamic-update-slice_fusion.10
  123.1 4.0 fusion.18
  134.1 7.5 broadcast_multiply_fusion
  141.6 7.8 broadcast.59.clone3.2
  149.5 186.1 %while.124 = (s32[]{:T(128)}, f32[32,16,128]{2,1,0:T(8,128)S(1)}, f32[32,64,16,128]{3,2,0,1:T(8,128)}, f32[32,64,16,128]{3,2,0,1:T(8,128)}, f32[32,64,16,128]{3,...) while((s32[]{:T(128)}, f32[32,16,128]{2,1,0:T(8,128)S(1)}, ...), condition=%wide.region_1.2_spmd.clone, body=%wide.region_0.0_spmd.clone.sunk | while | flops 327687 | bytes 1835166 | solution.py:64
  338.4 6.7 while.129
  345.1 12.4 %multiply_add_fusion.1 = f32[32,64,16,128]{3,2,0,1:T(8,128)} fusion(f32[32,64,16,128]{3,2,0,1:T(8,128)} %get-tuple-element.823, f32[64,16,128]{2,1,0:T(8,128)S(1)} %get-tuple-element.825, f32[32,64,128]{2,0,1:T(8,128)} %copy.41, f32[16,128]{1,0:T(8,128)S(1)} %exponential_negate_fusion), kind=kLoop, calls=%fused_computation.33 | loop fusion | flops 12582912 | bytes 35135488 | tf_op jit(solution)/shard_map/add | solution.py:91
  357.5 7.9 broadcast.59.clone3.1
  365.3 124.9 %while.130 = (s32[]{:T(128)}, f32[32,16,128]{2,1,0:T(8,128)S(1)}, f32[32,64,16,128]{3,2,0,1:T(8,128)}, f32[32,64,16,128]{3,2,0,1:T(8,128)}, f32[32,64,16,128]{3,2,0,1:T(8,128)}, /*index=5*/s32[]{:T(128)}, s32[]{:T(128)}) while((s32[]{:T(128)}, f32[32,16,128]{2,1,0:T(8,128)S(1)}, f32[32,64,16,128]{3,2,0,1:T(8,128)}, ...), condition=%wide.region_15.16_spmd.clone, body=%wide.region_14.15_spmd.clone.sunk | while | flops 196611 | bytes 1311319 | solution.py:64
  493.3 14.9 %while.125 = (s32[]{:T(128)}, f32[32,16,128]{2,1,0:T(8,128)}, s32[]{:T(128)}, f32[8,32,16,128]{3,2,1,0:T(8,128)}, f32[8,32,16,128]{3,2,1,0:T(8,128)}, /*index=5*/s32[]{:T(128)}, s32[]{:T(128)}, s32[]{:T(128)}, s32[]{:T(128)}) while((s32[]{:T(128)}, f32[32,16,128]{2,1,0:T(8,128)}, s32[]{:T(128)}, f32[8,32,16,128]{3,2,1,0:T(8,128)}, ...), condition=%wide.region_4.5_spmd.clone, body=%wide.region_3.4_spmd.clone.sunk | while | flops 262152 | bytes 1048739 | solution.py:22
  508.2 34.8 %all-gather.21.cloned.1.call-done = f32[256,16,128]{2,1,0:T(8,128)} async-done(((f32[32,16,128]{2,1,0:T(8,128)}), f32[256,16,128]{2,1,0:T(8,128)}) %all-gather.21.cloned.1.call-update) | async-done | bytes 2097168 | tf_op jit(solution)/shard_map/all_gather | solution.py:9
  543.0 10.2 %while.131 = (s32[]{:T(128)}, f32[32,16,128]{2,1,0:T(8,128)S(1)}, s32[]{:T(128)}, f32[8,32,16,128]{3,2,1,0:T(8,128)}, f32[8,32,16,128]{3,2,1,0:T(8,128)}, /*index=5*/s32[]{:T(128)}, s32[]{:T(128)}) while((s32[]{:T(128)}, f32[32,16,128]{2,1,0:T(8,128)S(1)}, s32[]{:T(128)}, f32[8,32,16,128]{3,2,1,0:T(8,128)}, ...), condition=%wide.region_17.18_spmd.clone, body=%wide.region_16.17_spmd.clone.sunk | while | flops 262148 | bytes 1048677 | solution.py:22
  553.1 23.2 %multiply_add_fusion = (f32[32,64,16,128]{3,2,0,1:T(8,128)}, f32[32,64,16,128]{3,2,0,1:T(8,128)}) fusion(f32[32,64,16,128]{3,2,0,1:T(8,128)} %get-tuple-element.828, f32[32,16,128]{2,1,0:T(8,128)S(1)} %get-tuple-element.827, f32[32,64,128]{2,0,1:T(8,128)} %copy-done.5, f32[16,128]{1,0:T(8,128)S(1)} %exponential_negate_fusion, ...), kind=kLoop, calls=%fused_computation.32 | loop fusion | flops 25165824 | bytes 69738496 | tf_op jit(solution)/shard_map/add | solution.py:96
  576.3 7.8 broadcast.59.clone2
  584.2 112.9 %while.126 = (s32[]{:T(128)}, f32[64,16,128]{2,1,0:T(8,128)S(1)}, f32[32,64,16,128]{3,2,0,1:T(8,128)}, f32[32,64,16,128]{3,2,1,0:T(8,128)}, f32[32,64,16,128]{3,...) while((s32[]{:T(128)}, f32[64,16,128]{2,1,0:T(8,128)S(1)}, f32[32,64,16,128]{3,2,0,1:T(8,128)}, ...), condition=%wide.region_6.7_spmd.clone, body=%wide.region_5.6_spmd.clone.sunk | while | flops 655364 | bytes 3670132 | solution.py:39
  701.1 2.9 copy.44
  704.0 11.4 %slice.19 = f32[31,64,16,128]{3,2,0,1:T(8,128)} slice(f32[32,64,16,128]{3,2,0,1:T(8,128)} %get-tuple-element.1542), slice={[0:31], [0:64], [0:16], [0:128]} | slice | bytes 32505856 | tf_op jit(solution)/shard_map/slice | solution.py:92
  715.5 13.7 %slice.18 = f32[32,63,16,128]{3,2,0,1:T(8,128)} slice(f32[32,64,16,128]{3,2,0,1:T(8,128)} %get-tuple-element.1087), slice={[0:32], [0:63], [0:16], [0:128]} | slice | bytes 33030144 | tf_op jit(solution)/shard_map/slice | solution.py:97
  732.4 27.4 %fusion.6 = f32[32,64,1,16]{3,2,1,0:T(1,128)} fusion(f32[32,64,128,1]{2,3,1,0:T(1,128)S(1)} %bitcast.158, f32[32,64,16,128]{3,2,0,1:T(8,128)S(1)} %bitcast.152), kind=kOutput, calls=%fused_computation.29 | convolution fusion | flops 50331648 | bytes 17956864 | tf_op jit(solution)/shard_map/hwnd,hwd->hwn/dot_general | solution.py:118
  759.8 2.9 copy.57
  762.8 6.7 while.127
  769.5 34.6 %multiply_reduce_fusion = (f32[128,16]{0,1:T(8,128)S(1)}, f32[32,64,16,128]{3,2,0,1:T(8,128)}, f32[32,64,16,128]{3,2,0,1:T(8,128)}) fusion(f32[128,32,64]{0,1,2:T(8,128)} %copy.74, f32[16,128]{1,0:T(8,128)S(1)} %exponential_negate_fusion, f32[32,64,128]{2,0,1:T(8,128)S(1)} %copy-done.7, f32[31,64,16,128]{3,2,0,1:T(8,128)} %slice.19, ...), kind=kLoop, calls=%fused_computation.28 | loop fusion | flops 50329600 | bytes 104349696 | tf_op jit(solution)/shard_map/hwnd,hwd->nd/dot_general | solution.py:119
  804.1 39.6 %psum.7 = f32[16,128]{1,0:T(8,128)S(1)} all-reduce(f32[16,128]{1,0:T(8,128)S(1)} %bitcast.166), channel_id=1, replica_groups=mesh['row'=4,'col'=8] {'row','col'}, use_global_device_ids=true, to_apply=%region_18.19 | all-reduce | flops 2048 | bytes 16384 | tf_op jit(solution)/shard_map/psum | solution.py:120
  844.3 18.2 %fusion.10 = f32[32,64,1,128]{3,2,1,0:T(1,128)S(1)} fusion(f32[32,64,16,1]{2,3,1,0:T(1,128)} %copy.44, f32[32,64,16,128]{3,2,0,1:T(8,128)} %get-tuple-element.1079), kind=kOutput, calls=%fused_computation.40 | convolution fusion | flops 50331648 | bytes 17956864 | tf_op jit(solution)/shard_map/hwnd,hwn->hwd/dot_general | solution.py:112
  862.5 10.9 %multiply_reduce_fusion.1 = f32[128,32,64]{0,1,2:T(8,128)} fusion(f32[32,64,16,128]{3,2,0,1:T(8,128)} %get-tuple-element.1078, f32[128,16]{0,1:T(8,128)S(1)} %get-tuple-element.1086), kind=kLoop, calls=%fused_computation.31 | loop fusion | flops 8126464 | bytes 17833984
  873.4 3.6 fusion.17
  877.1 28.9 %fusion.8 = f32[32,64,1,16]{3,2,1,0:T(1,128)S(1)} fusion(f32[32,64,128,1]{2,3,1,0:T(1,128)S(1)} %bitcast.157, f32[32,64,16,128]{3,2,0,1:T(8,128)} %get-tuple-element.1079), kind=kOutput, calls=%fused_computation.38 | convolution fusion | flops 50331648 | bytes 17956864 | tf_op jit(solution)/shard_map/hwnd,hwd->hwn/dot_general | solution.py:117
  (370 shorter events, 526.8 us)
Async XLA Ops:
  7.2 331.2 %all-gather.19.cloned.1.call-start = ((), (), s32[]{:S(2)}) async-start(), calls=%async_computation.4 | async-start | bytes 2621440 | tf_op jit(solution)/shard_map/all_gather | solution.py:9
  9.8 13.2 %copy-start.6 = (f32[32,64,128]{2,0,1:T(8,128)}, f32[32,64,128]{2,0,1:T(8,128)S(1)}, u32[]{:S(2)}) copy-start(f32[32,64,128]{2,0,1:T(8,128)S(1)} %copy.27) | copy-start | bytes 3145732
  23.0 5.8 copy-start
  35.0 88.1 %copy-start.3 = (f32[32,64,128]{2,1,0:T(8,128)S(1)}, f32[32,64,128]{2,1,0:T(8,128)}, u32[]{:S(2)}) copy-start(f32[32,64,128]{2,1,0:T(8,128)} %param.23) | copy-start | bytes 3145732
  35.0 95.5 %copy-start.10 = (f32[32,64,16]{1,2,0:T(8,128)S(1)}, f32[32,64,16]{1,2,0:T(8,128)}, u32[]{:S(2)}) copy-start(f32[32,64,16]{1,2,0:T(8,128)} %param.25) | copy-start | bytes 393220
  122.2 0.8 copy-start.4
  123.0 215.4 %all-gather.13.cloned.1.call-start = ((), (), s32[]{:S(2)}) async-start(), calls=%async_computation.1 | async-start | bytes 2621440 | tf_op jit(solution)/shard_map/all_gather | solution.py:9
  128.0 365.3 %all-gather.11.cloned.1.call-start = ((), (), s32[]{:S(2)}) async-start(), calls=%async_computation | async-start | bytes 2359296 | tf_op jit(solution)/shard_map/all_gather | solution.py:9
  128.7 1.0 copy-start.5
  130.4 362.9 %all-gather.15.cloned.1.call-start = ((), (), s32[]{:S(2)}) async-start(), calls=%async_computation.2 | async-start | bytes 2359296 | tf_op jit(solution)/shard_map/all_gather | solution.py:9
  335.6 0.7 copy-start.2
  336.3 206.7 %all-gather.21.cloned.1.call-start = ((), (), s32[]{:S(2)}) async-start(), calls=%async_computation.5 | async-start | bytes 2359296 | tf_op jit(solution)/shard_map/all_gather | solution.py:9
  490.3 0.7 copy-start.8
  491.0 271.8 %all-gather.17.cloned.1.call-start = ((), (), s32[]{:S(2)}) async-start(), calls=%async_computation.3 | async-start | bytes 2621440 | tf_op jit(solution)/shard_map/all_gather | solution.py:9
  697.0 0.8 copy-start.1
  715.5 13.7 %slice-start = ((s8[16777216]{0:T(1024)(128)(4,1)}), s8[4194304]{0:T(1024)(128)(4,1)S(1)}, s32[]{:S(2)}) async-start(s8[16777216]{0:T(1024)(128)(4,1)} %bitcast.151), calls=%async_computation.6 | async-start | bytes 8388608
  715.5 13.7 %copy-start.9 = (f32[32,64,128]{2,1,0:T(8,128)S(1)}, f32[32,64,128]{2,1,0:T(8,128)}, u32[]{:S(2)}) copy-start(f32[32,64,128]{2,1,0:T(8,128)} %param.27) | copy-start | bytes 3145732
  715.5 14.1 %slice-start.1 = ((s8[16777216]{0:T(1024)(128)(4,1)}), s8[4194304]{0:T(1024)(128)(4,1)S(1)}, s32[]{:S(2)}) async-start(s8[16777216]{0:T(1024)(128)(4,1)} %bitcast.151), calls=%async_computation.7 | async-start | bytes 8388608
  715.5 15.8 %slice-start.2 = ((s8[16777216]{0:T(1024)(128)(4,1)}), s8[4194304]{0:T(1024)(128)(4,1)S(1)}, s32[]{:S(2)}) async-start(s8[16777216]{0:T(1024)(128)(4,1)} %bitcast.151), calls=%async_computation.8 | async-start | bytes 8388608
  715.5 16.9 %slice-start.3 = ((s8[16777216]{0:T(1024)(128)(4,1)}), s8[4194304]{0:T(1024)(128)(4,1)S(1)}, s32[]{:S(2)}) async-start(s8[16777216]{0:T(1024)(128)(4,1)} %bitcast.151), calls=%async_computation.9 | async-start | bytes 8388608
  732.4 37.1 %copy-start.7 = (f32[32,64,128]{2,0,1:T(8,128)S(1)}, f32[32,64,128]{2,0,1:T(8,128)}, u32[]{:S(2)}) copy-start(f32[32,64,128]{2,0,1:T(8,128)} %copy-done.6) | copy-start | bytes 3145732
  769.5 74.2 %copy-start.11 = (f32[16,128]{1,0:T(8,128)S(1)}, f32[16,128]{1,0:T(8,128)}, u32[]{:S(2)}) copy-start(f32[16,128]{1,0:T(8,128)} %param.26) | copy-start | bytes 24580
Sparse Core Ops, SparseCore 0:
  123.1 25.2 all-gather.18
  150.0 22.5 all-gather.12
  175.4 49.2 all-gather.10
  336.4 51.9 all-gather.14
  491.1 51.8 all-gather.20
  698.0 21.0 all-gather.16
where the time goes:
time: 931 us; the launch traced here: 915 us
  other arithmetic  651 us (70%)
  local copies, waits for them, and re-layouts  97.6 us (10%)
  matrix products  74.5 us (8%)
  blocking collectives  39.6 us (4%)
  waiting for transfers between devices  34.9 us (4%)
  between operations  14.8 us (2%)
    dynamic_update_slice x64, other arithmetic, sweep_rows(): closing, values = lax.scan(advance, initial, (decays, driving))  142 us
    dynamic_update_slice x64, other arithmetic, advance(): values = lax.dynamic_update_index_in_dim(values, current, place, 1)  125 us
    dynamic_update_slice x64, other arithmetic, advance(): values = lax.dynamic_update_index_in_dim(values, value, place, 1)  108 us
    mul x64, other arithmetic, advance(): current = factor * value  76.2 us
    mul x32, other arithmetic, retreat(): return (factor * adjoint, adjoint)  49.2 us
    psum x1, blocking collectives, shards(): grad_decay = lax.psum(partial_sum, ('row', 'col')) * decay_rate  39.6 us
    select_n x24, other arithmetic, lap(): return jax.tree.map(lambda a, b: jnp.where(reached, a, b), new, before)  38.1 us
    all_gather x6, waiting for transfers between devices, carried_in(): everything = jax.tree.map(lambda part: lax.all_gather(part, axis), shard)  34.8 us
  transfers between devices with their start and end apart: 6, of which 1 were waited for; matrix products, arithmetic and copies ran while one was open for 48% of the time, Pallas kernels for 0%

commit v1 on v0

v1 whole, which is shorter than its diff:
```python
import functools

import jax
import jax.numpy as jnp
import numpy as np
from jax import lax
from jax.experimental import pallas as pl
from jax.experimental.pallas import tpu as pltpu
from jax.sharding import PartitionSpec as P

HS, WS, BI, BJ = 8, 16, 4, 4
POS = BI * BJ
LANES = 128
D = 128
F32 = jnp.float32
BF16 = jnp.bfloat16
LOG2E = 1.4426950408889634
LN2 = 0.6931471805599453


def lane_matrices():
    lane = np.arange(LANES)
    hs, ws = lane // WS, lane % WS
    same_w = ws[:, None] == ws[None]
    same_h = hs[:, None] == hs[None]
    above = same_w & (hs[:, None] < hs[None])
    below = same_w & (hs[:, None] > hs[None])
    left = same_h & (ws[:, None] < ws[None])
    right = same_h & (ws[:, None] > ws[None])
    rows_out = np.stack([
        np.stack([(g * 64 + j * WS + ws)[:, None] == lane[None] for j in range(BJ)])
        for g in range(2)
    ])
    cols_out = np.stack([
        np.stack([(g * 32 + i * HS + hs)[:, None] == lane[None] for i in range(BI)])
        for g in range(4)
    ])
    rows_in = np.swapaxes(rows_out, -1, -2)
    cols_in = np.swapaxes(cols_out, -1, -2)

    def twice(m):
        return jnp.asarray(np.concatenate([m, m], -2).astype(np.float32), BF16)

    return {
        "above": twice(above), "below": twice(below), "left": twice(left), "right": twice(right),
        "rows_out": twice(rows_out), "cols_out": twice(cols_out),
        "rows_in": twice(rows_in), "cols_in": twice(cols_in),
    }


def halves(x):
    high = x.astype(BF16)
    low = (x - high.astype(F32)).astype(BF16)
    return high, low


def lane_dot(x, matrix):
    return jnp.dot(jnp.concatenate(halves(x), 1), matrix, preferred_element_type=F32)


def lane_dot_exact(x, matrix):
    high, low = halves(x)
    rest = (x - high.astype(F32) - low.astype(F32)).astype(BF16)
    return jnp.dot(
        jnp.concatenate([high, low], 1), matrix, preferred_element_type=F32
    ) + jnp.dot(rest, matrix[:LANES], preferred_element_type=F32)


def gather_place(ref, i, j):
    return jnp.concatenate(
        [ref[hs * BI + i, pl.ds(j, WS, stride=BJ), :] for hs in range(HS)], 0
    )


def row_of(ref, p, n):
    return jnp.broadcast_to(ref[p, pl.ds(n, 1), :], (8, LANES))


def forward_rows_kernel(
    step, feat, write, rates, rates_pk, above, left, rows_out, cols_out,
    step_p, source_p, write_p, cum_rows, cum_cols, sum_rows, sum_cols, seg, leaving,
):
    states = rates.shape[0]
    for i in range(BI):
        for j in range(BJ):
            p = i * BJ + j
            s = gather_place(step, i, j).T
            step_p[p] = s
            source_p[p] = s * gather_place(feat, i, j).T
            write_p[p] = gather_place(write, i, j).T
    total = jnp.zeros((64, LANES), F32)
    for j in range(BJ):
        run = [step_p[j]]
        for i in range(1, BI):
            run.append(run[-1] + step_p[i * BJ + j])
        before = lane_dot_exact(run[-1], above[...])
        for i in range(BI):
            cum_rows[i * BJ + j] = before + run[i]
        for g in range(2):
            total += lane_dot_exact(run[-1][g * 64 : g * 64 + 64], rows_out[g, j])
    sum_rows[...] = total
    total = jnp.zeros((32, LANES), F32)
    for i in range(BI):
        run = [step_p[i * BJ]]
        for j in range(1, BJ):
            run.append(run[-1] + step_p[i * BJ + j])
        before = lane_dot_exact(run[-1], left[...])
        for j in range(BJ):
            cum_cols[i * BJ + j] = before + run[j]
        for g in range(4):
            total += lane_dot_exact(run[-1][g * 32 : g * 32 + 32], cols_out[g, i])
    sum_cols[...] = total

    def group(at, carry):
        d = pl.ds(pl.multiple_of((at // (states // 4)) * 8, 8), 8)
        for k in range(4):
            n = (at % (states // 4)) * 4 + k
            r = -rates[n, d]
            for j in range(BJ):
                acc = None
                for i in range(BI):
                    p = i * BJ + j
                    term = jnp.exp2(cum_rows[p, d] * r) * source_p[p, d] * row_of(write_p, p, n)
                    acc = term if acc is None else acc + term
                seg[n, j, d] = acc
        return carry

    lax.fori_loop(0, D // 8 * (states // 4), group, 0)

    for j in range(BJ):
        for g in range(2):
            part = seg[:, j, g * 64 : g * 64 + 64, :].reshape(states * 64, LANES)
            out = lane_dot(part, rows_out[g, j]).reshape(states, 64, LANES)
            if j == 0 and g == 0:
                leaving[...] = out
            else:
                leaving[...] += out
    for n in range(states):
        leaving[n] = leaving[n] * jnp.exp2(rates_pk[n] * sum_rows[...])


def adjoint_cols_kernel(
    grad, read, rates, cum_cols, cols_out, grad_p, read_p, seg, leaving,
):
    states = rates.shape[0]
    for i in range(BI):
        for j in range(BJ):
            p = i * BJ + j
            grad_p[p] = gather_place(grad, i, j).T
            read_p[p] = gather_place(read, i, j).T

    def group(at, carry):
        d = pl.ds(pl.multiple_of((at // (states // 4)) * 8, 8), 8)
        for k in range(4):
            n = (at % (states // 4)) * 4 + k
            r = rates[n, d]
            for i in range(BI):
                acc = None
                for j in range(BJ):
                    p = i * BJ + j
                    term = jnp.exp2(cum_cols[p, d] * r) * grad_p[p, d] * row_of(read_p, p, n)
                    acc = term if acc is None else acc + term
                seg[n, i, d] = acc
        return carry

    lax.fori_loop(0, D // 8 * (states // 4), group, 0)

    for i in range(BI):
        for g in range(4):
            part = seg[:, i, g * 32 : g * 32 + 32, :].reshape(states * 32, LANES)
            out = lane_dot(part, cols_out[g, i]).reshape(states, 32, LANES)
            if i == 0 and g == 0:
                leaving[...] = out
            else:
                leaving[...] += out


def spread(states, blocks, rows, seg, entering, order, enter, scale, out):
    for k in range(seg.shape[1]):
        for g in range(blocks):
            at = pl.ds(g * rows, rows)
            part = seg[:, k, at, :].reshape(states * rows, LANES)
            whole = lane_dot(part, order) + lane_dot(
                entering[...].reshape(states * rows, LANES), enter[g, k]
            )
            out[:, k, at, :] = whole.reshape(states, rows, LANES)
    def rescale(at, carry):
        n, d = at // (D // 8), pl.ds(pl.multiple_of((at % (D // 8)) * 8, 8), 8)
        for k in range(seg.shape[1]):
            out[n, k, d] = out[n, k, d] * scale(n, k, d)
        return carry
    lax.fori_loop(0, states * (D // 8), rescale, 0)


def forward_cols_kernel(
    seg_rows, entering, step_p, source_p, write_p, rates, rates_pk, cum_rows, cum_cols, sum_cols,
    above, rows_in, cols_out, start_rows, seg, leaving,
):
    states = rates.shape[0]
    spread(
        states, 2, 64, seg_rows, entering, above[...], rows_in,
        lambda n, j, d: jnp.exp2(rates[n, d] * (cum_rows[j, d] - step_p[j, d])), start_rows,
    )

    def group(at, carry):
        d = pl.ds(pl.multiple_of((at // (states // 4)) * 8, 8), 8)
        for k in range(4):
            n = (at % (states // 4)) * 4 + k
            r = rates[n, d]
            vert = [start_rows[n, j, d] for j in range(BJ)]
            for i in range(BI):
                state = None
                for j in range(BJ):
                    p = i * BJ + j
                    decay = jnp.exp2(step_p[p, d] * r)
                    vert[j] = decay * vert[j] + source_p[p, d] * row_of(write_p, p, n)
                    state = vert[j] if state is None else decay * state + vert[j]
                seg[n, i, d] = state * jnp.exp2(-r * cum_cols[i * BJ + BJ - 1, d])
        return carry

    lax.fori_loop(0, D // 8 * (states // 4), group, 0)
    for i in range(BI):
        for g in range(4):
            part = seg[:, i, g * 32 : g * 32 + 32, :].reshape(states * 32, LANES)
            out = lane_dot(part, cols_out[g, i]).reshape(states, 32, LANES)
            if i == 0 and g == 0:
                leaving[...] = out
            else:
                leaving[...] += out
    for n in range(states):
        leaving[n] = leaving[n] * jnp.exp2(rates_pk[n] * sum_cols[...])


def adjoint_rows_kernel(
    seg_cols, entering, step_p, grad_p, read_p, rates, rates_pk, cum_rows, cum_cols, sum_cols,
    right, cols_in, rows_out, start_cols, seg, leaving,
):
    states = rates.shape[0]
    for n in range(states):
        leaving[n, 0:32] = entering[n] * jnp.exp2(rates_pk[n] * sum_cols[...])
    spread(
        states, 4, 32, seg_cols, leaving.at[:, 0:32], right[...], cols_in,
        lambda n, i, d: jnp.exp2(-rates[n, d] * cum_cols[i * BJ + BJ - 1, d]), start_cols,
    )

    def group(at, carry):
        d = pl.ds(pl.multiple_of((at // (states // 4)) * 8, 8), 8)
        for k in range(4):
            n = (at % (states // 4)) * 4 + k
            r = rates[n, d]
            passed_v = [None] * BJ
            for i in reversed(range(BI)):
                passed = start_cols[n, i, d]
                for j in reversed(range(BJ)):
                    p = i * BJ + j
                    decay = jnp.exp2(step_p[p, d] * r)
                    adjoint = grad_p[p, d] * row_of(read_p, p, n) + passed
                    passed = decay * adjoint
                    if passed_v[j] is None:
                        passed_v[j] = passed
                    else:
                        passed_v[j] = decay * (adjoint + passed_v[j])
            for j in range(BJ):
                seg[n, j, d] = passed_v[j] * jnp.exp2(r * (cum_rows[j, d] - step_p[j, d]))
        return carry

    lax.fori_loop(0, D // 8 * (states // 4), group, 0)
    for j in range(BJ):
        for g in range(2):
            part = seg[:, j, g * 64 : g * 64 + 64, :].reshape(states * 64, LANES)
            out = lane_dot(part, rows_out[g, j]).reshape(states, 64, LANES)
            if j == 0 and g == 0:
                leaving[...] = out
            else:
                leaving[...] += out


def final_kernel(
    start_rows, start_cols, seg_s, enter_s, seg_v, enter_v,
    step_p, source_p, grad_p, write_p, read_p, rates, rates_v, cum_rows, cum_cols, sum_rows,
    left, below, rows_in, cols_in,
    grad_features, grad_step, grad_write, grad_read, grad_decay,
    in_s, in_v, scaled_v, through, rate_term, sum_w, sum_r, decay_term,
):
    states = rates.shape[0]
    spread(
        states, 4, 32, seg_s, enter_s, left[...], cols_in,
        lambda n, i, d: jnp.exp2(rates[n, d] * (cum_cols[i * BJ, d] - step_p[i * BJ, d])), in_s,
    )
    for n in range(states):
        scaled_v[n] = enter_v[n] * jnp.exp2(rates_v[n] * sum_rows[...])
    spread(
        states, 2, 64, seg_v, scaled_v, below[...], rows_in,
        lambda n, j, d: jnp.exp2(-rates[n, d] * cum_rows[(BI - 1) * BJ + j, d]), in_v,
    )
    sum_w[...] = jnp.zeros_like(sum_w)
    sum_r[...] = jnp.zeros_like(sum_r)

    def block(at, carry):
        d = pl.ds(pl.multiple_of(at * 8, 8), 8)
        for p in range(POS):
            through[p, d] = jnp.zeros((8, LANES), F32)
            rate_term[p, d] = jnp.zeros((8, LANES), F32)

        def one(n, carry):
            r = rates[n, d]
            vert = [start_rows[n, j, d] for j in range(BJ)]
            exps, decays, from_v, from_s = [], [], [], []
            for i in range(BI):
                state = in_s[n, i, d]
                for j in range(BJ):
                    p = i * BJ + j
                    m = step_p[p, d] * r
                    decay = jnp.exp2(m)
                    dv = decay * vert[j]
                    vert[j] = dv + source_p[p, d] * row_of(write_p, p, n)
                    ds = decay * state
                    state = ds + vert[j]
                    sum_r[p, n] += state * grad_p[p, d]
                    exps.append(m)
                    decays.append(decay)
                    from_v.append(dv)
                    from_s.append(ds)
            passed_v = [in_v[n, j, d] for j in range(BJ)]
            total = None
            for i in reversed(range(BI)):
                passed = start_cols[n, i, d]
                for j in reversed(range(BJ)):
                    p = i * BJ + j
                    adjoint = grad_p[p, d] * row_of(read_p, p, n) + passed
                    passed = decays[p] * adjoint
                    adjoint_v = adjoint + passed_v[j]
                    passed_v[j] = decays[p] * adjoint_v
                    q = (adjoint * from_s[p] + adjoint_v * from_v[p]) * exps[p]
                    total = q if total is None else total + q
                    rate_term[p, d] += q
                    through[p, d] += adjoint_v * row_of(write_p, p, n)
                    sum_w[p, n] += adjoint_v * source_p[p, d]
            decay_term[n, d] = total
            return carry

        lax.fori_loop(0, states, one, 0)
        for p in range(POS):
            t = through[p, d]
            s = step_p[p, d]
            rate_term[p, d] = (source_p[p, d] * t + rate_term[p, d] * LN2) / s
            through[p, d] = s * t
        return carry

    lax.fori_loop(0, D // 8, block, 0)
    for i in range(BI):
        for j in range(BJ):
            p = i * BJ + j
            for values, out in ((through, grad_features), (rate_term, grad_step)):
                back = values[p].T
                for hs in range(HS):
                    out[hs * BI + i, pl.ds(j, WS, stride=BJ), :] = back[hs * WS : hs * WS + WS]
            grad_write[p] = jnp.sum(sum_w[p], 1)
            grad_read[p] = jnp.sum(sum_r[p], 1)
    ones = jnp.ones((8, 2 * LANES), BF16)
    for n in range(states):
        part = jnp.concatenate(halves(decay_term[n]), 1)
        out = lax.dot_general(ones, part, (((1,), (1,)), ((), ())), preferred_element_type=F32)
        grad_decay[pl.ds(n, 1)] = out[0:1] * LN2


def run(kernel, outs, args, scratch=(), flops=0):
    shapes = [jax.ShapeDtypeStruct(s, F32) for s in outs]
    size = sum(a.size * a.dtype.itemsize for a in args) + 4 * sum(int(np.prod(s)) for s in outs)
    vmem = pl.BlockSpec(memory_space=pltpu.VMEM)
    return pl.pallas_call(
        kernel,
        out_shape=shapes,
        in_specs=[vmem] * len(args),
        out_specs=[vmem] * len(outs),
        scratch_shapes=[pltpu.VMEM(s, F32) for s in scratch],
        compiler_params=pltpu.CompilerParams(vmem_limit_bytes=60 << 20),
        cost_estimate=pl.CostEstimate(flops=flops, bytes_accessed=size, transcendentals=0),
    )(*args)


def row_carry(leaving, sums, rates, size, reverse):
    count = leaving.shape[0] // 2
    me = lax.axis_index("row")
    core = me % 2
    swap = [(k, k ^ 1) for k in range(size)]
    other_sums = lax.ppermute(sums, "row", swap)
    mine = lax.dynamic_slice_in_dim(leaving, core * count, count, 0)
    theirs = lax.ppermute(
        lax.dynamic_slice_in_dim(leaving, (1 - core) * count, count, 0), "row", swap
    )
    rate = lax.dynamic_slice_in_dim(rates, core * count, count, 0)
    first = core == (1 if reverse else 0)
    near = jnp.where(first, mine, theirs)
    far = jnp.where(first, theirs, mine)
    near_sum = jnp.where(first, sums, other_sums)
    far_sum = jnp.where(first, other_sums, sums)
    total = far + jnp.exp2(rate * far_sum) * near
    sign = -2 if reverse else 2

    def shift(x, by):
        return lax.ppermute(
            x, "row", [(k, k + by) for k in range(size) if 0 <= k + by < size]
        )

    entering = shift(total, sign)
    if size > 4:
        span = shift(near_sum + far_sum, sign)
        by = sign
        while abs(by) < size - 2:
            entering = entering + jnp.exp2(rate * span) * shift(entering, by)
            span = span + shift(span, by)
            by *= 2
    to_far = near + jnp.exp2(rate * near_sum) * entering
    keep = jnp.where(first, entering, to_far)
    give = jnp.where(first, to_far, entering)
    got = lax.ppermute(give, "row", swap)
    return jnp.concatenate(
        [jnp.where(core == 0, keep, got), jnp.where(core == 0, got, keep)], 0
    )


def col_carry(leaving, sums, rates, size, reverse):
    states, rows, _ = leaving.shape
    share = rows // size
    me = lax.axis_index("col")
    send = jnp.concatenate([leaving, sums[None]], 0)
    send = send.reshape(states + 1, size, share, LANES).swapaxes(0, 1)
    held = lax.all_to_all(send, "col", 0, 0)
    rate = lax.dynamic_slice_in_dim(rates, me * share, share, 1)
    before = jnp.zeros((states, share, LANES), F32)
    parts = [None] * size
    for k in reversed(range(size)) if reverse else range(size):
        parts[k] = before
        before = jnp.exp2(rate * held[k, states]) * before + held[k, :states]
    back = lax.all_to_all(jnp.stack(parts), "col", 0, 0)
    return back.swapaxes(0, 1).reshape(states, rows, LANES)


def shards(features, step_size, write_weights, read_weights, decay_log, out_grad, sizes):
    rows, cols = sizes
    states = decay_log.shape[0]
    tile_h, tile_w = features.shape[:2]
    mats = lane_matrices()
    rate = -jnp.exp(decay_log) * LOG2E
    rates = jnp.broadcast_to(rate[:, :, None], (states, D, LANES))
    rates_v = jnp.repeat(rate.reshape(states, 2, 64).swapaxes(1, 2), 64, 2)
    rates_s = jnp.repeat(rate.reshape(states, 4, 32).swapaxes(1, 2), 32, 2)
    plane = (POS, D, LANES)
    seg = (states, 4, D, LANES)
    (step_p, source_p, write_p, cum_rows, cum_cols, sum_rows, sum_cols, seg_rows, leave_rows) = run(
        forward_rows_kernel,
        [plane, plane, (POS, states, LANES), plane, plane, (64, LANES), (32, LANES), seg,
         (states, 64, LANES)],
        [step_size, features, write_weights, rates, rates_v, mats["above"], mats["left"],
         mats["rows_out"], mats["cols_out"]],
    )
    enter_rows = row_carry(leave_rows, sum_rows, rates_v, rows, False)
    grad_p, read_p, seg_cols, leave_cols = run(
        adjoint_cols_kernel,
        [plane, (POS, states, LANES), seg, (states, 32, LANES)],
        [out_grad, read_weights, rates, cum_cols, mats["cols_out"]],
    )
    enter_cols = col_carry(leave_cols, sum_cols, rates_s, cols, True)
    start_rows, seg_s, leave_s = run(
        forward_cols_kernel,
        [seg, seg, (states, 32, LANES)],
        [seg_rows, enter_rows, step_p, source_p, write_p, rates, rates_s, cum_rows, cum_cols,
         sum_cols, mats["above"], mats["rows_in"], mats["cols_out"]],
    )
    enter_s = col_carry(leave_s, sum_cols, rates_s, cols, False)
    start_cols, seg_v, leave_v = run(
        adjoint_rows_kernel,
        [seg, seg, (states, 64, LANES)],
        [seg_cols, enter_cols, step_p, grad_p, read_p, rates, rates_s, cum_rows, cum_cols,
         sum_cols, mats["right"], mats["cols_in"], mats["rows_out"]],
    )
    enter_v = row_carry(leave_v, sum_rows, rates_v, rows, True)
    grad_features, grad_step, grad_write, grad_read, grad_decay = run(
        final_kernel,
        [features.shape, features.shape, (POS, states, LANES), (POS, states, LANES), (states, D)],
        [start_rows, start_cols, seg_s, enter_s, seg_v, enter_v, step_p, source_p, grad_p,
         write_p, read_p, rates, rates_v, cum_rows, cum_cols, sum_rows, mats["left"],
         mats["below"], mats["rows_in"], mats["cols_in"]],
        [seg, seg, (states, 64, LANES), plane, plane, (POS, states, 8, LANES),
         (POS, states, 8, LANES), (states, D, LANES)],
    )

    def unpack(x):
        x = x.reshape(BI, BJ, states, HS, WS).transpose(3, 0, 4, 1, 2)
        return x.reshape(tile_h, tile_w, states)

    return (
        grad_features,
        grad_step,
        unpack(grad_write),
        unpack(grad_read),
        lax.psum(grad_decay, ("row", "col")),
    )


def solution(mesh):
    spec = P("row", "col", None)
    sizes = (mesh.shape["row"], mesh.shape["col"])
    return jax.shard_map(
        functools.partial(shards, sizes=sizes),
        mesh=mesh,
        in_specs=(spec, spec, spec, spec, P(), spec),
        out_specs=(spec, spec, spec, spec, P()),
        check_vma=False,
    )
```

time: 931 us -> 259 us (0.28); the launches traced: 915 us -> 258 us
  other arithmetic: 651 us -> 15.4 us
  Pallas kernels: 0 us -> 116 us
  local copies, waits for them, and re-layouts: 97.6 us -> 19.4 us
  matrix products: 74.5 us -> 0 us
  starting transfers between devices: 0.71 us -> 23.7 us
  between operations: 14.8 us -> 0.92 us
  waiting for transfers between devices: 34.9 us -> 44.3 us
    dynamic_update_slice x192 -> x0, other arithmetic: 376 us -> none  [the longest x64 142 us: sweep_rows(): closing, values = lax.scan(advance, initial, (decays, driving))]
    mul x100 -> x1, other arithmetic: 147 us -> 0.74 us  [shards(): rate = -jnp.exp(decay_log) * LOG2E]
    pallas_call x0 -> x5, Pallas kernels: none -> 116 us  [run(): pl.pallas_call(kernel, out_shape=shapes, in_specs=[vmem] * len(args), out...]
    dot_general x3 -> x0, matrix products: 74.5 us -> none  [the longest x1 28.9 us: shards(): jnp.einsum('hwnd,hwd->hwn', adjoint_v, step_size * features, precision=hi...]
    select_n x24 -> x4, other arithmetic: 38.1 us -> 1.3 us  [the longest x1 1.17 us: row_carry(): give = jnp.where(first, to_far, entering)]
    all_gather x6 -> x0, waiting for transfers between devices: 34.8 us -> none  [carried_in(): everything = jax.tree.map(lambda part: lax.all_gather(part, axis), shard)]
    dot_general x1 -> x0, other arithmetic: 34.6 us -> none  [shards(): jnp.einsum('hwnd,hwd->nd', exponent_grad, step_size, precision=highest)]
    add x2 -> x1, other arithmetic: 35.6 us -> 1.1 us  [row_carry(): total = far + jnp.exp2(rate * far_sum) * near]
  transfers between devices with their start and end apart: 6 -> 11, of which waited for: 1 -> 8; matrix products, arithmetic and copies ran while one was open for 48% -> 4% of each run, Pallas kernels for 0% -> 8%
where the time goes in v1:
time: 259 us; the launch traced here: 258 us
  Pallas kernels  116 us (45%)
  waiting for transfers between devices  44.3 us (17%)
  blocking collectives  38.8 us (15%)
  starting transfers between devices  23.7 us (9%)
  local copies, waits for them, and re-layouts  19.4 us (7%)
  other arithmetic  15.4 us (6%)
    pallas_call x5, Pallas kernels, run(): pl.pallas_call(kernel, out_shape=shapes, in_specs=[vmem] * len(args), out...  116 us
    psum x1, blocking collectives, shards(): lax.psum(grad_decay, ('row', 'col'))  38.8 us
    all_to_all x2, waiting for transfers between devices, col_carry(): held = lax.all_to_all(send, 'col', 0, 0)  16.8 us
    all_to_all x2, waiting for transfers between devices, col_carry(): back = lax.all_to_all(jnp.stack(parts), 'col', 0, 0)  16.4 us
    all_to_all x2, starting transfers between devices, col_carry(): held = lax.all_to_all(send, 'col', 0, 0)  10.8 us
    ppermute x2, waiting for transfers between devices, shift(): lax.ppermute(x, 'row', [(k, k + by) for k in range(size) if 0 <= k + by <...  8.48 us
    unnamed x28, local copies, waits for them, and re-layouts  8.17 us
    all_to_all x2, starting transfers between devices, col_carry(): back = lax.all_to_all(jnp.stack(parts), 'col', 0, 0)  7.22 us
  transfers between devices with their start and end apart: 11, of which 8 were waited for; matrix products, arithmetic and copies ran while one was open for 4% of the time, Pallas kernels for 8%

profile of v1, /device:TPU:0, one launch (start us, length us, event | category | flops | bytes accessed | tf_op | source)
XLA Modules:
  0.0 258.0 jit_solution(6560675784031769346)
XLA Ops:
  0.6 0.7 negate_multiply_fusion
  1.7 1.2 broadcast_in_dim.7
  3.0 1.4 reshape.68.rates_pk.rates_v
  4.4 2.3 copy.27.write
  6.6 1.3 copy.29.read
  8.0 1.4 broadcast_in_dim.6.rates
  9.3 11.3 %shard_map.173 = (f32[16,128,128]{2,1,0:T(8,128)}, f32[16,128,128]{2,1,0:T(8,128)}, f32[16,16,128]{2,1,0:T(8,128)}, f32[16,128,128]{2,1,0:T(8,128)}, f32[16,128,...) custom-call(f32[32,64,128]{2,1,0:T(8,128)} %step.1, ...), custom_call_target="tpu_custom_call" | custom-call | bytes 14598144 | tf_op jit(solution)/shard_map/pallas_call | solution.py:371
  20.6 9.5 %shard_map.175 = (f32[16,128,128]{2,1,0:T(8,128)}, f32[16,16,128]{2,1,0:T(8,128)}, f32[16,4,128,128]{3,2,1,0:T(8,128)}, f32[16,32,128]{2,1,0:T(8,128)}) custom-call(f32[32,64,128]{2,1,0:T(8,128)} %grad.1, f32[32,64,16]{2,1,0:T(8,128)} %copy.29.read, f32[16,128,128]{2,1,0:T(8,128)} %broadcast_in_dim.6.rates, f32[16,128,128]{2,1,0:T(8,128)} %get-tuple-element.36.cum_cols, ...), custom_call_target="tpu_custom_call" | custom-call | bytes 9961472 | tf_op jit(solution)/shard_map/pallas_call | solution.py:371
  30.1 1.7 fusion
  31.8 7.3 %all-to-all-start = ((f32[8,17,4,128]{3,2,1,0:T(4,128)}), f32[8,17,4,128]{3,2,1,0:T(4,128)S(1)}, u32[]{:S(2)}, u32[]{:S(2)}) async-start(f32[8,17,4,128]{3,2,1,0:T(4,128)} %fusion), calls=%async_computation | async-start | bytes 557056 | tf_op jit(solution)/shard_map/all_to_all | solution.py:429
  40.4 7.9 %all-to-all-done = f32[8,17,4,128]{3,2,1,0:T(4,128)S(1)} async-done(((f32[8,17,4,128]{3,2,1,0:T(4,128)}), f32[8,17,4,128]{3,2,1,0:T(4,128)S(1)}, u32[]{:S(2)}, u32[]{:S(2)}) %all-to-all-start) | async-done | bytes 278560 | tf_op jit(solution)/shard_map/all_to_all | solution.py:429
  48.3 0.7 constant_dynamic-update-slice_fusion.7
  49.7 0.6 constant_dynamic-update-slice_fusion.5
  50.9 0.6 constant_dynamic-update-slice_fusion.3
  53.4 3.6 %all-to-all-start.1 = ((f32[8,16,4,128]{3,2,1,0:T(4,128)}), f32[8,16,4,128]{3,2,1,0:T(4,128)S(1)}, u32[]{:S(2)}, u32[]{:S(2)}) async-start(f32[8,16,4,128]{3,2,1,0:T(4,128)} %constant_dynamic-update-slice_fusion), calls=%async_computation.1 | async-start | bytes 524288 | tf_op jit(solution)/shard_map/all_to_all | solution.py:436
  57.1 8.4 %all-to-all-done.1 = f32[8,16,4,128]{3,2,1,0:T(4,128)S(1)} async-done(((f32[8,16,4,128]{3,2,1,0:T(4,128)}), f32[8,16,4,128]{3,2,1,0:T(4,128)S(1)}, u32[]{:S(2)}, u32[]{:S(2)}) %all-to-all-start.1) | async-done | bytes 262176 | tf_op jit(solution)/shard_map/all_to_all | solution.py:436
  65.6 0.8 copy.33.entering
  66.4 20.2 %shard_map.176 = (f32[16,4,128,128]{3,2,1,0:T(8,128)}, f32[16,4,128,128]{3,2,1,0:T(8,128)}, f32[16,64,128]{2,1,0:T(8,128)}) custom-call(f32[16,4,128,128]{3,2,1,0:T(8,128)} %get-tuple-element.39.seg_cols, f32[16,32,128]{2,1,0:T(8,128)} %copy.33.entering, f32[16,128,128]{2,1,0:T(8,128)} %get-tuple-element.32.step_p, ...), custom_call_target="tpu_custom_call" | custom-call | bytes 20660224 | tf_op jit(solution)/shard_map/pallas_call | solution.py:371
  86.6 1.0 constant_dynamic-slice_fusion
  88.1 1.1 collective-permute-done.1
  89.2 1.1 multiply_add_fusion.1
  90.3 3.4 %collective-permute-start.2 = (f32[8,64,128]{2,1,0:T(8,128)S(1)}, f32[8,64,128]{2,1,0:T(8,128)S(1)}, u32[]{:S(2)}, u32[]{:S(2)}) collective-permute-start(f32[8,64,128]{2,1,0:T(8,128)S(1)} %get-tuple-element.79), channel_id=1, source_target_pairs={{0,16},{8,24},{1,17},{9,25},{2,18},{10,26},{3,19},{11,27},{4,20},{... | collective-permute-start | bytes 786440 | tf_op jit(solution)/shard_map/ppermute | solution.py:402
  93.8 1.5 collective-permute-start.5
  95.3 4.4 %collective-permute-done.2 = f32[8,64,128]{2,1,0:T(8,128)S(1)} collective-permute-done((f32[8,64,128]{2,1,0:T(8,128)S(1)}, f32[8,64,128]{2,1,0:T(8,128)S(1)}, u32[]{:S(2)}, u32[]{:S(2)}) %collective-permute-start.2) | collective-permute-done | bytes 262176 | tf_op jit(solution)/shard_map/ppermute | solution.py:402
  99.6 4.1 %collective-permute-done.5 = f32[8,64,128]{2,1,0:T(8,128)S(1)} collective-permute-done((f32[8,64,128]{2,1,0:T(8,128)S(1)}, f32[8,64,128]{2,1,0:T(8,128)S(1)}, u32[]{:S(2)}, u32[]{:S(2)}) %collective-permute-start.5) | collective-permute-done | bytes 262176 | tf_op jit(solution)/shard_map/ppermute | solution.py:402
  103.8 1.2 broadcast_select_fusion
  105.0 1.5 collective-permute-done.3
  106.6 0.8 pad_maximum_fusion.entering
  107.4 21.8 %shard_map.174 = (f32[16,4,128,128]{3,2,1,0:T(8,128)}, f32[16,4,128,128]{3,2,1,0:T(8,128)}, f32[16,32,128]{2,1,0:T(8,128)}) custom-call(f32[16,4,128,128]{3,2,1,0:T(8,128)} %get-tuple-element.29.seg_rows, f32[16,64,128]{2,1,0:T(8,128)} %pad_maximum_fusion.entering, f32[16,128,128]{2,1,0:T(8,128)} %get-tuple-element.32.step_p, ...), custom_call_target="tpu_custom_call" | custom-call | bytes 20660224 | tf_op jit(solution)/shard_map/pallas_call | solution.py:371
  129.2 1.7 fusion.1
  130.9 3.6 %all-to-all-start.2 = ((f32[8,17,4,128]{3,2,1,0:T(4,128)}), f32[8,17,4,128]{3,2,1,0:T(4,128)S(1)}, u32[]{:S(2)}, u32[]{:S(2)}) async-start(f32[8,17,4,128]{3,2,1,0:T(4,128)} %fusion.1), calls=%async_computation.2 | async-start | bytes 557056 | tf_op jit(solution)/shard_map/all_to_all | solution.py:429
  135.2 8.9 %all-to-all-done.2 = f32[8,17,4,128]{3,2,1,0:T(4,128)S(1)} async-done(((f32[8,17,4,128]{3,2,1,0:T(4,128)}), f32[8,17,4,128]{3,2,1,0:T(4,128)S(1)}, u32[]{:S(2)}, u32[]{:S(2)}) %all-to-all-start.2) | async-done | bytes 278560 | tf_op jit(solution)/shard_map/all_to_all | solution.py:429
  144.1 0.6 constant_dynamic-update-slice_fusion.14
  144.7 0.7 constant_dynamic-update-slice_fusion.13
  145.4 0.6 constant_dynamic-update-slice_fusion.12
  146.0 0.7 constant_dynamic-update-slice_fusion.11
  146.7 0.6 constant_dynamic-update-slice_fusion.10
  147.3 0.7 constant_dynamic-update-slice_fusion.9
  148.0 0.6 constant_dynamic-update-slice_fusion.8
  148.7 3.6 %all-to-all-start.3 = ((f32[8,16,4,128]{3,2,1,0:T(4,128)}), f32[8,16,4,128]{3,2,1,0:T(4,128)S(1)}, u32[]{:S(2)}, u32[]{:S(2)}) async-start(f32[8,16,4,128]{3,2,1,0:T(4,128)} %constant_dynamic-update-slice_fusion.8), calls=%async_computation.3 | async-start | bytes 524288 | tf_op jit(solution)/shard_map/all_to_all | solution.py:436
  152.3 0.8 pad_maximum_fusion.1.enter_v
  153.2 7.9 %all-to-all-done.3 = f32[8,16,4,128]{3,2,1,0:T(4,128)S(1)} async-done(((f32[8,16,4,128]{3,2,1,0:T(4,128)}), f32[8,16,4,128]{3,2,1,0:T(4,128)S(1)}, u32[]{:S(2)}, u32[]{:S(2)}) %all-to-all-start.3) | async-done | bytes 262176 | tf_op jit(solution)/shard_map/all_to_all | solution.py:436
  161.1 0.8 copy.36
  161.9 52.8 %shard_map.177 = (f32[32,64,128]{2,1,0:T(8,128)}, f32[32,64,128]{2,1,0:T(8,128)}, f32[16,16,128]{2,1,0:T(8,128)}, f32[16,16,128]{2,1,0:T(8,128)}, f32[16,128]{1,0:T(8,128)}) custom-call(f32[16,4,128,128]{3,2,1,0:T(8,128)} %get-tuple-element.38.start_rows, f32[16,4,128,128]{3,2,1,0:T(8,128)} %get-tuple-element.43.start_cols, ...), custom_call_target="tpu_custom_call" | custom-call | bytes 28745728 | tf_op jit(solution)/shard_map/pallas_call | solution.py:371
  214.7 1.3 reshape.73
  216.4 1.0 copy.39
  218.2 1.0 copy.40
  219.2 38.8 %psum.7 = f32[16,128]{1,0:T(8,128)} all-reduce(f32[16,128]{1,0:T(8,128)S(1)} %copy-done.9), channel_id=1, replica_groups=mesh['row'=4,'col'=8] {'row','col'}, use_global_device_ids=true, to_apply=%region_0.1 | all-reduce | flops 2048 | bytes 16384 | tf_op jit(solution)/shard_map/psum | solution.py:498
  (50 shorter events, 7.5 us)
Async XLA Ops:
  0.6 6.0 %copy-start.6 = (f32[32,64,16]{1,2,0:T(8,128)S(1)}, f32[32,64,16]{1,2,0:T(8,128)}, u32[]{:S(2)}) copy-start(f32[32,64,16]{1,2,0:T(8,128)} %param.17) | copy-start | bytes 393220
  20.6 9.5 %copy-start.4 = (f32[32,128]{1,0:T(8,128)S(1)}, f32[32,128]{1,0:T(8,128)}, u32[]{:S(2)}) copy-start(f32[32,128]{1,0:T(8,128)} %get-tuple-element.37.sum_cols) | copy-start | bytes 49156
  20.6 36.4 %copy-start.3 = (f32[16,64,128]{2,1,0:T(8,128)S(1)}, f32[16,64,128]{2,1,0:T(8,128)}, u32[]{:S(2)}) copy-start(f32[16,64,128]{2,1,0:T(8,128)} %get-tuple-element.30) | copy-start | bytes 1572868
  31.8 16.5 %all-to-all-start = ((f32[8,17,4,128]{3,2,1,0:T(4,128)}), f32[8,17,4,128]{3,2,1,0:T(4,128)S(1)}, u32[]{:S(2)}, u32[]{:S(2)}) async-start(f32[8,17,4,128]{3,2,1,0:T(4,128)} %fusion), calls=%async_computation | async-start | bytes 557056 | tf_op jit(solution)/shard_map/all_to_all | solution.py:429
  40.4 26.0 %copy-start.1 = (f32[16,32,128]{2,1,0:T(8,128)}, f32[16,32,128]{2,1,0:T(8,128)S(1)}, u32[]{:S(2)}) copy-start(f32[16,32,128]{2,1,0:T(8,128)S(1)} %reshape.70.rates_pk) | copy-start | bytes 786436
  53.4 12.1 %all-to-all-start.1 = ((f32[8,16,4,128]{3,2,1,0:T(4,128)}), f32[8,16,4,128]{3,2,1,0:T(4,128)S(1)}, u32[]{:S(2)}, u32[]{:S(2)}) async-start(f32[8,16,4,128]{3,2,1,0:T(4,128)} %constant_dynamic-update-slice_fusion), calls=%async_computation.1 | async-start | bytes 524288 | tf_op jit(solution)/shard_map/all_to_all | solution.py:436
  57.1 32.1 %collective-permute-start = (f32[8,64,128]{2,1,0:T(8,128)S(1)}, f32[8,64,128]{2,1,0:T(8,128)S(1)}, u32[]{:S(2)}, u32[]{:S(2)}) collective-permute-start(f32[8,64,128]{2,1,0:T(8,128)S(1)} %constant_dynamic-slice_fusion.2), channel_id=1, source_target_pairs={{0,8},{8,0},{16,24},{24,16},{1,9},{9,1},{17,25},{25,17},{2,10},{10... | collective-permute-start | bytes 786440 | tf_op jit(solution)/shard_map/ppermute | solution.py:389
  66.4 21.2 %copy-start.7 = (f32[64,128]{1,0:T(8,128)S(1)}, f32[64,128]{1,0:T(8,128)}, u32[]{:S(2)}) copy-start(f32[64,128]{1,0:T(8,128)} %get-tuple-element.31.sum_rows) | copy-start | bytes 98308
  66.4 22.8 %copy-start = (f32[16,64,128]{2,1,0:T(8,128)S(1)}, f32[16,64,128]{2,1,0:T(8,128)}, u32[]{:S(2)}) copy-start(f32[16,64,128]{2,1,0:T(8,128)} %reshape.68.rates_pk.rates_v) | copy-start | bytes 1572868
  87.5 1.7 collective-permute-start.4
  87.6 1.6 collective-permute-start.1
  90.3 9.3 %collective-permute-start.2 = (f32[8,64,128]{2,1,0:T(8,128)S(1)}, f32[8,64,128]{2,1,0:T(8,128)S(1)}, u32[]{:S(2)}, u32[]{:S(2)}) collective-permute-start(f32[8,64,128]{2,1,0:T(8,128)S(1)} %get-tuple-element.79), channel_id=1, source_target_pairs={{0,16},{8,24},{1,17},{9,25},{2,18},{10,26},{3,19},{11,27},{4,20},{... | collective-permute-start | bytes 786440 | tf_op jit(solution)/shard_map/ppermute | solution.py:402
  93.8 10.0 %collective-permute-start.5 = (f32[8,64,128]{2,1,0:T(8,128)S(1)}, f32[8,64,128]{2,1,0:T(8,128)S(1)}, u32[]{:S(2)}, u32[]{:S(2)}) collective-permute-start(f32[8,64,128]{2,1,0:T(8,128)S(1)} %get-tuple-element.78), channel_id=1, source_target_pairs={{16,0},{24,8},{17,1},{25,9},{18,2},{26,10},{19,3},{27,11},{20,4},{... | collective-permute-start | bytes 786440 | tf_op jit(solution)/shard_map/ppermute | solution.py:402
  104.9 1.6 collective-permute-start.3
  107.4 21.8 %copy-start.5 = (f32[32,128]{1,0:T(8,128)S(1)}, f32[32,128]{1,0:T(8,128)}, u32[]{:S(2)}) copy-start(f32[32,128]{1,0:T(8,128)} %get-tuple-element.37.sum_cols) | copy-start | bytes 49156
  107.4 36.7 %copy-start.2 = (f32[16,32,128]{2,1,0:T(8,128)S(1)}, f32[16,32,128]{2,1,0:T(8,128)}, u32[]{:S(2)}) copy-start(f32[16,32,128]{2,1,0:T(8,128)} %copy-done.1) | copy-start | bytes 786436
  130.9 13.1 %all-to-all-start.2 = ((f32[8,17,4,128]{3,2,1,0:T(4,128)}), f32[8,17,4,128]{3,2,1,0:T(4,128)S(1)}, u32[]{:S(2)}, u32[]{:S(2)}) async-start(f32[8,17,4,128]{3,2,1,0:T(4,128)} %fusion.1), calls=%async_computation.2 | async-start | bytes 557056 | tf_op jit(solution)/shard_map/all_to_all | solution.py:429
  135.2 17.1 %collective-permute-start.6 = (f32[8,64,128]{2,1,0:T(8,128)S(1)}, f32[8,64,128]{2,1,0:T(8,128)S(1)}, u32[]{:S(2)}, u32[]{:S(2)}) collective-permute-start(f32[8,64,128]{2,1,0:T(8,128)S(1)} %get-tuple-element.58), channel_id=1, source_target_pairs={{0,8},{8,0},{16,24},{24,16},{1,9},{9,1},{17,25},{25,17},{2,10},{10... | collective-permute-start | bytes 786440 | tf_op jit(solution)/shard_map/ppermute | solution.py:417
  148.7 12.5 %all-to-all-start.3 = ((f32[8,16,4,128]{3,2,1,0:T(4,128)}), f32[8,16,4,128]{3,2,1,0:T(4,128)S(1)}, u32[]{:S(2)}, u32[]{:S(2)}) async-start(f32[8,16,4,128]{3,2,1,0:T(4,128)} %constant_dynamic-update-slice_fusion.8), calls=%async_computation.3 | async-start | bytes 524288 | tf_op jit(solution)/shard_map/all_to_all | solution.py:436
  214.7 2.7 %copy-start.8 = (f32[16,16,128]{2,1,0:T(8,128)S(1)}, f32[16,16,128]{2,1,0:T(8,128)}, u32[]{:S(2)}) copy-start(f32[16,16,128]{2,1,0:T(8,128)} %get-tuple-element.51) | copy-start | bytes 393220
  215.9 3.3 %copy-start.9 = (f32[16,128]{1,0:T(8,128)S(1)}, f32[16,128]{1,0:T(8,128)}, u32[]{:S(2)}) copy-start(f32[16,128]{1,0:T(8,128)} %get-tuple-element.52) | copy-start | bytes 24580

commit v2 on v0

v2 whole, which is shorter than its diff:
```python
import functools

import jax
import jax.numpy as jnp
import numpy as np
from jax import lax
from jax.experimental import pallas as pl
from jax.experimental.pallas import tpu as pltpu
from jax.sharding import PartitionSpec as P

HS, WS, BI, BJ = 8, 16, 4, 4
POS = BI * BJ
LANES = 128
D = 128
GROUPS = 1
CHANNELS = D // GROUPS
PACKS = 4
PACK = CHANNELS // PACKS
STEPS = 4
BLOCK = CHANNELS // STEPS
INNER = PACKS // STEPS
F32 = jnp.float32
BF16 = jnp.bfloat16
LOG2E = 1.4426950408889634
LN2 = 0.6931471805599453


@functools.cache
def lane_matrices():
    lane = np.arange(LANES)
    hs, ws = lane // WS, lane % WS
    same_w = ws[:, None] == ws[None]
    same_h = hs[:, None] == hs[None]
    above = same_w & (hs[:, None] < hs[None])
    below = same_w & (hs[:, None] > hs[None])
    left = same_h & (ws[:, None] < ws[None])
    right = same_h & (ws[:, None] > ws[None])
    rows_out = np.stack([
        np.stack([((b // 2) * 64 + j * WS + ws)[:, None] == lane[None] for j in range(BJ)])
        for b in range(PACKS)
    ])
    cols_out = np.stack([
        np.stack([(b * 32 + i * HS + hs)[:, None] == lane[None] for i in range(BI)])
        for b in range(PACKS)
    ])

    def twice(m):
        return np.concatenate([m, m], -2)

    def wide(m):
        return twice(np.concatenate([np.swapaxes(m[:, k], -1, -2) for k in range(m.shape[1])], -1))

    def beside(m, order):
        return twice(np.concatenate([m, np.broadcast_to(order, m.shape)], -1))

    out = {
        "above": twice(above), "left": twice(left),
        "rows_above": beside(rows_out, above), "rows_below": beside(rows_out, below),
        "cols_left": beside(cols_out, left), "cols_right": beside(cols_out, right),
        "rows_in": wide(rows_out), "cols_in": wide(cols_out),
    }
    return {k: v.astype(np.float32) for k, v in out.items()}


def halves(x):
    high = x.astype(BF16)
    low = (x - high.astype(F32)).astype(BF16)
    return high, low


def lane_dot(matrix, *parts):
    parts = [h for x in parts for h in halves(x)]
    return jnp.dot(jnp.concatenate(parts, 1), matrix, preferred_element_type=F32)


def lane_dot_exact(x, matrix):
    high, low = halves(x)
    rest = (x - high.astype(F32) - low.astype(F32)).astype(BF16)
    return jnp.dot(
        jnp.concatenate([high, low], 1), matrix, preferred_element_type=F32
    ) + jnp.dot(rest, matrix[:LANES], preferred_element_type=F32)


def row_of(ref, p, n):
    return jnp.broadcast_to(ref[p, pl.ds(n, 1), :], (8, LANES))


def each_group(states, size, body):
    groups = states // size

    def one(at, carry):
        d = pl.ds(pl.multiple_of((at // groups) * 8, 8), 8)
        body([(at % groups) * size + k for k in range(size)], d)
        return carry

    lax.fori_loop(0, (BLOCK // 8) * groups, one, 0)


def run_segments(seg, matrix, t):
    states = seg.shape[0]
    at = pl.ds(t * PACK, PACK)
    total = None
    for k in range(4):
        both = lane_dot(matrix[t, k], seg[:, k, at].reshape(states * PACK, LANES))
        seg[:, k, at] = both[:, LANES:].reshape(states, PACK, LANES)
        total = both[:, :LANES] if total is None else total + both[:, :LANES]
    return total.reshape(states, PACK, LANES)


def send(b, seg, matrix, leaving, rows):
    @pl.when(b == 0)
    def _():
        leaving[...] = jnp.zeros_like(leaving)

    for t in range(INNER):
        q = b * INNER + t
        at = pl.ds(pl.multiple_of((q % 2) * PACK, PACK), PACK) if rows else slice(None)
        leaving[:, at] += run_segments(seg, matrix, t)


def take(b, seg, entering, enter, out, rows):
    states = seg.shape[0]
    for t in range(INNER):
        q = b * INNER + t
        at = pl.ds(pl.multiple_of((q % 2) * PACK, PACK), PACK) if rows else slice(None)
        first = lane_dot(enter[t], entering[:, at].reshape(states * PACK, LANES))
        at = pl.ds(t * PACK, PACK)
        for k in range(4):
            out[:, k, at] = seg[:, k, at] + first[:, k * LANES : (k + 1) * LANES].reshape(
                states, PACK, LANES
            )


def gather_plane(ref, j):
    return jnp.concatenate([ref[hs, 0, pl.ds(j, WS, stride=BJ), :] for hs in range(HS)], 0).T


def gather_states(ref, turned, out):
    for hs in range(HS):
        turned[hs] = ref[hs, 0].T
    for j in range(BJ):
        out[j] = jnp.concatenate(
            [turned[hs, pl.ds(j, WS, stride=BJ), :] for hs in range(HS)], 0
        ).T


def pack_rates(decay_log, rates, rates_v, rates_s):
    lane = lax.broadcasted_iota(jnp.int32, (PACK, LANES), 1)
    lane_v = lax.broadcasted_iota(jnp.int32, (2 * PACK, LANES), 1)
    rate = (-LOG2E * jnp.exp(decay_log[0])).T
    for n in range(rates.shape[0]):
        r = jnp.broadcast_to(rate[:, n : n + 1], (D, LANES))
        rates[n] = r
        for g in range(GROUPS):
            part = [r[g * CHANNELS + k * PACK : g * CHANNELS + (k + 1) * PACK] for k in range(4)]
            rates_v[g, n] = jnp.where(
                lane_v < 64, jnp.concatenate(part[:2], 0), jnp.concatenate(part[2:], 0)
            )
            rates_s[g, n] = jnp.where(
                lane < 64, jnp.where(lane < 32, part[0], part[1]),
                jnp.where(lane < 96, part[2], part[3]),
            )


def adjoint_cols_kernel(
    step, grad, read, decay_log, left, cols_right,
    step_p, grad_p, read_p, rates, rates_v, rates_s, before_cols, sum_cols, seg, sent,
    all_step, all_grad, all_rates, turned, leaving, *, share,
):
    states = seg.shape[0]
    i = pl.program_id(0)
    b = i - BI

    @pl.when(i < BI)
    def _():
        for j in range(BJ):
            s, g = gather_plane(step, j), gather_plane(grad, j)
            step_p[j] = s
            grad_p[j] = g
            all_step[i * BJ + j] = s
            all_grad[i * BJ + j] = g
        at = pl.ds(i * BJ, BJ)
        gather_states(read, turned, read_p.at[at])
        pack_rates(decay_log, rates, rates_v, rates_s)
        all_rates[pl.ds(i * (states // BI), states // BI)] = rates[...]
        row_total = step_p[0]
        for j in range(1, BJ):
            row_total = row_total + step_p[j]
        before_cols[i] = lane_dot_exact(row_total, left[...])

        @pl.when(i == 0)
        def _():
            sum_cols[...] = jnp.zeros_like(sum_cols)

        for g in range(GROUPS):
            for q in range(PACKS):
                at = g * CHANNELS + q * PACK
                sum_cols[g] += lane_dot_exact(
                    row_total[at : at + PACK], cols_right[q, i, :, :LANES]
                )

    @pl.when(i >= BI)
    def _():
        def group(ns, d):
            wide = pl.ds(pl.multiple_of(b * BLOCK + d.start, 8), 8)
            r = [all_rates[n, wide] for n in ns]
            for i in range(BI):
                acc = [None] * len(ns)
                c = before_cols[i, wide]
                for j in range(BJ):
                    p = i * BJ + j
                    c = c + all_step[p, wide]
                    g = all_grad[p, wide]
                    for k, n in enumerate(ns):
                        term = jnp.exp2(c * r[k]) * g * row_of(read_p, p, n)
                        acc[k] = term if acc[k] is None else acc[k] + term
                for k, n in enumerate(ns):
                    seg[n, i, d] = acc[k]

        each_group(states, 8, group)
        send(b, seg, cols_right.at[pl.ds(b * INNER, INNER)], leaving, False)

        @pl.when(b == STEPS - 1)
        def _():
            for k in range(states // share):
                sent[k, 0:share] = leaving[k * share : (k + 1) * share]
                sent[k, share] = sum_cols[0]


def forward_rows_kernel(
    feat, write, step_p, rates, rates_v, above, rows_above,
    source_p, write_p, before_rows, sum_rows, seg, leaving,
    all_step, all_source, turned, col_total,
):
    states = seg.shape[0]
    i = pl.program_id(0)
    b = i - BI

    @pl.when(i < BI)
    def _():
        for j in range(BJ):
            s = step_p[j]
            f = s * gather_plane(feat, j)
            source_p[j] = f
            all_step[i * BJ + j] = s
            all_source[i * BJ + j] = f
        gather_states(write, turned, write_p.at[pl.ds(i * BJ, BJ)])

        @pl.when(i == 0)
        def _():
            col_total[...] = step_p[...]

        @pl.when(i > 0)
        def _():
            col_total[...] += step_p[...]

        @pl.when(i == BI - 1)
        def _():
            for j in range(BJ):
                before_rows[j] = lane_dot_exact(col_total[j], above[...])
            for g in range(GROUPS):
                for r in range(2):
                    total = None
                    for q in (r, r + 2):
                        at = g * CHANNELS + q * PACK
                        for j in range(BJ):
                            one = lane_dot_exact(
                                col_total[j, at : at + PACK], rows_above[q, j, :, :LANES]
                            )
                            total = one if total is None else total + one
                    sum_rows[g, r * PACK : (r + 1) * PACK] = total

    @pl.when(i >= BI)
    def _():
        def group(ns, d):
            wide = pl.ds(pl.multiple_of(b * BLOCK + d.start, 8), 8)
            r = [-rates[n, d] for n in ns]
            for j in range(BJ):
                acc = [None] * len(ns)
                c = before_rows[j, wide]
                for i in range(BI):
                    p = i * BJ + j
                    c = c + all_step[p, wide]
                    s = all_source[p, wide]
                    for k, n in enumerate(ns):
                        term = jnp.exp2(c * r[k]) * s * row_of(write_p, p, n)
                        acc[k] = term if acc[k] is None else acc[k] + term
                for k, n in enumerate(ns):
                    seg[n, j, d] = acc[k]

        each_group(states, 8, group)
        send(b, seg, rows_above.at[pl.ds(b * INNER, INNER)], leaving, True)

        @pl.when(b == STEPS - 1)
        def _():
            for n in range(states):
                leaving[n] = leaving[n] * jnp.exp2(rates_v[0, n] * sum_rows[0])


def forward_cols_kernel(
    seg_rows, entering, step_p, source_p, write_p, rates, rates_s, before_rows, before_cols,
    sum_cols, rows_in, cols_out, start_rows, seg, leaving,
):
    states = seg.shape[0]
    b = pl.program_id(0)
    take(b, seg_rows, entering, rows_in, start_rows, True)

    def group(ns, d):
        r = [rates[n, d] for n in ns]
        vert = [[None] * BJ for _ in ns]
        for j in range(BJ):
            before = before_rows[j, d]
            for k, n in enumerate(ns):
                vert[k][j] = start_rows[n, j, d] * jnp.exp2(r[k] * before)
                start_rows[n, j, d] = vert[k][j]
        for i in range(BI):
            state = [None] * len(ns)
            after = before_cols[i, d]
            for j in range(BJ):
                p = i * BJ + j
                c, s = step_p[p, d], source_p[p, d]
                after = after + c
                for k, n in enumerate(ns):
                    decay = jnp.exp2(c * r[k])
                    vert[k][j] = decay * vert[k][j] + s * row_of(write_p, p, n)
                    state[k] = vert[k][j] if j == 0 else decay * state[k] + vert[k][j]
            for k, n in enumerate(ns):
                seg[n, i, d] = state[k] * jnp.exp2(-r[k] * after)

    each_group(states, 8, group)
    send(b, seg, cols_out, leaving, False)

    @pl.when(b == STEPS - 1)
    def _():
        for n in range(states):
            leaving[n] = leaving[n] * jnp.exp2(rates_s[0, n] * sum_cols[0])


def adjoint_rows_kernel(
    seg_cols, entering, step_p, grad_p, read_p, rates, rates_s, before_rows, before_cols,
    sum_cols, cols_in, rows_out, start_cols, seg, leaving, scaled,
):
    states = seg.shape[0]
    b = pl.program_id(0)

    @pl.when(b == 0)
    def _():
        for n in range(states):
            scaled[n] = entering[n] * jnp.exp2(rates_s[0, n] * sum_cols[0])

    take(b, seg_cols, scaled, cols_in, start_cols, False)

    def group(ns, d):
        r = [rates[n, d] for n in ns]
        passed_v = [[None] * BJ for _ in ns]
        for i in reversed(range(BI)):
            after = before_cols[i, d]
            for j in range(BJ):
                after = after + step_p[i * BJ + j, d]
            passed = []
            for k, n in enumerate(ns):
                passed.append(start_cols[n, i, d] * jnp.exp2(-r[k] * after))
                start_cols[n, i, d] = passed[k]
            for j in reversed(range(BJ)):
                p = i * BJ + j
                c, g = step_p[p, d], grad_p[p, d]
                for k, n in enumerate(ns):
                    decay = jnp.exp2(c * r[k])
                    adjoint = g * row_of(read_p, p, n) + passed[k]
                    passed[k] = decay * adjoint
                    if i == BI - 1:
                        passed_v[k][j] = passed[k]
                    else:
                        passed_v[k][j] = decay * (adjoint + passed_v[k][j])
        for j in range(BJ):
            before = before_rows[j, d]
            for k, n in enumerate(ns):
                seg[n, j, d] = passed_v[k][j] * jnp.exp2(r[k] * before)

    each_group(states, 8, group)
    send(b, seg, rows_out, leaving, True)


def final_kernel(
    start_rows, start_cols, seg_s, enter_s, seg_v, enter_v,
    step_p, source_p, grad_p, write_p, read_p, rates, rates_v, before_rows, before_cols, sum_rows,
    cols_in, rows_in,
    features_p, steps_p, sum_w, sum_r, grad_decay,
    in_s, in_v, scaled_v, decay_term, through, rate_term,
):
    states = rates.shape[0]
    b = pl.program_id(0)

    @pl.when(b == 0)
    def _():
        for n in range(states):
            scaled_v[n] = enter_v[n] * jnp.exp2(rates_v[0, n] * sum_rows[0])
        sum_w[...] = jnp.zeros_like(sum_w)
        sum_r[...] = jnp.zeros_like(sum_r)

    take(b, seg_s, enter_s, cols_in, in_s, False)
    take(b, seg_v, scaled_v, rows_in, in_v, True)
    through[...] = jnp.zeros_like(through)
    rate_term[...] = jnp.zeros_like(rate_term)

    def group(ns, d):
        many = range(len(ns))
        r = [rates[n, d] for n in ns]
        vert = [[start_rows[n, j, d] for j in range(BJ)] for n in ns]
        from_v, from_s = [{} for _ in many], [{} for _ in many]
        for i in range(BI):
            before = before_cols[i, d]
            state = [in_s[n, i, d] * jnp.exp2(r[k] * before) for k, n in enumerate(ns)]
            for j in range(BJ):
                p = i * BJ + j
                c, s, g = step_p[p, d], source_p[p, d], grad_p[p, d]
                for k, n in enumerate(ns):
                    m = c * r[k]
                    decay = jnp.exp2(m)
                    dv = decay * vert[k][j]
                    vert[k][j] = dv + s * row_of(write_p, p, n)
                    ds = decay * state[k]
                    state[k] = ds + vert[k][j]
                    sum_r[p, pl.ds(n * 8, 8)] += state[k] * g
                    from_v[k][p] = dv
                    from_s[k][p] = ds
        passed_v = [[None] * BJ for _ in ns]
        for j in range(BJ):
            after = before_rows[j, d]
            for i in range(BI):
                after = after + step_p[i * BJ + j, d]
            for k, n in enumerate(ns):
                passed_v[k][j] = in_v[n, j, d] * jnp.exp2(-r[k] * after)
        total = [None for _ in ns]
        for i in reversed(range(BI)):
            passed = [start_cols[n, i, d] for n in ns]
            for j in reversed(range(BJ)):
                p = i * BJ + j
                c, s, g = step_p[p, d], source_p[p, d], grad_p[p, d]
                sum_q, sum_t = None, None
                for k, n in enumerate(ns):
                    adjoint = g * row_of(read_p, p, n) + passed[k]
                    m = c * r[k]
                    decay = jnp.exp2(m)
                    passed[k] = decay * adjoint
                    adjoint_v = adjoint + passed_v[k][j]
                    passed_v[k][j] = decay * adjoint_v
                    q = (adjoint * from_s[k][p] + adjoint_v * from_v[k][p]) * m
                    total[k] = q if total[k] is None else total[k] + q
                    t = adjoint_v * row_of(write_p, p, n)
                    sum_q = q if sum_q is None else sum_q + q
                    sum_t = t if sum_t is None else sum_t + t
                    sum_w[p, pl.ds(n * 8, 8)] += adjoint_v * s
                rate_term[p, d] += sum_q
                through[p, d] += sum_t
        for k, n in enumerate(ns):
            decay_term[n, d] = total[k]

    each_group(states, 8, group)
    for p in range(POS):
        t = through[p]
        s = step_p[p]
        features_p[p] = s * t
        steps_p[p] = (source_p[p] * t + rate_term[p] * LN2) / s
    for n in range(states):
        all_decay = lax.dot_general(
            jnp.ones((8, 2 * LANES), BF16), jnp.concatenate(halves(decay_term[n]), 1),
            (((1,), (1,)), ((), ())), preferred_element_type=F32,
        )
        grad_decay[0, pl.ds(n, 1)] = all_decay[0:1] * LN2


def unpack_kernel(features_p, steps_p, sum_w, sum_r, features, steps, writes, reads, turned):
    for j in range(BJ):
        for values, out in ((features_p, features), (steps_p, steps)):
            back = values[j].T
            for hs in range(HS):
                out[hs, 0, pl.ds(j, WS, stride=BJ), :] = back[hs * WS : hs * WS + WS]
    for values, out in ((sum_w, writes), (sum_r, reads)):
        for j in range(BJ):
            states = writes.shape[2]
            back = sum(values[j, pl.ds(k, states, stride=8), :] for k in range(8)).T
            for hs in range(HS):
                turned[hs, pl.ds(j, WS, stride=BJ), :] = back[hs * WS : hs * WS + WS]
        for hs in range(HS):
            out[hs, 0] = turned[hs].T


def prefix_kernel(held, sums, rates, out, *, reverse):
    size, share = out.shape[:2]
    at = sums.shape[1] - 1
    order = list(reversed(range(size))) if reverse else list(range(size))
    for n in range(share):
        before = jnp.zeros(out.shape[2:], F32)
        for k in order:
            out[k, n] = before
            before = jnp.exp2(rates[n] * sums[k, at]) * before + held[k, n]


def run(kernel, ins, outs, scratch=(), group=0, micros=5, steps=STEPS, lead=0, limit=60):
    parts = lead if lead else steps

    def early(b):
        return jnp.minimum(b, lead - 1) if lead else b

    def late(b):
        return jnp.maximum(b - lead, 0) if lead else b

    def spec(shape, kind):
        rank = len(shape)
        block, at = list(shape), [None] * rank
        if kind == "first":
            block[0], at[0] = shape[0] // parts, early
        elif kind == "second":
            block[1], at[1] = 1, early
        elif kind == "states":
            block[1], at[1] = shape[1] // parts, early
        elif kind == "group":
            block[0], at[0] = 1, lambda b: group
        elif kind == "plane":
            block[-2], at[-2] = BLOCK, lambda b: group * STEPS + late(b)
        elif kind == "own":
            block[-2], at[-2] = BLOCK, late
        return pl.BlockSpec(tuple(block), lambda b: tuple(0 if f is None else f(b) for f in at))

    return pl.pallas_call(
        kernel,
        grid=(lead + steps,),
        out_shape=[jax.ShapeDtypeStruct(s, F32) for s, _ in outs],
        in_specs=[spec(a.shape, kind) for a, kind in ins],
        out_specs=[spec(s, kind) for s, kind in outs],
        scratch_shapes=[pltpu.VMEM(s, F32) for s in scratch],
        compiler_params=pltpu.CompilerParams(
            vmem_limit_bytes=limit << 20, dimension_semantics=("arbitrary",)
        ),
        cost_estimate=pl.CostEstimate(
            flops=0, bytes_accessed=int(micros * 3.3e6), transcendentals=0
        ),
    )(*[a for a, _ in ins])


def swap_cores(x, size):
    return lax.ppermute(x, "row", [(k, k ^ 1) for k in range(size)])


def tied(*arrays):
    return lax.optimization_barrier(arrays)


def row_total(leaving, sums, other_sums, rates, size, reverse):
    count = leaving.shape[0] // 2
    core = lax.axis_index("row") % 2
    mine = lax.dynamic_slice_in_dim(leaving, core * count, count, 0)
    theirs = swap_cores(lax.dynamic_slice_in_dim(leaving, (1 - core) * count, count, 0), size)
    rate = lax.dynamic_slice_in_dim(rates, core * count, count, 0)
    first = core == (1 if reverse else 0)
    near = jnp.where(first, mine, theirs)
    far = jnp.where(first, theirs, mine)
    near_sum = jnp.where(first, sums, other_sums)
    far_sum = jnp.where(first, other_sums, sums)
    total = far + jnp.exp2(rate * far_sum) * near
    return total, near, near_sum, far_sum, rate


def row_carry(total, near, near_sum, far_sum, rate, beside, size, reverse):
    core = lax.axis_index("row") % 2
    first = core == (1 if reverse else 0)
    sign = -2 if reverse else 2

    def shift(x, by):
        return lax.ppermute(
            x, "row", [(k, k + by) for k in range(size) if 0 <= k + by < size]
        )

    entering = shift(total, sign)
    if size > 4:
        span = shift(near_sum + far_sum, sign)
        by = sign
        while abs(by) < size - 2:
            entering = entering + jnp.exp2(rate * span) * shift(entering, by)
            span = span + shift(span, by)
            by *= 2
    entering, _ = tied(entering, beside)
    to_far = near + jnp.exp2(rate * near_sum) * entering
    keep = jnp.where(first, entering, to_far)
    got = swap_cores(jnp.where(first, to_far, entering), size)
    return jnp.concatenate(
        [jnp.where(core == 0, keep, got), jnp.where(core == 0, got, keep)], 0
    )


def col_gather(sent):
    return lax.all_to_all(sent, "col", 0, 0)


def col_carry(held, sums, rates, reverse):
    size, share = held.shape[0], rates.shape[0]
    vmem = pl.BlockSpec(memory_space=pltpu.VMEM)
    return pl.pallas_call(
        functools.partial(prefix_kernel, reverse=reverse),
        out_shape=jax.ShapeDtypeStruct((size, share) + held.shape[2:], F32),
        in_specs=[vmem] * 3,
        out_specs=vmem,
        compiler_params=pltpu.CompilerParams(vmem_limit_bytes=4 << 20),
    )(held, sums, rates)


def col_return(carries):
    back = lax.all_to_all(carries, "col", 0, 0)
    return back.reshape((-1,) + carries.shape[2:])


def total_of(x, rows, cols):
    for axis, size in (("row", rows), ("col", cols)):
        by = 1
        while by < size:
            x = x + lax.ppermute(x, axis, [(k, k ^ by) for k in range(size)])
            by *= 2
    return x


def shards(features, step_size, write_weights, read_weights, decay_log, out_grad, sizes):
    rows, cols = sizes
    states = decay_log.shape[0]
    share = states // cols
    tile_h, tile_w = features.shape[:2]
    mats = {k: jnp.asarray(v, BF16) for k, v in lane_matrices().items()}
    plane, quad = (POS, D, LANES), (4, D, LANES)
    seg = (states, 4, CHANNELS, LANES)
    small = (POS, states, LANES)
    packed = (HS, BI, tile_w, D)
    weights = (HS, BI, states, tile_w)
    size_v, size_s = (states, CHANNELS // 2, LANES), (states, CHANNELS // 4, LANES)
    me = lax.axis_index("col")
    todo = range(GROUPS)
    enter_rows, enter_cols, enter_s, enter_v = {}, {}, {}, {}
    seg_rows, seg_cols, seg_s, seg_v, start_rows, start_cols, col_sums = {}, {}, {}, {}, {}, {}, {}
    rate_s = {}
    for g in todo:
        (step_p, grad_p, read_p, rates, rates_v, rates_s, before_cols, sum_cols, seg_cols[g],
         sent) = run(
            functools.partial(adjoint_cols_kernel, share=share),
            [(step_size.reshape(packed), "second"), (out_grad.reshape(packed), "second"),
             (read_weights.swapaxes(1, 2).reshape(weights), "second"),
             (decay_log.reshape(BI, states // BI, D), "first"), (mats["left"], "whole"),
             (mats["cols_right"], "whole")],
            [(plane, "first"), (plane, "first"), (small, "whole"),
             ((states, D, LANES), "first"), ((GROUPS,) + size_v, "states"),
             ((GROUPS,) + size_s, "states"), (quad, "whole"), ((GROUPS,) + size_s[1:], "whole"),
             (seg, "own"), ((cols, share + 1) + size_s[1:], "whole")],
            [plane, plane, (states, D, LANES), (HS, tile_w, states), size_s], g, lead=BI,
        )
        rate_s[g] = lax.dynamic_slice_in_dim(rates_s[g], me * share, share, 0)
        held = col_gather(sent)
        step_p, _, rate_s[g] = tied(step_p, sent, rate_s[g])
        source_p, write_p, before_rows, sum_rows, seg_rows[g], leave_rows = run(
            forward_rows_kernel,
            [(features.reshape(packed), "second"),
             (write_weights.swapaxes(1, 2).reshape(weights), "second"), (step_p, "first"),
             (rates, "plane"), (rates_v, "group"), (mats["above"], "whole"),
             (mats["rows_above"], "whole")],
            [(plane, "first"), (small, "whole"), (quad, "whole"),
             ((GROUPS,) + size_v[1:], "whole"), (seg, "own"), (size_v, "whole")],
            [plane, plane, (HS, tile_w, states), quad], g, lead=BI,
        )
        other_rows = swap_cores(sum_rows, rows)
        total = row_total(leave_rows, sum_rows[g], other_rows[g], rates_v[g], rows, False)
        held, first = tied(held, total[0])
        col_sums[g] = held
        carries = col_carry(held, held, rate_s[g], True)
        enter_cols[g] = col_return(carries)
        enter_rows[g] = row_carry(first, *total[1:], carries, rows, False)
    for g in todo:
        start_rows[g], seg_s[g], leave_s = run(
            forward_cols_kernel,
            [(seg_rows[g], "own"), (enter_rows[g], "whole"), (step_p, "plane"),
             (source_p, "plane"), (write_p, "whole"), (rates, "plane"), (rates_s, "group"),
             (before_rows, "plane"), (before_cols, "plane"), (sum_cols, "group"),
             (mats["rows_in"], "first"), (mats["cols_left"], "first")],
            [(seg, "own"), (seg, "own"), (size_s, "whole")], (), g, 10,
        )
        held = col_gather(leave_s.reshape((cols, share) + size_s[1:]))
        enter_cols[g], _ = tied(enter_cols[g], leave_s)
        start_cols[g], seg_v[g], leave_v = run(
            adjoint_rows_kernel,
            [(seg_cols[g], "own"), (enter_cols[g], "whole"), (step_p, "plane"),
             (grad_p, "plane"), (read_p, "whole"), (rates, "plane"), (rates_s, "group"),
             (before_rows, "plane"), (before_cols, "plane"), (sum_cols, "group"),
             (mats["cols_in"], "first"), (mats["rows_below"], "first")],
            [(seg, "own"), (seg, "own"), (size_v, "whole")], [size_s], g, 10,
        )
        held, leave_v = tied(held, leave_v)
        carries = col_carry(held, col_sums[g], rate_s[g], False)
        enter_s[g] = col_return(carries)
        leave_v, carries = tied(leave_v, carries)
        total = row_total(leave_v, sum_rows[g], other_rows[g], rates_v[g], rows, True)
        enter_v[g] = row_carry(*total, enter_s[g], rows, True)
    sums = (POS, states * 8, LANES)
    own_plane = (POS, CHANNELS, LANES)
    parts = []
    for g in todo:
        parts.append(run(
            final_kernel,
            [(start_rows[g], "own"), (start_cols[g], "own"), (seg_s[g], "own"),
             (enter_s[g], "whole"), (seg_v[g], "own"), (enter_v[g], "whole"), (step_p, "plane"),
             (source_p, "plane"), (grad_p, "plane"), (write_p, "whole"), (read_p, "whole"),
             (rates, "plane"), (rates_v, "group"), (before_rows, "plane"),
             (before_cols, "plane"), (sum_rows, "group"), (mats["cols_in"], "first"), (mats["rows_in"], "first")],
            [(own_plane, "own"), (own_plane, "own"), (sums, "whole"), (sums, "whole"),
             ((STEPS, states, BLOCK), "first")],
            [(states, 4, BLOCK, LANES), (states, 4, BLOCK, LANES), size_v,
             (states, BLOCK, LANES), (POS, BLOCK, LANES), (POS, BLOCK, LANES)],
            g, 27,
        ))
    features_p, steps_p, sum_w, sum_r, grad_decay = parts[0]
    grad_decay = grad_decay.swapaxes(0, 1).reshape(states, D)
    grad_decay = total_of(grad_decay, rows, cols)
    grad_features, grad_step, grad_write, grad_read = run(
        unpack_kernel,
        [(features_p, "first"), (steps_p, "first"), (sum_w, "first"), (sum_r, "first")],
        [(packed, "second"), (packed, "second"), (weights, "second"), (weights, "second")],
        [(HS, tile_w, states)], 0, 5, BI,
    )
    weights = (tile_h, states, tile_w)
    return (
        grad_features.reshape(features.shape),
        grad_step.reshape(features.shape),
        grad_write.reshape(weights).swapaxes(1, 2),
        grad_read.reshape(weights).swapaxes(1, 2),
        grad_decay,
    )


def solution(mesh):
    spec = P("row", "col", None)
    sizes = (mesh.shape["row"], mesh.shape["col"])
    return jax.shard_map(
        functools.partial(shards, sizes=sizes),
        mesh=mesh,
        in_specs=(spec, spec, spec, spec, P(), spec),
        out_specs=(spec, spec, spec, spec, P()),
        check_vma=False,
    )
```

time: 931 us -> 157 us (0.17); the launches traced: 915 us -> 156 us
  other arithmetic: 651 us -> 7.31 us
  local copies, waits for them, and re-layouts: 97.6 us -> 3.57 us
  Pallas kernels: 0 us -> 81.6 us
  matrix products: 74.5 us -> 0 us
  blocking collectives: 39.6 us -> 0 us
  starting transfers between devices: 0.71 us -> 37.9 us
  between operations: 14.8 us -> 0.84 us
  waiting for transfers between devices: 34.9 us -> 24.9 us
    dynamic_update_slice x192 -> x0, other arithmetic: 376 us -> none  [the longest x64 142 us: sweep_rows(): closing, values = lax.scan(advance, initial, (decays, driving))]
    mul x100 -> x1, other arithmetic: 147 us -> 0.77 us  [row_carry(): to_far = near + jnp.exp2(rate * near_sum) * entering]
    pallas_call x0 -> x8, Pallas kernels: none -> 81.6 us  [the longest x6 80.1 us: run(): pl.pallas_call(kernel, grid=(lead + steps,), out_shape=[jax.ShapeDtypeStr...]
    dot_general x3 -> x0, matrix products: 74.5 us -> none  [the longest x1 28.9 us: shards(): jnp.einsum('hwnd,hwd->hwn', adjoint_v, step_size * features, precision=hi...]
    psum x1 -> x0, blocking collectives: 39.6 us -> none  [shards(): grad_decay = lax.psum(partial_sum, ('row', 'col')) * decay_rate]
    select_n x24 -> x4, other arithmetic: 38.1 us -> 2.19 us  [the longest x2 2.07 us: row_carry(): got = swap_cores(jnp.where(first, to_far, entering), size)]
    all_gather x6 -> x0, waiting for transfers between devices: 34.8 us -> none  [carried_in(): everything = jax.tree.map(lambda part: lax.all_gather(part, axis), shard)]
    dot_general x1 -> x0, other arithmetic: 34.6 us -> none  [shards(): jnp.einsum('hwnd,hwd->nd', exponent_grad, step_size, precision=highest)]
  transfers between devices with their start and end apart: 6 -> 16, of which waited for: 1 -> 9; matrix products, arithmetic and copies ran while one was open for 48% -> 4% of each run, Pallas kernels for 0% -> 27%
where the time goes in v2:
time: 157 us; the launch traced here: 156 us
  Pallas kernels  81.6 us (52%)
  starting transfers between devices  37.9 us (24%)
  waiting for transfers between devices  24.9 us (16%)
  other arithmetic  7.31 us (5%)
  local copies, waits for them, and re-layouts  3.57 us (2%)
    pallas_call x6, Pallas kernels, run(): pl.pallas_call(kernel, grid=(lead + steps,), out_shape=[jax.ShapeDtypeStr...  80.1 us
    all_to_all x2, starting transfers between devices, col_gather(): return lax.all_to_all(sent, 'col', 0, 0)  13.4 us
    all_to_all x2, starting transfers between devices, col_return(): back = lax.all_to_all(carries, 'col', 0, 0)  12 us
    ppermute x5, waiting for transfers between devices, total_of(): x = x + lax.ppermute(x, axis, [(k, k ^ by) for k in range(size)])  7.85 us
    all_to_all x2, waiting for transfers between devices, col_return(): back = lax.all_to_all(carries, 'col', 0, 0)  7.23 us
    ppermute x2, waiting for transfers between devices, shift(): lax.ppermute(x, 'row', [(k, k + by) for k in range(size) if 0 <= k + by <...  6.97 us
    ppermute x5, starting transfers between devices, total_of(): x = x + lax.ppermute(x, axis, [(k, k ^ by) for k in range(size)])  6.92 us
    ppermute x2, starting transfers between devices, shift(): lax.ppermute(x, 'row', [(k, k + by) for k in range(size) if 0 <= k + by <...  4.73 us
  transfers between devices with their start and end apart: 16, of which 9 were waited for; matrix products, arithmetic and copies ran while one was open for 4% of the time, Pallas kernels for 27%

profile of v2, /device:TPU:0, one launch (start us, length us, event | category | flops | bytes accessed | tf_op | source)
XLA Modules:
  0.0 156.0 jit_solution(16900847313209569322)
XLA Ops:
  0.6 12.8 %shard_map.173 = (f32[16,128,128]{2,1,0:T(8,128)}, f32[16,128,128]{2,1,0:T(8,128)}, f32[16,16,128]{2,1,0:T(8,128)}, f32[16,128,128]{2,1,0:T(8,128)}, f32[1,16,64...) custom-call(f32[8,4,64,128]{3,2,1,0:T(8,128)} %bitcast.72, ...), custom_call_target="tpu_custom_call" | custom-call | bytes 16500000 | tf_op jit(solution)/shard_map/pallas_call | solution.py:526
  13.5 7.4 %all-to-all-start = ((f32[8,3,32,128]{3,2,1,0:T(8,128)}), f32[8,3,32,128]{3,2,1,0:T(8,128)S(1)}, u32[]{:S(2)}, u32[]{:S(2)}) async-start(f32[8,3,32,128]{3,2,1,0:T(8,128)} %get-tuple-element.47), calls=%async_computation | async-start | bytes 786432 | tf_op jit(solution)/shard_map/all_to_all | solution.py:593
  20.9 0.8 dynamic-slice_bitcast_fusion.rates
  21.6 12.0 %shard_map.174 = (f32[16,128,128]{2,1,0:T(8,128)}, f32[16,16,128]{2,1,0:T(8,128)}, f32[4,128,128]{2,1,0:T(8,128)}, f32[1,64,128]{2,1,0:T(8,128)}, f32[16,4,128,128]{3,2,1,0:T(8,128)}, /*index=5*/f32[16,64,128]{2,1,0:T(8,128)}) custom-call(f32[8,4,64,128]{3,2,1,0:T(8,128)} %bitcast.75, f32[8,4,16,64]{3,2,1,0:T(8,128)} %bitcast.77, ...), custom_call_target="tpu_custom_call" | custom-call | bytes 16500000 | tf_op jit(solution)/shard_map/pallas_call | solution.py:526
  33.6 1.0 constant_dynamic-slice_fusion.1
  34.6 0.1 collective-permute-start
  34.6 0.5 collective-permute-start.1
  35.1 1.3 collective-permute-done.1
  36.4 0.8 select_bitcast_fusion
  37.2 1.0 fusion.3
  38.3 3.4 %collective-permute-start.2 = (f32[8,64,128]{2,1,0:T(8,128)S(1)}, f32[8,64,128]{2,1,0:T(8,128)S(1)}, u32[]{:S(2)}, u32[]{:S(2)}) collective-permute-start(f32[8,64,128]{2,1,0:T(8,128)S(1)} %fusion.3), channel_id=1, source_target_pairs={{0,16},{8,24},{1,17},{9,25},{2,18},{10,26},{3,19},{11,27},{4,20},{... | collective-permute-start | bytes 786440 | tf_op jit(solution)/shard_map/ppermute | solution.py:571
  41.7 0.7 shard_map.175
  42.4 5.1 %collective-permute-done.2 = f32[8,64,128]{2,1,0:T(8,128)S(1)} collective-permute-done((f32[8,64,128]{2,1,0:T(8,128)S(1)}, f32[8,64,128]{2,1,0:T(8,128)S(1)}, u32[]{:S(2)}, u32[]{:S(2)}) %collective-permute-start.2) | collective-permute-done | bytes 262176 | tf_op jit(solution)/shard_map/ppermute | solution.py:571
  47.5 1.0 broadcast_select_fusion.6
  48.6 0.1 collective-permute-start.3
  48.7 6.0 %all-to-all-start.1 = ((f32[8,2,32,128]{3,2,1,0:T(8,128)}), f32[8,2,32,128]{3,2,1,0:T(8,128)S(1)}, u32[]{:S(2)}, u32[]{:S(2)}) async-start(f32[8,2,32,128]{3,2,1,0:T(8,128)} %shard_map.175), calls=%async_computation.1 | async-start | bytes 524288 | tf_op jit(solution)/shard_map/all_to_all | solution.py:609
  54.7 0.1 broadcast_select_fusion.5
  54.7 0.8 pad_maximum_fusion.entering
  55.6 12.5 %shard_map.176 = (f32[16,4,128,128]{3,2,1,0:T(8,128)}, f32[16,4,128,128]{3,2,1,0:T(8,128)}, f32[16,32,128]{2,1,0:T(8,128)}) custom-call(f32[16,4,128,128]{3,2,1,0:T(8,128)} %get-tuple-element.52.seg_rows, f32[16,64,128]{2,1,0:T(8,128)} %pad_maximum_fusion.entering, f32[16,128,128]{2,1,0:T(8,128)} %get-tuple-element.49.step_p, ...), custom_call_target="tpu_custom_call" | custom-call | bytes 33000000 | tf_op jit(solution)/shard_map/pallas_call | solution.py:526
  68.1 6.0 %all-to-all-start.2 = ((f32[8,2,32,128]{3,2,1,0:T(8,128)}), f32[8,2,32,128]{3,2,1,0:T(8,128)S(1)}, u32[]{:S(2)}, u32[]{:S(2)}) async-start(f32[8,2,32,128]{3,2,1,0:T(8,128)} %bitcast.78), calls=%async_computation.2 | async-start | bytes 524288 | tf_op jit(solution)/shard_map/all_to_all | solution.py:593
  74.1 12.4 %shard_map.177 = (f32[16,4,128,128]{3,2,1,0:T(8,128)}, f32[16,4,128,128]{3,2,1,0:T(8,128)}, f32[16,64,128]{2,1,0:T(8,128)}) custom-call(f32[16,4,128,128]{3,2,1,0:T(8,128)} %get-tuple-element.65.seg_cols, f32[16,32,128]{2,1,0:T(8,128)} %bitcast.74, f32[16,128,128]{2,1,0:T(8,128)} %get-tuple-element.49.step_p, f32[16,128,128]{2,1,0:T(8,128)} %get-tuple-element.68.grad_p, ...), custom_call_target="tpu_custom_call" | custom-call | bytes 33000000 | tf_op jit(solution)/shard_map/pallas_call | solution.py:526
  86.5 0.7 shard_map.178
  87.2 1.0 constant_dynamic-slice_fusion
  88.2 0.1 collective-permute-start.4
  88.3 6.0 %all-to-all-start.3 = ((f32[8,2,32,128]{3,2,1,0:T(8,128)}), f32[8,2,32,128]{3,2,1,0:T(8,128)S(1)}, u32[]{:S(2)}, u32[]{:S(2)}) async-start(f32[8,2,32,128]{3,2,1,0:T(8,128)} %shard_map.178), calls=%async_computation.3 | async-start | bytes 524288 | tf_op jit(solution)/shard_map/all_to_all | solution.py:609
  94.3 1.0 fusion.11
  95.3 1.3 collective-permute-start.5
  96.6 7.2 %all-to-all-done.3 = f32[8,2,32,128]{3,2,1,0:T(8,128)S(1)} async-done(((f32[8,2,32,128]{3,2,1,0:T(8,128)}), f32[8,2,32,128]{3,2,1,0:T(8,128)S(1)}, u32[]{:S(2)}, u32[]{:S(2)}) %all-to-all-start.3) | async-done | bytes 262176 | tf_op jit(solution)/shard_map/all_to_all | solution.py:609
  103.8 1.9 %collective-permute-done.5 = f32[8,64,128]{2,1,0:T(8,128)S(1)} collective-permute-done((f32[8,64,128]{2,1,0:T(8,128)S(1)}, f32[8,64,128]{2,1,0:T(8,128)S(1)}, u32[]{:S(2)}, u32[]{:S(2)}) %collective-permute-start.5) | collective-permute-done | bytes 262176 | tf_op jit(solution)/shard_map/ppermute | solution.py:571
  105.7 1.0 broadcast_select_fusion
  106.8 0.1 collective-permute-start.6
  106.8 1.5 collective-permute-done.6
  108.4 0.1 broadcast_select_fusion.3
  108.4 0.8 pad_maximum_fusion.1.enter_v
  109.3 25.2 %shard_map.179 = (f32[16,128,128]{2,1,0:T(8,128)}, f32[16,128,128]{2,1,0:T(8,128)}, f32[16,128,128]{2,1,0:T(8,128)}, f32[16,128,128]{2,1,0:T(8,128)}, f32[4,16,32]{2,1,0:T(8,128)}) custom-call(f32[16,4,128,128]{3,2,1,0:T(8,128)} %get-tuple-element.64.start_rows, f32[16,4,128,128]{3,2,1,0:T(8,128)} %get-tuple-element.70.start_cols, ...), custom_call_target="tpu_custom_call" | custom-call | bytes 89100000 | tf_op jit(solution)/shard_map/pallas_call | solution.py:526
  134.5 0.8 copy.19
  135.3 0.1 reshape.67
  135.4 0.1 collective-permute-start.7
  135.5 1.0 collective-permute-done.7
  136.6 0.7 collective-permute-start.8
  137.2 3.0 %collective-permute-done.8 = f32[16,128]{1,0:T(8,128)S(1)} collective-permute-done((f32[16,128]{1,0:T(8,128)S(1)}, f32[16,128]{1,0:T(8,128)S(1)}, u32[]{:S(2)}, u32[]{:S(2)}) %collective-permute-start.8) | collective-permute-done | bytes 8224 | tf_op jit(solution)/shard_map/ppermute | solution.py:617
  140.2 1.7 %collective-permute-start.9 = (f32[16,128]{1,0:T(8,128)S(1)}, f32[16,128]{1,0:T(8,128)S(1)}, u32[]{:S(2)}, u32[]{:S(2)}) collective-permute-start(f32[16,128]{1,0:T(8,128)S(1)} %add.56), channel_id=1, source_target_pairs={{0,1},{1,0},{2,3},{3,2},{4,5},{5,4},{6,7},{7,6},{8,9},{9,8},{10,11... | collective-permute-start | bytes 24584 | tf_op jit(solution)/shard_map/ppermute | solution.py:617
  141.9 1.9 %collective-permute-done.9 = f32[16,128]{1,0:T(8,128)S(1)} collective-permute-done((f32[16,128]{1,0:T(8,128)S(1)}, f32[16,128]{1,0:T(8,128)S(1)}, u32[]{:S(2)}, u32[]{:S(2)}) %collective-permute-start.9) | collective-permute-done | bytes 8224 | tf_op jit(solution)/shard_map/ppermute | solution.py:617
  143.9 1.7 %collective-permute-start.10 = (f32[16,128]{1,0:T(8,128)S(1)}, f32[16,128]{1,0:T(8,128)S(1)}, u32[]{:S(2)}, u32[]{:S(2)}) collective-permute-start(f32[16,128]{1,0:T(8,128)S(1)} %add.57), channel_id=1, source_target_pairs={{0,2},{1,3},{2,0},{3,1},{4,6},{5,7},{6,4},{7,5},{8,10},{9,11},{10,... | collective-permute-start | bytes 24584 | tf_op jit(solution)/shard_map/ppermute | solution.py:617
  145.6 1.9 %collective-permute-done.10 = f32[16,128]{1,0:T(8,128)S(1)} collective-permute-done((f32[16,128]{1,0:T(8,128)S(1)}, f32[16,128]{1,0:T(8,128)S(1)}, u32[]{:S(2)}, u32[]{:S(2)}) %collective-permute-start.10) | collective-permute-done | bytes 8224 | tf_op jit(solution)/shard_map/ppermute | solution.py:617
  147.5 2.6 %collective-permute-start.11 = (f32[16,128]{1,0:T(8,128)S(1)}, f32[16,128]{1,0:T(8,128)S(1)}, u32[]{:S(2)}, u32[]{:S(2)}) collective-permute-start(f32[16,128]{1,0:T(8,128)S(1)} %add.58), channel_id=1, source_target_pairs={{0,4},{1,5},{2,6},{3,7},{4,0},{5,1},{6,2},{7,3},{8,12},{9,13},{10,... | collective-permute-start | bytes 24584 | tf_op jit(solution)/shard_map/ppermute | solution.py:617
  150.2 5.3 %shard_map.180 = (f32[8,4,64,128]{3,2,1,0:T(8,128)}, f32[8,4,64,128]{3,2,1,0:T(8,128)}, f32[8,4,16,64]{3,2,1,0:T(8,128)}, f32[8,4,16,64]{3,2,1,0:T(8,128)}) custom-call(f32[16,128,128]{2,1,0:T(8,128)} %get-tuple-element.78.features_p, f32[16,128,128]{2,1,0:T(8,128)} %get-tuple-element.79.steps_p, f32[16,128,128]{2,1,0:T(8,128)} %get-tuple-element.80.sum_w, ...), custom_call_target="tpu_custom_call" | custom-call | bytes 16500000 | tf_op jit(solution)/shard_map/pallas_call | solution.py:526
  155.4 0.6 add.59
  (17 shorter events, 0.0 us)
Async XLA Ops:
  13.4 23.8 %copy-start = (f32[1,16,64,128]{3,2,1,0:T(8,128)S(1)}, f32[1,16,64,128]{3,2,1,0:T(8,128)}, u32[]{:S(2)}) copy-start(f32[1,16,64,128]{3,2,1,0:T(8,128)} %get-tuple-element.51.rates_v) | copy-start | bytes 1572868
  13.5 24.8 %all-to-all-start = ((f32[8,3,32,128]{3,2,1,0:T(8,128)}), f32[8,3,32,128]{3,2,1,0:T(8,128)S(1)}, u32[]{:S(2)}, u32[]{:S(2)}) async-start(f32[8,3,32,128]{3,2,1,0:T(8,128)} %get-tuple-element.47), calls=%async_computation | async-start | bytes 786432 | tf_op jit(solution)/shard_map/all_to_all | solution.py:593
  34.6 2.6 %collective-permute-start = (f32[8,64,128]{2,1,0:T(8,128)S(1)}, f32[8,64,128]{2,1,0:T(8,128)S(1)}, u32[]{:S(2)}, u32[]{:S(2)}) collective-permute-start(f32[8,64,128]{2,1,0:T(8,128)S(1)} %constant_dynamic-slice_fusion.1), channel_id=1, source_target_pairs={{0,8},{8,0},{16,24},{24,16},{1,9},{9,1},{17,25},{25,17},{2,10},{10... | collective-permute-start | bytes 786440 | tf_op jit(solution)/shard_map/ppermute | solution.py:543
  34.6 1.8 %collective-permute-start.1 = (f32[1,64,128]{2,1,0:T(8,128)}, f32[1,64,128]{2,1,0:T(8,128)S(1)}, u32[]{:S(2)}, u32[]{:S(2)}) collective-permute-start(f32[1,64,128]{2,1,0:T(8,128)} %get-tuple-element.54.sum_rows), channel_id=1, source_target_pairs={{0,8},{8,0},{16,24},{24,16},{1,9},{9,1},{17,25},{25,17},{2,10},{10... | collective-permute-start | bytes 98312 | tf_op jit(solution)/shard_map/ppermute | solution.py:543
  38.3 9.3 %collective-permute-start.2 = (f32[8,64,128]{2,1,0:T(8,128)S(1)}, f32[8,64,128]{2,1,0:T(8,128)S(1)}, u32[]{:S(2)}, u32[]{:S(2)}) collective-permute-start(f32[8,64,128]{2,1,0:T(8,128)S(1)} %fusion.3), channel_id=1, source_target_pairs={{0,16},{8,24},{1,17},{9,25},{2,18},{10,26},{3,19},{11,27},{4,20},{... | collective-permute-start | bytes 786440 | tf_op jit(solution)/shard_map/ppermute | solution.py:571
  48.6 6.1 %collective-permute-start.3 = (f32[8,64,128]{2,1,0:T(8,128)S(1)}, f32[8,64,128]{2,1,0:T(8,128)S(1)}, u32[]{:S(2)}, u32[]{:S(2)}) collective-permute-start(f32[8,64,128]{2,1,0:T(8,128)S(1)} %get-tuple-element.89), channel_id=1, source_target_pairs={{0,8},{8,0},{16,24},{24,16},{1,9},{9,1},{17,25},{25,17},{2,10},{10... | collective-permute-start | bytes 786440 | tf_op jit(solution)/shard_map/ppermute | solution.py:543
  48.7 19.4 %all-to-all-start.1 = ((f32[8,2,32,128]{3,2,1,0:T(8,128)}), f32[8,2,32,128]{3,2,1,0:T(8,128)S(1)}, u32[]{:S(2)}, u32[]{:S(2)}) async-start(f32[8,2,32,128]{3,2,1,0:T(8,128)} %shard_map.175), calls=%async_computation.1 | async-start | bytes 524288 | tf_op jit(solution)/shard_map/all_to_all | solution.py:609
  68.1 6.0 %copy-start.2 = (f32[8,2,32,128]{3,2,1,0:T(8,128)}, f32[8,2,32,128]{3,2,1,0:T(8,128)S(1)}, u32[]{:S(2)}) copy-start(f32[8,2,32,128]{3,2,1,0:T(8,128)S(1)} %all-to-all-done.1) | copy-start | bytes 786436
  68.1 18.4 %all-to-all-start.2 = ((f32[8,2,32,128]{3,2,1,0:T(8,128)}), f32[8,2,32,128]{3,2,1,0:T(8,128)S(1)}, u32[]{:S(2)}, u32[]{:S(2)}) async-start(f32[8,2,32,128]{3,2,1,0:T(8,128)} %bitcast.78), calls=%async_computation.2 | async-start | bytes 524288 | tf_op jit(solution)/shard_map/all_to_all | solution.py:593
  88.2 6.1 %collective-permute-start.4 = (f32[8,64,128]{2,1,0:T(8,128)S(1)}, f32[8,64,128]{2,1,0:T(8,128)S(1)}, u32[]{:S(2)}, u32[]{:S(2)}) collective-permute-start(f32[8,64,128]{2,1,0:T(8,128)S(1)} %constant_dynamic-slice_fusion), channel_id=1, source_target_pairs={{0,8},{8,0},{16,24},{24,16},{1,9},{9,1},{17,25},{25,17},{2,10},{10... | collective-permute-start | bytes 786440 | tf_op jit(solution)/shard_map/ppermute | solution.py:543
  88.3 15.6 %all-to-all-start.3 = ((f32[8,2,32,128]{3,2,1,0:T(8,128)}), f32[8,2,32,128]{3,2,1,0:T(8,128)S(1)}, u32[]{:S(2)}, u32[]{:S(2)}) async-start(f32[8,2,32,128]{3,2,1,0:T(8,128)} %shard_map.178), calls=%async_computation.3 | async-start | bytes 524288 | tf_op jit(solution)/shard_map/all_to_all | solution.py:609
  95.3 10.4 %collective-permute-start.5 = (f32[8,64,128]{2,1,0:T(8,128)S(1)}, f32[8,64,128]{2,1,0:T(8,128)S(1)}, u32[]{:S(2)}, u32[]{:S(2)}) collective-permute-start(f32[8,64,128]{2,1,0:T(8,128)S(1)} %fusion.11), channel_id=1, source_target_pairs={{16,0},{24,8},{17,1},{25,9},{18,2},{26,10},{19,3},{27,11},{20,4},{... | collective-permute-start | bytes 786440 | tf_op jit(solution)/shard_map/ppermute | solution.py:571
  103.8 5.4 %copy-start.1 = (f32[8,2,32,128]{3,2,1,0:T(8,128)}, f32[8,2,32,128]{3,2,1,0:T(8,128)S(1)}, u32[]{:S(2)}) copy-start(f32[8,2,32,128]{3,2,1,0:T(8,128)S(1)} %all-to-all-done.3) | copy-start | bytes 786436
  106.8 1.6 %collective-permute-start.6 = (f32[8,64,128]{2,1,0:T(8,128)S(1)}, f32[8,64,128]{2,1,0:T(8,128)S(1)}, u32[]{:S(2)}, u32[]{:S(2)}) collective-permute-start(f32[8,64,128]{2,1,0:T(8,128)S(1)} %get-tuple-element.87), channel_id=1, source_target_pairs={{0,8},{8,0},{16,24},{24,16},{1,9},{9,1},{17,25},{25,17},{2,10},{10... | collective-permute-start | bytes 786440 | tf_op jit(solution)/shard_map/ppermute | solution.py:543
  135.4 1.2 collective-permute-start.7
  136.6 3.7 %collective-permute-start.8 = (f32[16,128]{1,0:T(8,128)S(1)}, f32[16,128]{1,0:T(8,128)S(1)}, u32[]{:S(2)}, u32[]{:S(2)}) collective-permute-start(f32[16,128]{1,0:T(8,128)S(1)} %add.55), channel_id=1, source_target_pairs={{0,16},{8,24},{16,0},{24,8},{1,17},{9,25},{17,1},{25,9},{2,18},{10... | collective-permute-start | bytes 24584 | tf_op jit(solution)/shard_map/ppermute | solution.py:617
  140.2 3.7 %collective-permute-start.9 = (f32[16,128]{1,0:T(8,128)S(1)}, f32[16,128]{1,0:T(8,128)S(1)}, u32[]{:S(2)}, u32[]{:S(2)}) collective-permute-start(f32[16,128]{1,0:T(8,128)S(1)} %add.56), channel_id=1, source_target_pairs={{0,1},{1,0},{2,3},{3,2},{4,5},{5,4},{6,7},{7,6},{8,9},{9,8},{10,11... | collective-permute-start | bytes 24584 | tf_op jit(solution)/shard_map/ppermute | solution.py:617
  143.9 3.7 %collective-permute-start.10 = (f32[16,128]{1,0:T(8,128)S(1)}, f32[16,128]{1,0:T(8,128)S(1)}, u32[]{:S(2)}, u32[]{:S(2)}) collective-permute-start(f32[16,128]{1,0:T(8,128)S(1)} %add.57), channel_id=1, source_target_pairs={{0,2},{1,3},{2,0},{3,1},{4,6},{5,7},{6,4},{7,5},{8,10},{9,11},{10,... | collective-permute-start | bytes 24584 | tf_op jit(solution)/shard_map/ppermute | solution.py:617
  147.5 7.9 %collective-permute-start.11 = (f32[16,128]{1,0:T(8,128)S(1)}, f32[16,128]{1,0:T(8,128)S(1)}, u32[]{:S(2)}, u32[]{:S(2)}) collective-permute-start(f32[16,128]{1,0:T(8,128)S(1)} %add.58), channel_id=1, source_target_pairs={{0,4},{1,5},{2,6},{3,7},{4,0},{5,1},{6,2},{7,3},{8,12},{9,13},{10,... | collective-permute-start | bytes 24584 | tf_op jit(solution)/shard_map/ppermute | solution.py:617

commit v3 on v0

v3 whole, which is shorter than its diff:
```python
import functools

import jax
import jax.numpy as jnp
import numpy as np
from jax import lax
from jax.experimental import pallas as pl
from jax.experimental.pallas import tpu as pltpu
from jax.sharding import PartitionSpec as P

HS, WS, BI, BJ = 8, 16, 4, 4
POS = BI * BJ
LANES = 128
D = 128
STEPS = 4
BLOCK = D // STEPS
F32 = jnp.float32
BF16 = jnp.bfloat16
LOG2E = 1.4426950408889634
LN2 = 0.6931471805599453


@functools.cache
def lane_orders():
    lane = np.arange(LANES)
    hs, ws = lane // WS, lane % WS
    same_w = ws[:, None] == ws[None]
    same_h = hs[:, None] == hs[None]
    out = {
        "above": same_w & (hs[:, None] < hs[None]), "below": same_w & (hs[:, None] > hs[None]),
        "left": same_h & (ws[:, None] < ws[None]), "right": same_h & (ws[:, None] > ws[None]),
    }
    return {k: np.concatenate([v, v], 0).astype(np.float32) for k, v in out.items()}


def lane_places(rows, out):
    at = lax.broadcasted_iota(jnp.int32, (2 * LANES, LANES), 0) % LANES
    lane = lax.broadcasted_iota(jnp.int32, (2 * LANES, LANES), 1)
    segment, edge = (at, lane) if out else (lane, at)
    return edge - (segment % WS if rows else segment // WS)


def edge_start(b, k, rows):
    return (b // 2) * 64 + k * WS if rows else b * 32 + k * HS


def placed(places, start):
    return jnp.where(places == start, 1.0, 0.0).astype(BF16)


def halves(x):
    high = x.astype(BF16)
    low = (x - high.astype(F32)).astype(BF16)
    return high, low


def lane_dot(matrix, *parts):
    parts = [h for x in parts for h in halves(x)]
    return jnp.dot(jnp.concatenate(parts, 1), matrix, preferred_element_type=F32)


def lane_dot_exact(x, matrix):
    high, low = halves(x)
    rest = (x - high.astype(F32) - low.astype(F32)).astype(BF16)
    return jnp.dot(
        jnp.concatenate([high, low], 1), matrix, preferred_element_type=F32
    ) + jnp.dot(rest, matrix[:LANES], preferred_element_type=F32)


def row_of(ref, p, n):
    return jnp.broadcast_to(ref[p, pl.ds(n, 1), :], (8, LANES))


def block_of(b):
    return pl.ds(pl.multiple_of(b * BLOCK, BLOCK), BLOCK)


def half_of(b):
    return pl.ds(pl.multiple_of((b % 2) * BLOCK, BLOCK), BLOCK)


def each_group(b, states, size, body):
    groups = states // size

    def one(at, carry):
        d = pl.ds(pl.multiple_of(b * BLOCK + (at // groups) * 8, 8), 8)
        body([(at % groups) * size + k for k in range(size)], d)
        return carry

    lax.fori_loop(0, (BLOCK // 8) * groups, one, 0)


def send(b, seg, order, leaving, rows):
    states = seg.shape[0]
    at = block_of(b)
    total = None
    places = lane_places(rows, True)
    for k in range(4):
        matrix = jnp.concatenate([placed(places, edge_start(b, k, rows)), order[...]], 1)
        both = lane_dot(matrix, seg[:, k, at].reshape(states * BLOCK, LANES))
        seg[:, k, at] = both[:, LANES:].reshape(states, BLOCK, LANES)
        total = both[:, :LANES] if total is None else total + both[:, :LANES]
    total = total.reshape(states, BLOCK, LANES)
    if rows:
        leaving[:, half_of(b)] += total
    else:
        leaving[...] += total


def take(b, seg, entering, out, rows):
    states = seg.shape[0]
    entering = entering[:, half_of(b)] if rows else entering[...]
    places = lane_places(rows, False)
    matrix = jnp.concatenate([placed(places, edge_start(b, k, rows)) for k in range(4)], 1)
    first = lane_dot(matrix, entering.reshape(states * BLOCK, LANES))
    at = block_of(b)
    for k in range(4):
        out[:, k, at] = seg[:, k, at] + first[:, k * LANES : (k + 1) * LANES].reshape(
            states, BLOCK, LANES
        )


def part_by_core(core, whole, keep, give):
    count = whole.shape[0] // 2
    for n in range(count):
        low, high = whole[n], whole[count + n]
        keep[n] = jnp.where(core[0] == 0, low, high)
        give[n] = jnp.where(core[0] == 0, high, low)


def join_by_core(core, keep, got, whole):
    count = whole.shape[0] // 2
    for n in range(count):
        whole[n] = jnp.where(core[0] == 0, keep[n], got[n])
        whole[count + n] = jnp.where(core[0] == 0, got[n], keep[n])


def gather_plane(ref, i, j):
    return jnp.concatenate([ref[hs, i, pl.ds(j, WS, stride=BJ), :] for hs in range(HS)], 0).T


def gather_states(ref, i, turned, out):
    for hs in range(HS):
        turned[hs] = ref[hs, i].T
    for j in range(BJ):
        out[i * BJ + j] = jnp.concatenate(
            [turned[hs, pl.ds(j, WS, stride=BJ), :] for hs in range(HS)], 0
        ).T


def pack_rates(i, decay_log, rates, rates_v, rates_s):
    lane = lax.broadcasted_iota(jnp.int32, (BLOCK, LANES), 1)
    lane_v = lax.broadcasted_iota(jnp.int32, (2 * BLOCK, LANES), 1)
    rate = (-LOG2E * jnp.exp(decay_log[i])).T
    count = rates.shape[0] // BI
    for k in range(count):
        n = i * count + k
        r = jnp.broadcast_to(rate[:, k : k + 1], (D, LANES))
        rates[n] = r
        part = [r[q * BLOCK : (q + 1) * BLOCK] for q in range(4)]
        rates_v[n] = jnp.where(lane_v < 64, r[: 2 * BLOCK], r[2 * BLOCK :])
        rates_s[n] = jnp.where(
            lane < 64, jnp.where(lane < 32, part[0], part[1]),
            jnp.where(lane < 96, part[2], part[3]),
        )


class AdjointCols:
    def first(self, step, grad, read, decay_log, place, left, right,
              step_p, grad_p, rates, seg, read_p, rates_v, rates_s, own_rates, before_cols,
              sum_cols, sum_rows, sent, turned, leaving):
        sum_cols[...] = jnp.zeros_like(sum_cols)
        leaving[...] = jnp.zeros_like(leaving)

    def lead(self, i, step, grad, read, decay_log, place, left, right,
             step_p, grad_p, rates, seg, read_p, rates_v, rates_s, own_rates, before_cols,
             sum_cols, sum_rows, sent, turned, leaving):
        row_total = None
        for j in range(BJ):
            s = gather_plane(step, i, j)
            step_p[i * BJ + j] = s
            grad_p[i * BJ + j] = gather_plane(grad, i, j)
            row_total = s if row_total is None else row_total + s
        gather_states(read, i, turned, read_p)
        pack_rates(i, decay_log, rates, rates_v, rates_s)
        before_cols[i] = lane_dot_exact(row_total, left[...])
        places = lane_places(False, True)
        for q in range(STEPS):
            sum_cols[...] += lane_dot_exact(
                row_total[q * BLOCK : (q + 1) * BLOCK], placed(places, edge_start(q, i, False))
            )

    def main(self, b, step, grad, read, decay_log, place, left, right,
             step_p, grad_p, rates, seg, read_p, rates_v, rates_s, own_rates, before_cols,
             sum_cols, sum_rows, sent, turned, leaving):
        states = seg.shape[0]

        def group(ns, d):
            r = [rates[n, d] for n in ns]
            for i in range(BI):
                acc = [None] * len(ns)
                c = before_cols[i, d]
                for j in range(BJ):
                    p = i * BJ + j
                    c = c + step_p[p, d]
                    g = grad_p[p, d]
                    for k, n in enumerate(ns):
                        term = jnp.exp2(c * r[k]) * g * row_of(read_p, p, n)
                        acc[k] = term if acc[k] is None else acc[k] + term
                for k, n in enumerate(ns):
                    seg[n, i, d] = acc[k]

        each_group(b, states, 16, group)
        send(b, seg, right, leaving, False)

    def last(self, step, grad, read, decay_log, place, left, right,
             step_p, grad_p, rates, seg, read_p, rates_v, rates_s, own_rates, before_cols,
             sum_cols, sum_rows, sent, turned, leaving):
        share = own_rates.shape[0]
        for k in range(sent.shape[0]):
            sent[k, 0:share] = leaving[k * share : (k + 1) * share]
            sent[k, share] = sum_cols[...]
        for k in range(share):
            own_rates[k] = rates_s[place[0] * share + k]
        places = lane_places(True, True)
        for r in range(2):
            total = None
            for q in (r, r + 2):
                for j in range(BJ):
                    run = None
                    for i in range(BI):
                        s = step_p[i * BJ + j, q * BLOCK : (q + 1) * BLOCK]
                        run = s if run is None else run + s
                    one = lane_dot_exact(run, placed(places, edge_start(q, j, True)))
                    total = one if total is None else total + one
            sum_rows[r * BLOCK : (r + 1) * BLOCK] = total


class ForwardRows:
    def first(self, feat, step_p, rates, write, rates_v, sum_rows, core, above,
              source_p, seg, write_p, before_rows, keep, give, turned, leaving):
        leaving[...] = jnp.zeros_like(leaving)

    def lead(self, i, feat, step_p, rates, write, rates_v, sum_rows, core, above,
             source_p, seg, write_p, before_rows, keep, give, turned, leaving):
        for j in range(BJ):
            source_p[i * BJ + j] = step_p[i * BJ + j] * gather_plane(feat, i, j)
        gather_states(write, i, turned, write_p)

        @pl.when(i == BI - 1)
        def _():
            for j in range(BJ):
                run = step_p[j]
                for k in range(1, BI):
                    run = run + step_p[k * BJ + j]
                before_rows[j] = lane_dot_exact(run, above[...])

    def main(self, b, feat, step_p, rates, write, rates_v, sum_rows, core, above,
             source_p, seg, write_p, before_rows, keep, give, turned, leaving):
        states = seg.shape[0]

        def group(ns, d):
            r = [-rates[n, d] for n in ns]
            for j in range(BJ):
                acc = [None] * len(ns)
                c = before_rows[j, d]
                for i in range(BI):
                    p = i * BJ + j
                    c = c + step_p[p, d]
                    s = source_p[p, d]
                    for k, n in enumerate(ns):
                        term = jnp.exp2(c * r[k]) * s * row_of(write_p, p, n)
                        acc[k] = term if acc[k] is None else acc[k] + term
                for k, n in enumerate(ns):
                    seg[n, j, d] = acc[k]

        each_group(b, states, 16, group)
        send(b, seg, above, leaving, True)

    def last(self, feat, step_p, rates, write, rates_v, sum_rows, core, above,
             source_p, seg, write_p, before_rows, keep, give, turned, leaving):
        for n in range(leaving.shape[0]):
            leaving[n] = leaving[n] * jnp.exp2(rates_v[n] * sum_rows[...])
        part_by_core(core, leaving, keep, give)


class ForwardCols:
    def first(self, step_p, source_p, rates, seg_rows, keep, got, write_p, rates_s, before_rows,
              before_cols, sum_cols, core, left, start_rows, seg, leaving, entering):
        leaving[...] = jnp.zeros_like(leaving)
        join_by_core(core, keep, got, entering)

    def main(self, b, step_p, source_p, rates, seg_rows, keep, got, write_p, rates_s, before_rows,
             before_cols, sum_cols, core, left, start_rows, seg, leaving, entering):
        states = seg.shape[0]
        take(b, seg_rows, entering, start_rows, True)

        def group(ns, d):
            r = [rates[n, d] for n in ns]
            vert = [[None] * BJ for _ in ns]
            for j in range(BJ):
                before = before_rows[j, d]
                for k, n in enumerate(ns):
                    vert[k][j] = start_rows[n, j, d] * jnp.exp2(r[k] * before)
                    start_rows[n, j, d] = vert[k][j]
            for i in range(BI):
                state = [None] * len(ns)
                after = before_cols[i, d]
                for j in range(BJ):
                    p = i * BJ + j
                    c, s = step_p[p, d], source_p[p, d]
                    after = after + c
                    for k, n in enumerate(ns):
                        decay = jnp.exp2(c * r[k])
                        vert[k][j] = decay * vert[k][j] + s * row_of(write_p, p, n)
                        state[k] = vert[k][j] if j == 0 else decay * state[k] + vert[k][j]
                for k, n in enumerate(ns):
                    seg[n, i, d] = state[k] * jnp.exp2(-r[k] * after)

        each_group(b, states, 8, group)
        send(b, seg, left, leaving, False)

    def last(self, step_p, source_p, rates, seg_rows, keep, got, write_p, rates_s, before_rows,
             before_cols, sum_cols, core, left, start_rows, seg, leaving, entering):
        for n in range(leaving.shape[0]):
            leaving[n] = leaving[n] * jnp.exp2(rates_s[n] * sum_cols[...])


class AdjointRows:
    def first(self, step_p, grad_p, rates, seg_cols, entering, read_p, rates_s, before_rows,
              before_cols, sum_cols, core, below, start_cols, seg, keep, give,
              scaled, leaving):
        leaving[...] = jnp.zeros_like(leaving)
        for n in range(scaled.shape[0]):
            scaled[n] = entering[n] * jnp.exp2(rates_s[n] * sum_cols[...])

    def main(self, b, step_p, grad_p, rates, seg_cols, entering, read_p, rates_s, before_rows,
             before_cols, sum_cols, core, below, start_cols, seg, keep, give,
             scaled, leaving):
        states = seg.shape[0]
        take(b, seg_cols, scaled, start_cols, False)

        def group(ns, d):
            r = [rates[n, d] for n in ns]
            passed_v = [[None] * BJ for _ in ns]
            for i in reversed(range(BI)):
                after = before_cols[i, d]
                for j in range(BJ):
                    after = after + step_p[i * BJ + j, d]
                passed = []
                for k, n in enumerate(ns):
                    passed.append(start_cols[n, i, d] * jnp.exp2(-r[k] * after))
                    start_cols[n, i, d] = passed[k]
                for j in reversed(range(BJ)):
                    p = i * BJ + j
                    c, g = step_p[p, d], grad_p[p, d]
                    for k, n in enumerate(ns):
                        decay = jnp.exp2(c * r[k])
                        adjoint = g * row_of(read_p, p, n) + passed[k]
                        passed[k] = decay * adjoint
                        if i == BI - 1:
                            passed_v[k][j] = passed[k]
                        else:
                            passed_v[k][j] = decay * (adjoint + passed_v[k][j])
            for j in range(BJ):
                before = before_rows[j, d]
                for k, n in enumerate(ns):
                    seg[n, j, d] = passed_v[k][j] * jnp.exp2(r[k] * before)

        each_group(b, states, 8, group)
        send(b, seg, below, leaving, True)

    def last(self, step_p, grad_p, rates, seg_cols, entering, read_p, rates_s, before_rows,
             before_cols, sum_cols, core, below, start_cols, seg, keep, give,
             scaled, leaving):
        part_by_core(core, leaving, keep, give)


class Final:
    def first(self, step_p, source_p, grad_p, rates, start_rows, start_cols, seg_s, seg_v,
              enter_s, keep, got, write_p, read_p, rates_v, before_rows, before_cols, sum_rows,
              core, features_p, steps_p, sum_w, sum_r, grad_decay,
              entering, decay_term):
        join_by_core(core, keep, got, entering)
        for n in range(entering.shape[0]):
            entering[n] = entering[n] * jnp.exp2(rates_v[n] * sum_rows[...])
        sum_w[...] = jnp.zeros_like(sum_w)
        sum_r[...] = jnp.zeros_like(sum_r)

    def main(self, b, step_p, source_p, grad_p, rates, start_rows, start_cols, seg_s, seg_v,
             enter_s, keep, got, write_p, read_p, rates_v, before_rows, before_cols, sum_rows,
             core, features_p, steps_p, sum_w, sum_r, grad_decay,
             entering, decay_term):
        states = rates.shape[0]
        take(b, seg_s, enter_s, seg_s, False)
        take(b, seg_v, entering, seg_v, True)
        at = block_of(b)
        features_p[:, at] = jnp.zeros((POS, BLOCK, LANES), F32)
        steps_p[:, at] = jnp.zeros((POS, BLOCK, LANES), F32)

        def group(ns, d):
            r = [rates[n, d] for n in ns]
            vert = [[start_rows[n, j, d] for j in range(BJ)] for n in ns]
            from_v, from_s = [{} for _ in ns], [{} for _ in ns]
            for i in range(BI):
                before = before_cols[i, d]
                state = [seg_s[n, i, d] * jnp.exp2(r[k] * before) for k, n in enumerate(ns)]
                for j in range(BJ):
                    p = i * BJ + j
                    c, s, g = step_p[p, d], source_p[p, d], grad_p[p, d]
                    for k, n in enumerate(ns):
                        decay = jnp.exp2(c * r[k])
                        dv = decay * vert[k][j]
                        vert[k][j] = dv + s * row_of(write_p, p, n)
                        ds = decay * state[k]
                        state[k] = ds + vert[k][j]
                        sum_r[p, pl.ds(n * 8, 8)] += state[k] * g
                        from_v[k][p] = dv
                        from_s[k][p] = ds
            passed_v = [[None] * BJ for _ in ns]
            for j in range(BJ):
                after = before_rows[j, d]
                for i in range(BI):
                    after = after + step_p[i * BJ + j, d]
                for k, n in enumerate(ns):
                    passed_v[k][j] = seg_v[n, j, d] * jnp.exp2(-r[k] * after)
            total = [None for _ in ns]
            for i in reversed(range(BI)):
                passed = [start_cols[n, i, d] for n in ns]
                for j in reversed(range(BJ)):
                    p = i * BJ + j
                    c, s, g = step_p[p, d], source_p[p, d], grad_p[p, d]
                    sum_q, sum_t = None, None
                    for k, n in enumerate(ns):
                        adjoint = g * row_of(read_p, p, n) + passed[k]
                        m = c * r[k]
                        decay = jnp.exp2(m)
                        passed[k] = decay * adjoint
                        adjoint_v = adjoint + passed_v[k][j]
                        passed_v[k][j] = decay * adjoint_v
                        q = (adjoint * from_s[k][p] + adjoint_v * from_v[k][p]) * m
                        total[k] = q if total[k] is None else total[k] + q
                        t = adjoint_v * row_of(write_p, p, n)
                        sum_q = q if sum_q is None else sum_q + q
                        sum_t = t if sum_t is None else sum_t + t
                        sum_w[p, pl.ds(n * 8, 8)] += adjoint_v * s
                    steps_p[p, d] += sum_q
                    features_p[p, d] += sum_t
            for k, n in enumerate(ns):
                decay_term[n, d] = total[k]

        each_group(b, states, 8, group)
        for p in range(POS):
            t, s = features_p[p, at], step_p[p, at]
            features_p[p, at] = s * t
            steps_p[p, at] = (source_p[p, at] * t + steps_p[p, at] * LN2) / s

    def last(self, step_p, source_p, grad_p, rates, start_rows, start_cols, seg_s, seg_v,
             enter_s, keep, got, write_p, read_p, rates_v, before_rows, before_cols, sum_rows,
             core, features_p, steps_p, sum_w, sum_r, grad_decay,
             entering, decay_term):
        for n in range(rates.shape[0]):
            out = lax.dot_general(
                jnp.ones((8, 2 * LANES), BF16), jnp.concatenate(halves(decay_term[n]), 1),
                (((1,), (1,)), ((), ())), preferred_element_type=F32,
            )
            grad_decay[pl.ds(n, 1)] = out[0:1] * LN2


class Unpack:
    def lead(self, i, features_p, steps_p, sum_w, sum_r, features, steps, writes, reads, turned):
        for j in range(BJ):
            for values, out in ((features_p, features), (steps_p, steps)):
                back = values[i * BJ + j].T
                for hs in range(HS):
                    out[hs, i, pl.ds(j, WS, stride=BJ), :] = back[hs * WS : hs * WS + WS]
        states = writes.shape[2]
        for values, out in ((sum_w, writes), (sum_r, reads)):
            for j in range(BJ):
                back = sum(values[i * BJ + j, pl.ds(k, states, stride=8), :] for k in range(8)).T
                for hs in range(HS):
                    turned[hs, pl.ds(j, WS, stride=BJ), :] = back[hs * WS : hs * WS + WS]
            for hs in range(HS):
                out[hs, i] = turned[hs].T


def prefix_kernel(held, sums, rates, out, *, reverse):
    size, share = out.shape[:2]
    at = sums.shape[1] - 1
    order = list(reversed(range(size))) if reverse else list(range(size))
    for n in range(share):
        before = jnp.zeros(out.shape[2:], F32)
        for k in order:
            out[k, n] = before
            before = jnp.exp2(rates[n] * sums[k, at]) * before + held[k, n]


def cut(ref, kind, k):
    if kind == "channels":
        index = (slice(None),) * (len(ref.shape) - 2) + (block_of(k),)
        return ref.at[index]
    if kind == "second":
        return ref.at[:, k]
    size = ref.shape[0] // BI
    return ref.at[pl.ds(k * size, size)]


def run(stage, ins, outs, scratch=(), micros=5):
    in_kinds, out_kinds = [k for _, k in ins], [k for _, k in outs]
    shapes = [a.shape for a, _ in ins] + [s for s, _ in outs]
    kinds = in_kinds + out_kinds
    streamed = [at for at, k in enumerate(kinds) if k not in ("whole", "scalar")]
    count = len(ins)

    def kernel(*refs):
        given = list(refs[: len(kinds)])
        rest = refs[len(kinds) :]
        buffers, sems = rest[: len(streamed)], rest[len(streamed)]
        extra = rest[len(streamed) + 1 :]
        views = list(given)
        copies = {}
        for slot, at in enumerate(streamed):
            views[at] = buffers[slot]

            def copy(k, slot=slot, at=at):
                far, near = cut(given[at], kinds[at], k), cut(buffers[slot], kinds[at], k)
                pair = (far, near) if at < count else (near, far)
                return pltpu.make_async_copy(*pair, sems.at[slot, k])

            copies[at] = copy

        def chosen(inputs, channels):
            return [
                copies[at] for at in streamed
                if (at < count) == inputs and (kinds[at] == "channels") == channels
            ]

        for channels in (False, True):
            for k in range(STEPS):
                for copy in chosen(True, channels):
                    copy(k).start()
        if hasattr(stage, "first"):
            stage.first(*views, *extra)
        for channels, part in ((False, "lead"), (True, "main")):
            def one(k, carry):
                for copy in chosen(True, channels):
                    copy(k).wait()
                if hasattr(stage, part):
                    getattr(stage, part)(k, *views, *extra)
                for copy in chosen(False, channels):
                    copy(k).start()
                return carry

            if hasattr(stage, part) or chosen(True, channels):
                lax.fori_loop(0, STEPS, one, 0)
        if hasattr(stage, "last"):
            stage.last(*views, *extra)
        for channels in (False, True):
            for k in range(STEPS):
                for copy in chosen(False, channels):
                    copy(k).wait()

    def spec(kind):
        if kind == "whole":
            return pl.BlockSpec(memory_space=pltpu.VMEM)
        if kind == "scalar":
            return pl.BlockSpec(memory_space=pltpu.SMEM)
        return pl.BlockSpec(memory_space=pl.ANY)

    return pl.pallas_call(
        kernel,
        out_shape=[jax.ShapeDtypeStruct(s, F32) for s, _ in outs],
        in_specs=[spec(k) for k in in_kinds],
        out_specs=[spec(k) for k in out_kinds],
        scratch_shapes=[pltpu.VMEM(shapes[at], F32) for at in streamed]
        + [pltpu.SemaphoreType.DMA((len(streamed), STEPS))]
        + [pltpu.VMEM(s, F32) for s in scratch],
        compiler_params=pltpu.CompilerParams(vmem_limit_bytes=60 << 20),
        cost_estimate=pl.CostEstimate(
            flops=0, bytes_accessed=int(micros * 3.3e6), transcendentals=0
        ),
    )(*[a for a, _ in ins])


def swap_cores(x, size):
    return lax.ppermute(x, "row", [(k, k ^ 1) for k in range(size)])


def tied(*arrays):
    return lax.optimization_barrier(arrays)


def row_total(keep, give, sums, other_sums, rates, size, reverse):
    count = keep.shape[0]
    core = lax.axis_index("row") % 2
    theirs = swap_cores(give, size)
    rate = lax.dynamic_slice_in_dim(rates, core * count, count, 0)
    first = core == (1 if reverse else 0)
    near = jnp.where(first, keep, theirs)
    far = jnp.where(first, theirs, keep)
    near_sum = jnp.where(first, sums, other_sums)
    far_sum = jnp.where(first, other_sums, sums)
    total = far + jnp.exp2(rate * far_sum) * near
    return total, near, near_sum, far_sum, rate


def row_carry(total, near, near_sum, far_sum, rate, beside, size, reverse):
    core = lax.axis_index("row") % 2
    first = core == (1 if reverse else 0)
    sign = -2 if reverse else 2

    def shift(x, by):
        return lax.ppermute(
            x, "row", [(k, k + by) for k in range(size) if 0 <= k + by < size]
        )

    entering = shift(total, sign)
    if size > 4:
        span = shift(near_sum + far_sum, sign)
        by = sign
        while abs(by) < size - 2:
            entering = entering + jnp.exp2(rate * span) * shift(entering, by)
            span = span + shift(span, by)
            by *= 2
    entering, _ = tied(entering, beside)
    to_far = near + jnp.exp2(rate * near_sum) * entering
    keep = jnp.where(first, entering, to_far)
    give = jnp.where(first, to_far, entering)
    return keep, swap_cores(give, size)


def col_gather(sent):
    return lax.all_to_all(sent, "col", 0, 0)


def col_carry(held, sums, rates, reverse):
    size, share = held.shape[0], rates.shape[0]
    vmem = pl.BlockSpec(memory_space=pltpu.VMEM)
    return pl.pallas_call(
        functools.partial(prefix_kernel, reverse=reverse),
        out_shape=jax.ShapeDtypeStruct((size, share) + held.shape[2:], F32),
        in_specs=[vmem] * 3,
        out_specs=vmem,
        compiler_params=pltpu.CompilerParams(vmem_limit_bytes=4 << 20),
    )(held, sums, rates)


def col_return(carries):
    back = lax.all_to_all(carries, "col", 0, 0)
    return back.reshape((-1,) + carries.shape[2:])


def total_of(x, rows, cols):
    by = 1
    while by < rows:
        x = x + lax.ppermute(x, "row", [(k, k ^ by) for k in range(rows)])
        by *= 2
    parts = lax.all_to_all(jnp.broadcast_to(x[None], (cols,) + x.shape), "col", 0, 0)
    return jnp.sum(parts, 0)


def shards(features, step_size, write_weights, read_weights, decay_log, out_grad, sizes):
    rows, cols = sizes
    states = decay_log.shape[0]
    share = states // cols
    tile_h, tile_w = features.shape[:2]
    orders = {k: jnp.asarray(v, BF16) for k, v in lane_orders().items()}
    plane, quad = (POS, D, LANES), (4, D, LANES)
    seg = (states, 4, D, LANES)
    all_rates = (states, D, LANES)
    small = (POS, states, LANES)
    packed = (HS, BI, tile_w, D)
    weights = (HS, BI, states, tile_w)
    turned = (HS, tile_w, states)
    size_v, size_s = (states, D // 2, LANES), (states, D // 4, LANES)
    half_v = (states // 2,) + size_v[1:]
    core = (lax.axis_index("row") % 2).astype(jnp.int32).reshape(1)
    place = lax.axis_index("col").astype(jnp.int32).reshape(1)

    (step_p, grad_p, rates, seg_cols, read_p, rates_v, rates_s, own_rates, before_cols, sum_cols,
     sum_rows, sent) = run(
        AdjointCols(),
        [(step_size.reshape(packed), "second"), (out_grad.reshape(packed), "second"),
         (read_weights.swapaxes(1, 2).reshape(weights), "second"),
         (decay_log.reshape(BI, states // BI, D), "whole"), (place, "scalar"),
         (orders["left"], "whole"), (orders["right"], "whole")],
        [(plane, "first"), (plane, "first"), (all_rates, "first"), (seg, "channels"),
         (small, "whole"), (size_v, "whole"), (size_s, "whole"), ((share,) + size_s[1:], "whole"),
         (quad, "whole"), (size_s[1:], "whole"), (size_v[1:], "whole"),
         ((cols, share + 1) + size_s[1:], "whole")],
        [turned, size_s],
    )
    held = col_gather(sent)
    other_rows = swap_cores(sum_rows, rows)
    step_p, _ = tied(step_p, sent)
    source_p, seg_rows, write_p, before_rows, keep, give = run(
        ForwardRows(),
        [(features.reshape(packed), "second"), (step_p, "first"), (rates, "channels"),
         (write_weights.swapaxes(1, 2).reshape(weights), "second"), (rates_v, "whole"),
         (sum_rows, "whole"), (core, "scalar"), (orders["above"], "whole")],
        [(plane, "first"), (seg, "channels"), (small, "whole"), (quad, "whole"),
         (half_v, "whole"), (half_v, "whole")],
        [turned, size_v],
    )
    total = row_total(keep, give, sum_rows, other_rows, rates_v, rows, False)
    held, first = tied(held, total[0])
    col_sums = held
    carries = col_carry(held, held, own_rates, True)
    enter_cols = col_return(carries)
    keep, got = row_carry(first, *total[1:], carries, rows, False)
    start_rows, seg_s, leave_s = run(
        ForwardCols(),
        [(step_p, "channels"), (source_p, "channels"), (rates, "channels"),
         (seg_rows, "channels"), (keep, "whole"), (got, "whole"), (write_p, "whole"),
         (rates_s, "whole"), (before_rows, "whole"), (before_cols, "whole"),
         (sum_cols, "whole"), (core, "scalar"), (orders["left"], "whole")],
        [(seg, "channels"), (seg, "channels"), (size_s, "whole")], [size_v], 10,
    )
    held = col_gather(leave_s.reshape((cols, share) + size_s[1:]))
    enter_cols, _ = tied(enter_cols, leave_s)
    start_cols, seg_v, keep, give = run(
        AdjointRows(),
        [(step_p, "channels"), (grad_p, "channels"), (rates, "channels"),
         (seg_cols, "channels"), (enter_cols, "whole"), (read_p, "whole"), (rates_s, "whole"),
         (before_rows, "whole"), (before_cols, "whole"), (sum_cols, "whole"), (core, "scalar"),
         (orders["below"], "whole")],
        [(seg, "channels"), (seg, "channels"), (half_v, "whole"), (half_v, "whole")],
        [size_s, size_v], 10,
    )
    held, give = tied(held, give)
    carries = col_carry(held, col_sums, own_rates, False)
    enter_s = col_return(carries)
    total = row_total(keep, give, sum_rows, other_rows, rates_v, rows, True)
    keep, got = row_carry(*total, enter_s, rows, True)
    features_p, steps_p, sum_w, sum_r, grad_decay = run(
        Final(),
        [(step_p, "channels"), (source_p, "channels"), (grad_p, "channels"),
         (rates, "channels"), (start_rows, "channels"), (start_cols, "channels"),
         (seg_s, "channels"), (seg_v, "channels"), (enter_s, "whole"), (keep, "whole"),
         (got, "whole"), (write_p, "whole"), (read_p, "whole"), (rates_v, "whole"),
         (before_rows, "whole"), (before_cols, "whole"), (sum_rows, "whole"), (core, "scalar")],
        [(plane, "channels"), (plane, "channels"), ((POS, states * 8, LANES), "whole"),
         ((POS, states * 8, LANES), "whole"), ((states, D), "whole")],
        [size_v, all_rates], 25,
    )
    grad_decay = total_of(grad_decay, rows, cols)
    grad_features, grad_step, grad_write, grad_read = run(
        Unpack(),
        [(features_p, "first"), (steps_p, "first"), (sum_w, "first"), (sum_r, "first")],
        [(packed, "second"), (packed, "second"), (weights, "second"), (weights, "second")],
        [turned],
    )
    weights = (tile_h, states, tile_w)
    return (
        grad_features.reshape(features.shape),
        grad_step.reshape(features.shape),
        grad_write.reshape(weights).swapaxes(1, 2),
        grad_read.reshape(weights).swapaxes(1, 2),
        grad_decay,
    )


def solution(mesh):
    spec = P("row", "col", None)
    sizes = (mesh.shape["row"], mesh.shape["col"])
    return jax.shard_map(
        functools.partial(shards, sizes=sizes),
        mesh=mesh,
        in_specs=(spec, spec, spec, spec, P(), spec),
        out_specs=(spec, spec, spec, spec, P()),
        check_vma=False,
    )
```

time: 931 us -> 147 us (0.16); the launches traced: 915 us -> 146 us
  other arithmetic: 651 us -> 5.93 us
  local copies, waits for them, and re-layouts: 97.6 us -> 2.07 us
  Pallas kernels: 0 us -> 79.8 us
  matrix products: 74.5 us -> 0 us
  blocking collectives: 39.6 us -> 0 us
  starting transfers between devices: 0.71 us -> 37.2 us
  waiting for transfers between devices: 34.9 us -> 20.2 us
  between operations: 14.8 us -> 0.82 us
    dynamic_update_slice x192 -> x0, other arithmetic: 376 us -> none  [the longest x64 142 us: sweep_rows(): closing, values = lax.scan(advance, initial, (decays, driving))]
    mul x100 -> x0, other arithmetic: 147 us -> none  [the longest x64 76.2 us: advance(): current = factor * value]
    pallas_call x0 -> x8, Pallas kernels: none -> 79.8 us  [the longest x6 78.3 us: run(): pl.pallas_call(kernel, out_shape=[jax.ShapeDtypeStruct(s, F32) for s, _ i...]
    dot_general x3 -> x0, matrix products: 74.5 us -> none  [the longest x1 28.9 us: shards(): jnp.einsum('hwnd,hwd->hwn', adjoint_v, step_size * features, precision=hi...]
    psum x1 -> x0, blocking collectives: 39.6 us -> none  [shards(): grad_decay = lax.psum(partial_sum, ('row', 'col')) * decay_rate]
    select_n x24 -> x3, other arithmetic: 38.1 us -> 2.56 us  [the longest x2 2.55 us: row_carry(): give = jnp.where(first, to_far, entering)]
    all_gather x6 -> x0, waiting for transfers between devices: 34.8 us -> none  [carried_in(): everything = jax.tree.map(lambda part: lax.all_gather(part, axis), shard)]
    dot_general x1 -> x0, other arithmetic: 34.6 us -> none  [shards(): jnp.einsum('hwnd,hwd->nd', exponent_grad, step_size, precision=highest)]
  transfers between devices with their start and end apart: 6 -> 14, of which waited for: 1 -> 9; matrix products, arithmetic and copies ran while one was open for 48% -> 3% of each run, Pallas kernels for 0% -> 29%
where the time goes in v3:
time: 147 us; the launch traced here: 146 us
  Pallas kernels  79.8 us (54%)
  starting transfers between devices  37.2 us (25%)
  waiting for transfers between devices  20.2 us (14%)
  other arithmetic  5.93 us (4%)
  local copies, waits for them, and re-layouts  2.07 us (1%)
    pallas_call x6, Pallas kernels, run(): pl.pallas_call(kernel, out_shape=[jax.ShapeDtypeStruct(s, F32) for s, _ i...  78.3 us
    all_to_all x2, starting transfers between devices, col_gather(): return lax.all_to_all(sent, 'col', 0, 0)  13.4 us
    all_to_all x2, starting transfers between devices, col_return(): back = lax.all_to_all(carries, 'col', 0, 0)  12 us
    all_to_all x2, waiting for transfers between devices, col_return(): back = lax.all_to_all(carries, 'col', 0, 0)  7.24 us
    all_to_all x1, starting transfers between devices, total_of(): lax.all_to_all(jnp.broadcast_to(x[None], (cols,) + x.shape), 'col', 0, 0)  5.71 us
    ppermute x2, starting transfers between devices, shift(): lax.ppermute(x, 'row', [(k, k + by) for k in range(size) if 0 <= k + by <...  4.73 us
    ppermute x2, waiting for transfers between devices, total_of(): x = x + lax.ppermute(x, 'row', [(k, k ^ by) for k in range(rows)])  4.69 us
    ppermute x5, waiting for transfers between devices, swap_cores(): return lax.ppermute(x, 'row', [(k, k ^ 1) for k in range(size)])  3.94 us
  transfers between devices with their start and end apart: 14, of which 9 were waited for; matrix products, arithmetic and copies ran while one was open for 3% of the time, Pallas kernels for 29%

profile of v3, /device:TPU:0, one launch (start us, length us, event | category | flops | bytes accessed | tf_op | source)
XLA Modules:
  0.0 146.0 jit_solution(11910863535984079348)
XLA Ops:
  0.6 11.3 %shard_map.137 = (f32[16,128,128]{2,1,0:T(8,128)}, f32[16,128,128]{2,1,0:T(8,128)}, f32[16,128,128]{2,1,0:T(8,128)}, f32[16,4,128,128]{3,2,1,0:T(8,128)}, f32[16...) custom-call(f32[8,4,64,128]{3,2,1,0:T(8,128)} %bitcast.25, ...), custom_call_target="tpu_custom_call" | custom-call | bytes 16500000 | tf_op jit(solution)/shard_map/pallas_call | solution.py:570
  12.0 0.0 copy-start.4
  12.0 7.4 %all-to-all-start = ((f32[8,3,32,128]{3,2,1,0:T(8,128)}), f32[8,3,32,128]{3,2,1,0:T(8,128)S(1)}, u32[]{:S(2)}, u32[]{:S(2)}) async-start(f32[8,3,32,128]{3,2,1,0:T(8,128)} %get-tuple-element.48), calls=%async_computation | async-start | bytes 786432 | tf_op jit(solution)/shard_map/all_to_all | solution.py:633
  19.4 10.5 %shard_map.138 = (f32[16,128,128]{2,1,0:T(8,128)}, f32[16,4,128,128]{3,2,1,0:T(8,128)}, f32[16,16,128]{2,1,0:T(8,128)}, f32[4,128,128]{2,1,0:T(8,128)}, f32[8,64,128]{2,1,0:T(8,128)}, /*index=5*/f32[8,64,128]{2,1,0:T(8,128)}) custom-call(f32[8,4,64,128]{3,2,1,0:T(8,128)} %bitcast.27, f32[16,128,128]{2,1,0:T(8,128)} %get-tuple-element.49.refs_1_.refs_0_, ...), custom_call_target="tpu_custom_call" | custom-call | bytes 16500000 | tf_op jit(solution)/shard_map/pallas_call | solution.py:570
  29.9 0.1 collective-permute-start
  30.0 0.5 collective-permute-start.1
  30.5 1.1 collective-permute-done.1
  31.6 0.1 collective-permute-done
  31.7 1.0 multiply_add_fusion.3
  32.8 0.0 all-to-all-done.held.sums
  32.8 3.4 %collective-permute-start.2 = (f32[8,64,128]{2,1,0:T(8,128)S(1)}, f32[8,64,128]{2,1,0:T(8,128)S(1)}, u32[]{:S(2)}, u32[]{:S(2)}) collective-permute-start(f32[8,64,128]{2,1,0:T(8,128)S(1)} %multiply_add_fusion.3), channel_id=1, source_target_pairs={{0,16},{8,24},{1,17},{9,25},{2,18},{10,26},{3,19},{11,27},{4,20},{... | collective-permute-start | bytes 786440 | tf_op jit(solution)/shard_map/ppermute | solution.py:613
  36.2 0.0 copy-done
  36.2 0.7 shard_map.139
  37.0 6.0 %all-to-all-start.1 = ((f32[8,2,32,128]{3,2,1,0:T(8,128)}), f32[8,2,32,128]{3,2,1,0:T(8,128)S(1)}, u32[]{:S(2)}, u32[]{:S(2)}) async-start(f32[8,2,32,128]{3,2,1,0:T(8,128)} %shard_map.139), calls=%async_computation.1 | async-start | bytes 524288 | tf_op jit(solution)/shard_map/all_to_all | solution.py:649
  43.0 0.0 collective-permute-done.2
  43.0 1.8 %fusion = (f32[8,64,128]{2,1,0:T(8,128)S(1)}, f32[8,64,128]{2,1,0:T(8,128)}) fusion(f32[8,64,128]{2,1,0:T(8,128)S(1)} %collective-permute-done.2, f32[16,64,128]{2,1,0:T(8,128)S(1)} %copy-done.1, s32[]{:T(128)S(6)} %select_n.82, f32[64,128]{1,0:T(8,128)S(1)} %get-tuple-element.95, pred[]{:T(512)S(6)} %eq.14, f32[8,64,128]{2,1,0:T(8,128)} %get-tuple-element.57, ...), kind=kLoop, calls=%fused_computation.4 | loop fusion | flops 458752 | bytes 1605637 | tf_op jit(solution)/shard_map/jit(_where)/select_n | solution.py:628
  44.8 0.0 collective-permute-start.3
  44.8 1.5 %collective-permute-done.3.refs_5_ = f32[8,64,128]{2,1,0:T(8,128)S(1)} collective-permute-done((f32[8,64,128]{2,1,0:T(8,128)S(1)}, f32[8,64,128]{2,1,0:T(8,128)S(1)}, u32[]{:S(2)}, u32[]{:S(2)}) %collective-permute-start.3) | collective-permute-done | bytes 262176 | tf_op jit(solution)/shard_map/ppermute | solution.py:586
  46.3 0.7 copy-done.6
  47.0 13.1 %shard_map.140 = (f32[16,4,128,128]{3,2,1,0:T(8,128)}, f32[16,4,128,128]{3,2,1,0:T(8,128)}, f32[16,32,128]{2,1,0:T(8,128)}) custom-call(f32[16,128,128]{2,1,0:T(8,128)} %get-tuple-element.49.refs_1_.refs_0_, f32[16,128,128]{2,1,0:T(8,128)} %get-tuple-element.53.refs_1_, f32[16,128,128]{2,1,0:T(8,128)} %get-tuple-element.50.refs_2_.refs_3_, ...), custom_call_target="tpu_custom_call" | custom-call | bytes 33000000 | tf_op jit(solution)/shard_map/pallas_call | solution.py:570
  60.1 0.0 all-to-all-done.1
  60.1 6.0 %all-to-all-start.2 = ((f32[8,2,32,128]{3,2,1,0:T(8,128)}), f32[8,2,32,128]{3,2,1,0:T(8,128)S(1)}, u32[]{:S(2)}, u32[]{:S(2)}) async-start(f32[8,2,32,128]{3,2,1,0:T(8,128)} %bitcast.29), calls=%async_computation.2 | async-start | bytes 524288 | tf_op jit(solution)/shard_map/all_to_all | solution.py:633
  66.1 0.0 copy-done.3
  66.1 13.0 %shard_map.141 = (f32[16,4,128,128]{3,2,1,0:T(8,128)}, f32[16,4,128,128]{3,2,1,0:T(8,128)}, f32[8,64,128]{2,1,0:T(8,128)}, f32[8,64,128]{2,1,0:T(8,128)}) custom-call(f32[16,128,128]{2,1,0:T(8,128)} %get-tuple-element.49.refs_1_.refs_0_, f32[16,128,128]{2,1,0:T(8,128)} %get-tuple-element.54.refs_1_.refs_2_, ...), custom_call_target="tpu_custom_call" | custom-call | bytes 33000000 | tf_op jit(solution)/shard_map/pallas_call | solution.py:570
  79.1 0.0 all-to-all-done.2.held
  79.1 0.1 collective-permute-start.4
  79.2 0.7 shard_map.142
  79.9 6.0 %all-to-all-start.3 = ((f32[8,2,32,128]{3,2,1,0:T(8,128)}), f32[8,2,32,128]{3,2,1,0:T(8,128)S(1)}, u32[]{:S(2)}, u32[]{:S(2)}) async-start(f32[8,2,32,128]{3,2,1,0:T(8,128)} %shard_map.142), calls=%async_computation.3 | async-start | bytes 524288 | tf_op jit(solution)/shard_map/all_to_all | solution.py:649
  85.9 0.0 collective-permute-done.4
  85.9 1.0 multiply_add_fusion.1
  87.0 1.3 collective-permute-start.5
  88.3 7.2 %all-to-all-done.3 = f32[8,2,32,128]{3,2,1,0:T(8,128)S(1)} async-done(((f32[8,2,32,128]{3,2,1,0:T(8,128)}), f32[8,2,32,128]{3,2,1,0:T(8,128)S(1)}, u32[]{:S(2)}, u32[]{:S(2)}) %all-to-all-start.3) | async-done | bytes 262176 | tf_op jit(solution)/shard_map/all_to_all | solution.py:649
  95.5 1.8 %collective-permute-done.5 = f32[8,64,128]{2,1,0:T(8,128)S(1)} collective-permute-done((f32[8,64,128]{2,1,0:T(8,128)S(1)}, f32[8,64,128]{2,1,0:T(8,128)S(1)}, u32[]{:S(2)}, u32[]{:S(2)}) %collective-permute-start.5) | collective-permute-done | bytes 262176 | tf_op jit(solution)/shard_map/ppermute | solution.py:613
  97.3 0.8 fusion.2
  98.1 0.3 collective-permute-start.6
  98.4 1.2 collective-permute-done.6.refs_10_
  99.6 0.7 copy-done.5
  100.3 26.0 %shard_map.143 = (f32[16,128,128]{2,1,0:T(8,128)}, f32[16,128,128]{2,1,0:T(8,128)}, f32[16,128,128]{2,1,0:T(8,128)}, f32[16,128,128]{2,1,0:T(8,128)}, f32[16,128]{1,0:T(8,128)}) custom-call(f32[16,128,128]{2,1,0:T(8,128)} %get-tuple-element.49.refs_1_.refs_0_, f32[16,128,128]{2,1,0:T(8,128)} %get-tuple-element.53.refs_1_, ...), custom_call_target="tpu_custom_call" | custom-call | bytes 82500000 | tf_op jit(solution)/shard_map/pallas_call | solution.py:570
  126.3 0.4 collective-permute-start.7
  126.7 1.0 collective-permute-done.7
  127.8 0.7 add.36
  128.5 0.0 collective-permute-start.8
  128.5 3.6 %collective-permute-done.8 = f32[16,128]{1,0:T(8,128)S(1)} collective-permute-done((f32[16,128]{1,0:T(8,128)S(1)}, f32[16,128]{1,0:T(8,128)S(1)}, u32[]{:S(2)}, u32[]{:S(2)}) %collective-permute-start.8) | collective-permute-done | bytes 8224 | tf_op jit(solution)/shard_map/ppermute | solution.py:656
  132.1 0.6 broadcast_in_dim.2
  132.8 5.7 %all-to-all-start.4 = ((f32[8,16,128]{2,1,0:T(8,128)}), f32[8,16,128]{2,1,0:T(8,128)S(1)}, u32[]{:S(2)}, u32[]{:S(2)}) async-start(f32[8,16,128]{2,1,0:T(8,128)} %broadcast_in_dim.2), calls=%async_computation.4 | async-start | bytes 131072 | tf_op jit(solution)/shard_map/all_to_all | solution.py:658
  138.5 4.4 %shard_map.144 = (f32[8,4,64,128]{3,2,1,0:T(8,128)}, f32[8,4,64,128]{3,2,1,0:T(8,128)}, f32[8,4,16,64]{3,2,1,0:T(8,128)}, f32[8,4,16,64]{3,2,1,0:T(8,128)}) custom-call(f32[16,128,128]{2,1,0:T(8,128)} %get-tuple-element.80.refs_0_, f32[16,128,128]{2,1,0:T(8,128)} %get-tuple-element.81.refs_1_, f32[16,128,128]{2,1,0:T(8,128)} %get-tuple-element.82.refs_2_, ...), custom_call_target="tpu_custom_call" | custom-call | bytes 16500000 | tf_op jit(solution)/shard_map/pallas_call | solution.py:570
  142.9 2.5 %all-to-all-done.4 = f32[8,16,128]{2,1,0:T(8,128)S(1)} async-done(((f32[8,16,128]{2,1,0:T(8,128)}), f32[8,16,128]{2,1,0:T(8,128)S(1)}, u32[]{:S(2)}, u32[]{:S(2)}) %all-to-all-start.4) | async-done | bytes 65568 | tf_op jit(solution)/shard_map/all_to_all | solution.py:658
  145.4 0.6 reduce_sum.9
  (11 shorter events, 0.0 us)
Async XLA Ops:
  12.0 18.0 %copy-start.4 = (f32[64,128]{1,0:T(8,128)S(1)}, f32[64,128]{1,0:T(8,128)}, u32[]{:S(2)}) copy-start(f32[64,128]{1,0:T(8,128)} %get-tuple-element.52.refs_5_.refs_16_) | copy-start | bytes 98308
  12.0 19.8 %copy-start.1 = (f32[16,64,128]{2,1,0:T(8,128)S(1)}, f32[16,64,128]{2,1,0:T(8,128)}, u32[]{:S(2)}) copy-start(f32[16,64,128]{2,1,0:T(8,128)} %get-tuple-element.51.refs_4_.refs_13_) | copy-start | bytes 1572868
  12.0 24.2 %copy-start = (f32[2,32,128]{2,1,0:T(8,128)S(1)}, f32[2,32,128]{2,1,0:T(8,128)}, u32[]{:S(2)}) copy-start(f32[2,32,128]{2,1,0:T(8,128)} %get-tuple-element.60.rates) | copy-start | bytes 98308
  12.0 20.8 %all-to-all-start = ((f32[8,3,32,128]{3,2,1,0:T(8,128)}), f32[8,3,32,128]{3,2,1,0:T(8,128)S(1)}, u32[]{:S(2)}, u32[]{:S(2)}) async-start(f32[8,3,32,128]{3,2,1,0:T(8,128)} %get-tuple-element.48), calls=%async_computation | async-start | bytes 786432 | tf_op jit(solution)/shard_map/all_to_all | solution.py:633
  29.9 1.8 %collective-permute-start = (f32[8,64,128]{2,1,0:T(8,128)}, f32[8,64,128]{2,1,0:T(8,128)S(1)}, u32[]{:S(2)}, u32[]{:S(2)}) collective-permute-start(f32[8,64,128]{2,1,0:T(8,128)} %get-tuple-element.56), channel_id=1, source_target_pairs={{0,8},{8,0},{16,24},{24,16},{1,9},{9,1},{17,25},{25,17},{2,10},{10... | collective-permute-start | bytes 786440 | tf_op jit(solution)/shard_map/ppermute | solution.py:586
  30.0 1.6 %collective-permute-start.1 = (f32[64,128]{1,0:T(8,128)S(1)}, f32[64,128]{1,0:T(8,128)S(1)}, u32[]{:S(2)}, u32[]{:S(2)}) collective-permute-start(f32[64,128]{1,0:T(8,128)S(1)} %copy-done.4), channel_id=1, source_target_pairs={{0,8},{8,0},{16,24},{24,16},{1,9},{9,1},{17,25},{25,17},{2,10},{10... | collective-permute-start | bytes 98312 | tf_op jit(solution)/shard_map/ppermute | solution.py:586
  32.8 10.2 %collective-permute-start.2 = (f32[8,64,128]{2,1,0:T(8,128)S(1)}, f32[8,64,128]{2,1,0:T(8,128)S(1)}, u32[]{:S(2)}, u32[]{:S(2)}) collective-permute-start(f32[8,64,128]{2,1,0:T(8,128)S(1)} %multiply_add_fusion.3), channel_id=1, source_target_pairs={{0,16},{8,24},{1,17},{9,25},{2,18},{10,26},{3,19},{11,27},{4,20},{... | collective-permute-start | bytes 786440 | tf_op jit(solution)/shard_map/ppermute | solution.py:613
  37.0 23.1 %all-to-all-start.1 = ((f32[8,2,32,128]{3,2,1,0:T(8,128)}), f32[8,2,32,128]{3,2,1,0:T(8,128)S(1)}, u32[]{:S(2)}, u32[]{:S(2)}) async-start(f32[8,2,32,128]{3,2,1,0:T(8,128)} %shard_map.139), calls=%async_computation.1 | async-start | bytes 524288 | tf_op jit(solution)/shard_map/all_to_all | solution.py:649
  44.8 1.5 %collective-permute-start.3 = (f32[8,64,128]{2,1,0:T(8,128)S(1)}, f32[8,64,128]{2,1,0:T(8,128)S(1)}, u32[]{:S(2)}, u32[]{:S(2)}) collective-permute-start(f32[8,64,128]{2,1,0:T(8,128)S(1)} %get-tuple-element.91), channel_id=1, source_target_pairs={{0,8},{8,0},{16,24},{24,16},{1,9},{9,1},{17,25},{25,17},{2,10},{10... | collective-permute-start | bytes 786440 | tf_op jit(solution)/shard_map/ppermute | solution.py:586
  46.3 0.7 copy-start.6
  60.1 6.0 %copy-start.3 = (f32[8,2,32,128]{3,2,1,0:T(8,128)}, f32[8,2,32,128]{3,2,1,0:T(8,128)S(1)}, u32[]{:S(2)}) copy-start(f32[8,2,32,128]{3,2,1,0:T(8,128)S(1)} %all-to-all-done.1) | copy-start | bytes 786436
  60.1 19.0 %all-to-all-start.2 = ((f32[8,2,32,128]{3,2,1,0:T(8,128)}), f32[8,2,32,128]{3,2,1,0:T(8,128)S(1)}, u32[]{:S(2)}, u32[]{:S(2)}) async-start(f32[8,2,32,128]{3,2,1,0:T(8,128)} %bitcast.29), calls=%async_computation.2 | async-start | bytes 524288 | tf_op jit(solution)/shard_map/all_to_all | solution.py:633
  79.1 6.8 %collective-permute-start.4 = (f32[8,64,128]{2,1,0:T(8,128)}, f32[8,64,128]{2,1,0:T(8,128)S(1)}, u32[]{:S(2)}, u32[]{:S(2)}) collective-permute-start(f32[8,64,128]{2,1,0:T(8,128)} %get-tuple-element.77), channel_id=1, source_target_pairs={{0,8},{8,0},{16,24},{24,16},{1,9},{9,1},{17,25},{25,17},{2,10},{10... | collective-permute-start | bytes 786440 | tf_op jit(solution)/shard_map/ppermute | solution.py:586
  79.9 15.6 %all-to-all-start.3 = ((f32[8,2,32,128]{3,2,1,0:T(8,128)}), f32[8,2,32,128]{3,2,1,0:T(8,128)S(1)}, u32[]{:S(2)}, u32[]{:S(2)}) async-start(f32[8,2,32,128]{3,2,1,0:T(8,128)} %shard_map.142), calls=%async_computation.3 | async-start | bytes 524288 | tf_op jit(solution)/shard_map/all_to_all | solution.py:649
  87.0 10.3 %collective-permute-start.5 = (f32[8,64,128]{2,1,0:T(8,128)S(1)}, f32[8,64,128]{2,1,0:T(8,128)S(1)}, u32[]{:S(2)}, u32[]{:S(2)}) collective-permute-start(f32[8,64,128]{2,1,0:T(8,128)S(1)} %multiply_add_fusion.1), channel_id=1, source_target_pairs={{16,0},{24,8},{17,1},{25,9},{18,2},{26,10},{19,3},{27,11},{20,4},{... | collective-permute-start | bytes 786440 | tf_op jit(solution)/shard_map/ppermute | solution.py:613
  95.5 4.1 %copy-start.2 = (f32[8,2,32,128]{3,2,1,0:T(8,128)}, f32[8,2,32,128]{3,2,1,0:T(8,128)S(1)}, u32[]{:S(2)}) copy-start(f32[8,2,32,128]{3,2,1,0:T(8,128)S(1)} %all-to-all-done.3) | copy-start | bytes 786436
  98.1 1.5 %collective-permute-start.6 = (f32[8,64,128]{2,1,0:T(8,128)S(1)}, f32[8,64,128]{2,1,0:T(8,128)S(1)}, u32[]{:S(2)}, u32[]{:S(2)}) collective-permute-start(f32[8,64,128]{2,1,0:T(8,128)S(1)} %get-tuple-element.89), channel_id=1, source_target_pairs={{0,8},{8,0},{16,24},{24,16},{1,9},{9,1},{17,25},{25,17},{2,10},{10... | collective-permute-start | bytes 786440 | tf_op jit(solution)/shard_map/ppermute | solution.py:586
  99.6 0.7 copy-start.5
  126.3 1.5 collective-permute-start.7
  128.5 3.7 %collective-permute-start.8 = (f32[16,128]{1,0:T(8,128)S(1)}, f32[16,128]{1,0:T(8,128)S(1)}, u32[]{:S(2)}, u32[]{:S(2)}) collective-permute-start(f32[16,128]{1,0:T(8,128)S(1)} %add.36), channel_id=1, source_target_pairs={{0,16},{8,24},{16,0},{24,8},{1,17},{9,25},{17,1},{25,9},{2,18},{10... | collective-permute-start | bytes 24584 | tf_op jit(solution)/shard_map/ppermute | solution.py:656
  132.8 12.6 %all-to-all-start.4 = ((f32[8,16,128]{2,1,0:T(8,128)}), f32[8,16,128]{2,1,0:T(8,128)S(1)}, u32[]{:S(2)}, u32[]{:S(2)}) async-start(f32[8,16,128]{2,1,0:T(8,128)} %broadcast_in_dim.2), calls=%async_computation.4 | async-start | bytes 131072 | tf_op jit(solution)/shard_map/all_to_all | solution.py:658

commit v4 on v3

--- a/solution.py
+++ b/solution.py
@@ -402,6 +402,7 @@
             r = [rates[n, d] for n in ns]
             vert = [[start_rows[n, j, d] for j in range(BJ)] for n in ns]
             from_v, from_s = [{} for _ in ns], [{} for _ in ns]
+            exps = [{} for _ in ns]
             for i in range(BI):
                 before = before_cols[i, d]
                 state = [seg_s[n, i, d] * jnp.exp2(r[k] * before) for k, n in enumerate(ns)]
@@ -409,7 +410,8 @@
                     p = i * BJ + j
                     c, s, g = step_p[p, d], source_p[p, d], grad_p[p, d]
                     for k, n in enumerate(ns):
-                        decay = jnp.exp2(c * r[k])
+                        m = c * r[k]
+                        decay = jnp.exp2(m)
                         dv = decay * vert[k][j]
                         vert[k][j] = dv + s * row_of(write_p, p, n)
                         ds = decay * state[k]
@@ -417,6 +419,7 @@
                         sum_r[p, pl.ds(n * 8, 8)] += state[k] * g
                         from_v[k][p] = dv
                         from_s[k][p] = ds
+                        exps[k][p] = m
             passed_v = [[None] * BJ for _ in ns]
             for j in range(BJ):
                 after = before_rows[j, d]
@@ -429,11 +432,11 @@
                 passed = [start_cols[n, i, d] for n in ns]
                 for j in reversed(range(BJ)):
                     p = i * BJ + j
-                    c, s, g = step_p[p, d], source_p[p, d], grad_p[p, d]
+                    s, g = source_p[p, d], grad_p[p, d]
                     sum_q, sum_t = None, None
                     for k, n in enumerate(ns):
                         adjoint = g * row_of(read_p, p, n) + passed[k]
-                        m = c * r[k]
+                        m = exps[k][p]
                         decay = jnp.exp2(m)
                         passed[k] = decay * adjoint
                         adjoint_v = adjoint + passed_v[k][j]
@@ -508,60 +511,65 @@
 def run(stage, ins, outs, scratch=(), micros=5):
     in_kinds, out_kinds = [k for _, k in ins], [k for _, k in outs]
     shapes = [a.shape for a, _ in ins] + [s for s, _ in outs]
+    types = [a.dtype for a, _ in ins] + [F32 for _ in outs]
     kinds = in_kinds + out_kinds
-    streamed = [at for at, k in enumerate(kinds) if k not in ("whole", "scalar")]
+    phase = {"whole": 0, "second": 1, "first": 1, "channels": 2}
+    copied = [at for at, k in enumerate(kinds) if k in phase]
     count = len(ins)
 
     def kernel(*refs):
         given = list(refs[: len(kinds)])
         rest = refs[len(kinds) :]
-        buffers, sems = rest[: len(streamed)], rest[len(streamed)]
-        extra = rest[len(streamed) + 1 :]
+        buffers, sems = rest[: len(copied)], rest[len(copied)]
+        extra = rest[len(copied) + 1 :]
         views = list(given)
-        copies = {}
-        for slot, at in enumerate(streamed):
+        into, out_of = [[], [], []], [[], [], []]
+        for slot, at in enumerate(copied):
             views[at] = buffers[slot]
 
             def copy(k, slot=slot, at=at):
-                far, near = cut(given[at], kinds[at], k), cut(buffers[slot], kinds[at], k)
+                far, near = given[at], buffers[slot]
+                if kinds[at] != "whole":
+                    far, near = cut(far, kinds[at], k), cut(near, kinds[at], k)
                 pair = (far, near) if at < count else (near, far)
                 return pltpu.make_async_copy(*pair, sems.at[slot, k])
 
-            copies[at] = copy
-
-        def chosen(inputs, channels):
-            return [
-                copies[at] for at in streamed
-                if (at < count) == inputs and (kinds[at] == "channels") == channels
-            ]
-
-        for channels in (False, True):
-            for k in range(STEPS):
-                for copy in chosen(True, channels):
+            (into if at < count else out_of)[phase[kinds[at]]].append(copy)
+
+        def part(which, name):
+            def one(k, carry):
+                for copy in into[which]:
+                    copy(k).wait()
+                getattr(stage, name)(k, *views, *extra)
+                for copy in out_of[which]:
                     copy(k).start()
+                return carry
+
+            lax.fori_loop(0, STEPS, one, 0)
+
+        for which in range(3):
+            for k in range(STEPS if which else 1):
+                for copy in into[which]:
+                    copy(k).start()
+        for copy in into[0]:
+            copy(0).wait()
         if hasattr(stage, "first"):
             stage.first(*views, *extra)
-        for channels, part in ((False, "lead"), (True, "main")):
-            def one(k, carry):
-                for copy in chosen(True, channels):
-                    copy(k).wait()
-                if hasattr(stage, part):
-                    getattr(stage, part)(k, *views, *extra)
-                for copy in chosen(False, channels):
-                    copy(k).start()
-                return carry
-
-            if hasattr(stage, part) or chosen(True, channels):
-                lax.fori_loop(0, STEPS, one, 0)
+        if hasattr(stage, "lead"):
+            part(1, "lead")
+        if hasattr(stage, "main"):
+            part(2, "main")
         if hasattr(stage, "last"):
             stage.last(*views, *extra)
-        for channels in (False, True):
-            for k in range(STEPS):
-                for copy in chosen(False, channels):
+        for copy in out_of[0]:
+            copy(0).start()
+        for which in range(3):
+            for k in range(STEPS if which else 1):
+                for copy in out_of[which]:
                     copy(k).wait()
 
     def spec(kind):
-        if kind == "whole":
+        if kind == "small":
             return pl.BlockSpec(memory_space=pltpu.VMEM)
         if kind == "scalar":
             return pl.BlockSpec(memory_space=pltpu.SMEM)
@@ -572,8 +580,8 @@
         out_shape=[jax.ShapeDtypeStruct(s, F32) for s, _ in outs],
         in_specs=[spec(k) for k in in_kinds],
         out_specs=[spec(k) for k in out_kinds],
-        scratch_shapes=[pltpu.VMEM(shapes[at], F32) for at in streamed]
-        + [pltpu.SemaphoreType.DMA((len(streamed), STEPS))]
+        scratch_shapes=[pltpu.VMEM(shapes[at], types[at]) for at in copied]
+        + [pltpu.SemaphoreType.DMA((len(copied), STEPS))]
         + [pltpu.VMEM(s, F32) for s in scratch],
         compiler_params=pltpu.CompilerParams(vmem_limit_bytes=60 << 20),
         cost_estimate=pl.CostEstimate(
@@ -682,7 +690,7 @@
         AdjointCols(),
         [(step_size.reshape(packed), "second"), (out_grad.reshape(packed), "second"),
          (read_weights.swapaxes(1, 2).reshape(weights), "second"),
-         (decay_log.reshape(BI, states // BI, D), "whole"), (place, "scalar"),
+         (decay_log.reshape(BI, states // BI, D), "small"), (place, "scalar"),
          (orders["left"], "whole"), (orders["right"], "whole")],
         [(plane, "first"), (plane, "first"), (all_rates, "first"), (seg, "channels"),
          (small, "whole"), (size_v, "whole"), (size_s, "whole"), ((share,) + size_s[1:], "whole"),
@@ -728,10 +736,11 @@
         [size_s, size_v], 10,
     )
     held, give = tied(held, give)
+    total = row_total(keep, give, sum_rows, other_rows, rates_v, rows, True)
+    held, first = tied(held, total[0])
     carries = col_carry(held, col_sums, own_rates, False)
     enter_s = col_return(carries)
-    total = row_total(keep, give, sum_rows, other_rows, rates_v, rows, True)
-    keep, got = row_carry(*total, enter_s, rows, True)
+    keep, got = row_carry(first, *total[1:], carries, rows, True)
     features_p, steps_p, sum_w, sum_r, grad_decay = run(
         Final(),
         [(step_p, "channels"), (source_p, "channels"), (grad_p, "channels"),

time: 147 us -> 139 us (0.946)
  Pallas kernels: 79.8 us -> 74.1 us
  waiting for transfers between devices: 20.2 us -> 18.2 us
    pallas_call x6, Pallas kernels: 78.3 us -> 72.6 us  [run(): pl.pallas_call(kernel, out_shape=[jax.ShapeDtypeStruct(s, F32) for s, _ i...]
    all_to_all x1, starting transfers between devices: 5.71 us -> 3.59 us  [total_of(): lax.all_to_all(jnp.broadcast_to(x[None], (cols,) + x.shape), 'col', 0, 0)]
    ppermute x2, starting transfers between devices: 0.42 us -> 2.44 us  [total_of(): x = x + lax.ppermute(x, 'row', [(k, k ^ by) for k in range(rows)])]
    ppermute x2, waiting for transfers between devices: 4.69 us -> 3 us  [total_of(): x = x + lax.ppermute(x, 'row', [(k, k ^ by) for k in range(rows)])]
  transfers between devices with their start and end apart: 14 -> 14, of which waited for: 9 -> 9; matrix products, arithmetic and copies ran while one was open for 3% -> 3% of each run, Pallas kernels for 29% -> 28%
where the time goes in v4:
time: 139 us; the launch traced here: 138 us
  Pallas kernels  74.1 us (53%)
  starting transfers between devices  37 us (27%)
  waiting for transfers between devices  18.2 us (13%)
  other arithmetic  5.93 us (4%)
  local copies, waits for them, and re-layouts  2.15 us (2%)
    pallas_call x6, Pallas kernels, run(): pl.pallas_call(kernel, out_shape=[jax.ShapeDtypeStruct(s, F32) for s, _ i...  72.6 us
    all_to_all x2, starting transfers between devices, col_gather(): return lax.all_to_all(sent, 'col', 0, 0)  13.4 us
    all_to_all x2, starting transfers between devices, col_return(): back = lax.all_to_all(carries, 'col', 0, 0)  12 us
    all_to_all x2, waiting for transfers between devices, col_return(): back = lax.all_to_all(carries, 'col', 0, 0)  5.97 us
    ppermute x2, starting transfers between devices, shift(): lax.ppermute(x, 'row', [(k, k + by) for k in range(size) if 0 <= k + by <...  4.72 us
    ppermute x5, waiting for transfers between devices, swap_cores(): return lax.ppermute(x, 'row', [(k, k ^ 1) for k in range(size)])  4.49 us
    all_to_all x1, starting transfers between devices, total_of(): lax.all_to_all(jnp.broadcast_to(x[None], (cols,) + x.shape), 'col', 0, 0)  3.59 us
    ppermute x2, waiting for transfers between devices, total_of(): x = x + lax.ppermute(x, 'row', [(k, k ^ by) for k in range(rows)])  3 us
  transfers between devices with their start and end apart: 14, of which 9 were waited for; matrix products, arithmetic and copies ran while one was open for 3% of the time, Pallas kernels for 28%

profile of v4, /device:TPU:0, one launch (start us, length us, event | category | flops | bytes accessed | tf_op | source)
XLA Modules:
  0.0 138.2 jit_solution(2142922557382744824)
XLA Ops:
  0.6 10.9 %shard_map.137 = (f32[16,128,128]{2,1,0:T(8,128)}, f32[16,128,128]{2,1,0:T(8,128)}, f32[16,128,128]{2,1,0:T(8,128)}, f32[16,4,128,128]{3,2,1,0:T(8,128)}, f32[16...) custom-call(f32[8,4,64,128]{3,2,1,0:T(8,128)} %bitcast.25, ...), custom_call_target="tpu_custom_call" | custom-call | bytes 16500000 | tf_op jit(solution)/shard_map/pallas_call | solution.py:578
  11.5 0.0 copy-start.4
  11.6 0.0 copy-start.1
  11.6 7.4 %all-to-all-start = ((f32[8,3,32,128]{3,2,1,0:T(8,128)}), f32[8,3,32,128]{3,2,1,0:T(8,128)S(1)}, u32[]{:S(2)}, u32[]{:S(2)}) async-start(f32[8,3,32,128]{3,2,1,0:T(8,128)} %get-tuple-element.50), calls=%async_computation | async-start | bytes 786432 | tf_op jit(solution)/shard_map/all_to_all | solution.py:641
  19.0 9.2 %shard_map.138 = (f32[16,128,128]{2,1,0:T(8,128)}, f32[16,4,128,128]{3,2,1,0:T(8,128)}, f32[16,16,128]{2,1,0:T(8,128)}, f32[4,128,128]{2,1,0:T(8,128)}, f32[8,64,128]{2,1,0:T(8,128)}, /*index=5*/f32[8,64,128]{2,1,0:T(8,128)}) custom-call(f32[8,4,64,128]{3,2,1,0:T(8,128)} %bitcast.27, f32[16,128,128]{2,1,0:T(8,128)} %get-tuple-element.51.refs_1_.refs_0_, ...), custom_call_target="tpu_custom_call" | custom-call | bytes 16500000 | tf_op jit(solution)/shard_map/pallas_call | solution.py:578
  28.2 0.1 collective-permute-start
  28.3 0.5 collective-permute-start.1
  28.8 1.1 collective-permute-done.1
  29.9 0.1 collective-permute-done
  30.0 1.0 multiply_add_fusion.3
  31.0 0.0 all-to-all-done.held.sums
  31.0 3.4 %collective-permute-start.2 = (f32[8,64,128]{2,1,0:T(8,128)S(1)}, f32[8,64,128]{2,1,0:T(8,128)S(1)}, u32[]{:S(2)}, u32[]{:S(2)}) collective-permute-start(f32[8,64,128]{2,1,0:T(8,128)S(1)} %multiply_add_fusion.3), channel_id=1, source_target_pairs={{0,16},{8,24},{1,17},{9,25},{2,18},{10,26},{3,19},{11,27},{4,20},{... | collective-permute-start | bytes 786440 | tf_op jit(solution)/shard_map/ppermute | solution.py:621
  34.5 0.7 shard_map.139
  35.2 6.0 %all-to-all-start.1 = ((f32[8,2,32,128]{3,2,1,0:T(8,128)}), f32[8,2,32,128]{3,2,1,0:T(8,128)S(1)}, u32[]{:S(2)}, u32[]{:S(2)}) async-start(f32[8,2,32,128]{3,2,1,0:T(8,128)} %shard_map.139), calls=%async_computation.1 | async-start | bytes 524288 | tf_op jit(solution)/shard_map/all_to_all | solution.py:657
  41.2 0.0 collective-permute-done.2
  41.2 1.8 %fusion = (f32[8,64,128]{2,1,0:T(8,128)S(1)}, f32[8,64,128]{2,1,0:T(8,128)}) fusion(f32[8,64,128]{2,1,0:T(8,128)S(1)} %collective-permute-done.2, f32[16,64,128]{2,1,0:T(8,128)S(1)} %copy-done.1, s32[]{:T(128)S(6)} %select_n.82, f32[64,128]{1,0:T(8,128)S(1)} %get-tuple-element.99, pred[]{:T(512)S(6)} %eq.14, f32[8,64,128]{2,1,0:T(8,128)} %get-tuple-element.59, ...), kind=kLoop, calls=%fused_computation.4 | loop fusion | flops 458752 | bytes 1605637 | tf_op jit(solution)/shard_map/jit(_where)/select_n | solution.py:636
  43.0 0.0 collective-permute-start.3
  43.0 1.5 %collective-permute-done.3.refs_5_ = f32[8,64,128]{2,1,0:T(8,128)S(1)} collective-permute-done((f32[8,64,128]{2,1,0:T(8,128)S(1)}, f32[8,64,128]{2,1,0:T(8,128)S(1)}, u32[]{:S(2)}, u32[]{:S(2)}) %collective-permute-start.3) | collective-permute-done | bytes 262176 | tf_op jit(solution)/shard_map/ppermute | solution.py:594
  44.5 0.7 copy-done.6
  45.2 11.9 %shard_map.140 = (f32[16,4,128,128]{3,2,1,0:T(8,128)}, f32[16,4,128,128]{3,2,1,0:T(8,128)}, f32[16,32,128]{2,1,0:T(8,128)}) custom-call(f32[16,128,128]{2,1,0:T(8,128)} %get-tuple-element.51.refs_1_.refs_0_, f32[16,128,128]{2,1,0:T(8,128)} %get-tuple-element.55.refs_1_, f32[16,128,128]{2,1,0:T(8,128)} %get-tuple-element.52.refs_2_.refs_3_, ...), custom_call_target="tpu_custom_call" | custom-call | bytes 33000000 | tf_op jit(solution)/shard_map/pallas_call | solution.py:578
  57.2 0.0 all-to-all-done.1
  57.2 6.0 %all-to-all-start.2 = ((f32[8,2,32,128]{3,2,1,0:T(8,128)}), f32[8,2,32,128]{3,2,1,0:T(8,128)S(1)}, u32[]{:S(2)}, u32[]{:S(2)}) async-start(f32[8,2,32,128]{3,2,1,0:T(8,128)} %bitcast.29), calls=%async_computation.2 | async-start | bytes 524288 | tf_op jit(solution)/shard_map/all_to_all | solution.py:641
  63.2 11.8 %shard_map.141 = (f32[16,4,128,128]{3,2,1,0:T(8,128)}, f32[16,4,128,128]{3,2,1,0:T(8,128)}, f32[8,64,128]{2,1,0:T(8,128)}, f32[8,64,128]{2,1,0:T(8,128)}) custom-call(f32[16,128,128]{2,1,0:T(8,128)} %get-tuple-element.51.refs_1_.refs_0_, f32[16,128,128]{2,1,0:T(8,128)} %get-tuple-element.56.refs_1_.refs_2_, ...), custom_call_target="tpu_custom_call" | custom-call | bytes 33000000 | tf_op jit(solution)/shard_map/pallas_call | solution.py:578
  75.0 0.0 all-to-all-done.2.held
  75.0 0.1 collective-permute-start.4
  75.1 1.7 %collective-permute-done.4 = f32[8,64,128]{2,1,0:T(8,128)S(1)} collective-permute-done((f32[8,64,128]{2,1,0:T(8,128)}, f32[8,64,128]{2,1,0:T(8,128)S(1)}, u32[]{:S(2)}, u32[]{:S(2)}) %collective-permute-start.4) | collective-permute-done | bytes 262176 | tf_op jit(solution)/shard_map/ppermute | solution.py:594
  76.8 1.0 multiply_add_fusion.1
  77.9 1.3 collective-permute-start.5
  79.2 0.7 shard_map.142
  79.9 6.0 %all-to-all-start.3 = ((f32[8,2,32,128]{3,2,1,0:T(8,128)}), f32[8,2,32,128]{3,2,1,0:T(8,128)S(1)}, u32[]{:S(2)}, u32[]{:S(2)}) async-start(f32[8,2,32,128]{3,2,1,0:T(8,128)} %shard_map.142), calls=%async_computation.3 | async-start | bytes 524288 | tf_op jit(solution)/shard_map/all_to_all | solution.py:657
  85.9 2.2 %collective-permute-done.5 = f32[8,64,128]{2,1,0:T(8,128)S(1)} collective-permute-done((f32[8,64,128]{2,1,0:T(8,128)S(1)}, f32[8,64,128]{2,1,0:T(8,128)S(1)}, u32[]{:S(2)}, u32[]{:S(2)}) %collective-permute-start.5) | collective-permute-done | bytes 262176 | tf_op jit(solution)/shard_map/ppermute | solution.py:621
  88.1 0.8 fusion.2
  88.9 0.3 collective-permute-start.6
  89.1 6.0 %all-to-all-done.3 = f32[8,2,32,128]{3,2,1,0:T(8,128)S(1)} async-done(((f32[8,2,32,128]{3,2,1,0:T(8,128)}), f32[8,2,32,128]{3,2,1,0:T(8,128)S(1)}, u32[]{:S(2)}, u32[]{:S(2)}) %all-to-all-start.3) | async-done | bytes 262176 | tf_op jit(solution)/shard_map/all_to_all | solution.py:657
  95.1 0.0 collective-permute-done.6.refs_10_
  95.1 0.7 copy-done.2
  95.8 0.1 copy-done.5
  95.9 24.4 %shard_map.143 = (f32[16,128,128]{2,1,0:T(8,128)}, f32[16,128,128]{2,1,0:T(8,128)}, f32[16,128,128]{2,1,0:T(8,128)}, f32[16,128,128]{2,1,0:T(8,128)}, f32[16,128]{1,0:T(8,128)}) custom-call(f32[16,128,128]{2,1,0:T(8,128)} %get-tuple-element.51.refs_1_.refs_0_, f32[16,128,128]{2,1,0:T(8,128)} %get-tuple-element.55.refs_1_, ...), custom_call_target="tpu_custom_call" | custom-call | bytes 82500000 | tf_op jit(solution)/shard_map/pallas_call | solution.py:578
  120.3 0.1 collective-permute-start.7
  120.4 1.4 collective-permute-done.7
  121.8 0.7 add.36
  122.5 2.4 %collective-permute-start.8 = (f32[16,128]{1,0:T(8,128)S(1)}, f32[16,128]{1,0:T(8,128)S(1)}, u32[]{:S(2)}, u32[]{:S(2)}) collective-permute-start(f32[16,128]{1,0:T(8,128)S(1)} %add.36), channel_id=1, source_target_pairs={{0,16},{8,24},{16,0},{24,8},{1,17},{9,25},{17,1},{25,9},{2,18},{10... | collective-permute-start | bytes 24584 | tf_op jit(solution)/shard_map/ppermute | solution.py:664
  124.8 1.6 %collective-permute-done.8 = f32[16,128]{1,0:T(8,128)S(1)} collective-permute-done((f32[16,128]{1,0:T(8,128)S(1)}, f32[16,128]{1,0:T(8,128)S(1)}, u32[]{:S(2)}, u32[]{:S(2)}) %collective-permute-start.8) | collective-permute-done | bytes 8224 | tf_op jit(solution)/shard_map/ppermute | solution.py:664
  126.5 0.6 broadcast_in_dim.2
  127.1 3.6 %all-to-all-start.4 = ((f32[8,16,128]{2,1,0:T(8,128)}), f32[8,16,128]{2,1,0:T(8,128)S(1)}, u32[]{:S(2)}, u32[]{:S(2)}) async-start(f32[8,16,128]{2,1,0:T(8,128)} %broadcast_in_dim.2), calls=%async_computation.4 | async-start | bytes 131072 | tf_op jit(solution)/shard_map/all_to_all | solution.py:666
  130.7 4.4 %shard_map.144 = (f32[8,4,64,128]{3,2,1,0:T(8,128)}, f32[8,4,64,128]{3,2,1,0:T(8,128)}, f32[8,4,16,64]{3,2,1,0:T(8,128)}, f32[8,4,16,64]{3,2,1,0:T(8,128)}) custom-call(f32[16,128,128]{2,1,0:T(8,128)} %get-tuple-element.84.refs_0_, f32[16,128,128]{2,1,0:T(8,128)} %get-tuple-element.85.refs_1_, f32[16,128,128]{2,1,0:T(8,128)} %get-tuple-element.86.refs_2_, ...), custom_call_target="tpu_custom_call" | custom-call | bytes 16500000 | tf_op jit(solution)/shard_map/pallas_call | solution.py:578
  135.1 2.5 %all-to-all-done.4 = f32[8,16,128]{2,1,0:T(8,128)S(1)} async-done(((f32[8,16,128]{2,1,0:T(8,128)}), f32[8,16,128]{2,1,0:T(8,128)S(1)}, u32[]{:S(2)}, u32[]{:S(2)}) %all-to-all-start.4) | async-done | bytes 65568 | tf_op jit(solution)/shard_map/all_to_all | solution.py:666
  137.6 0.6 reduce_sum.9
  (11 shorter events, 0.0 us)
Async XLA Ops:
  11.5 16.7 %copy-start.4 = (f32[64,128]{1,0:T(8,128)S(1)}, f32[64,128]{1,0:T(8,128)}, u32[]{:S(2)}) copy-start(f32[64,128]{1,0:T(8,128)} %get-tuple-element.54.refs_5_.refs_16_) | copy-start | bytes 98308
  11.6 18.4 %copy-start.1 = (f32[16,64,128]{2,1,0:T(8,128)S(1)}, f32[16,64,128]{2,1,0:T(8,128)}, u32[]{:S(2)}) copy-start(f32[16,64,128]{2,1,0:T(8,128)} %get-tuple-element.53.refs_4_.refs_13_) | copy-start | bytes 1572868
  11.6 22.9 %copy-start = (f32[2,32,128]{2,1,0:T(8,128)S(1)}, f32[2,32,128]{2,1,0:T(8,128)}, u32[]{:S(2)}) copy-start(f32[2,32,128]{2,1,0:T(8,128)} %get-tuple-element.62.rates) | copy-start | bytes 98308
  11.6 19.5 %all-to-all-start = ((f32[8,3,32,128]{3,2,1,0:T(8,128)}), f32[8,3,32,128]{3,2,1,0:T(8,128)S(1)}, u32[]{:S(2)}, u32[]{:S(2)}) async-start(f32[8,3,32,128]{3,2,1,0:T(8,128)} %get-tuple-element.50), calls=%async_computation | async-start | bytes 786432 | tf_op jit(solution)/shard_map/all_to_all | solution.py:641
  28.2 1.8 %collective-permute-start = (f32[8,64,128]{2,1,0:T(8,128)}, f32[8,64,128]{2,1,0:T(8,128)S(1)}, u32[]{:S(2)}, u32[]{:S(2)}) collective-permute-start(f32[8,64,128]{2,1,0:T(8,128)} %get-tuple-element.58), channel_id=1, source_target_pairs={{0,8},{8,0},{16,24},{24,16},{1,9},{9,1},{17,25},{25,17},{2,10},{10... | collective-permute-start | bytes 786440 | tf_op jit(solution)/shard_map/ppermute | solution.py:594
  28.3 1.6 %collective-permute-start.1 = (f32[64,128]{1,0:T(8,128)S(1)}, f32[64,128]{1,0:T(8,128)S(1)}, u32[]{:S(2)}, u32[]{:S(2)}) collective-permute-start(f32[64,128]{1,0:T(8,128)S(1)} %copy-done.4), channel_id=1, source_target_pairs={{0,8},{8,0},{16,24},{24,16},{1,9},{9,1},{17,25},{25,17},{2,10},{10... | collective-permute-start | bytes 98312 | tf_op jit(solution)/shard_map/ppermute | solution.py:594
  31.0 10.2 %collective-permute-start.2 = (f32[8,64,128]{2,1,0:T(8,128)S(1)}, f32[8,64,128]{2,1,0:T(8,128)S(1)}, u32[]{:S(2)}, u32[]{:S(2)}) collective-permute-start(f32[8,64,128]{2,1,0:T(8,128)S(1)} %multiply_add_fusion.3), channel_id=1, source_target_pairs={{0,16},{8,24},{1,17},{9,25},{2,18},{10,26},{3,19},{11,27},{4,20},{... | collective-permute-start | bytes 786440 | tf_op jit(solution)/shard_map/ppermute | solution.py:621
  35.2 21.9 %all-to-all-start.1 = ((f32[8,2,32,128]{3,2,1,0:T(8,128)}), f32[8,2,32,128]{3,2,1,0:T(8,128)S(1)}, u32[]{:S(2)}, u32[]{:S(2)}) async-start(f32[8,2,32,128]{3,2,1,0:T(8,128)} %shard_map.139), calls=%async_computation.1 | async-start | bytes 524288 | tf_op jit(solution)/shard_map/all_to_all | solution.py:657
  43.0 1.5 %collective-permute-start.3 = (f32[8,64,128]{2,1,0:T(8,128)S(1)}, f32[8,64,128]{2,1,0:T(8,128)S(1)}, u32[]{:S(2)}, u32[]{:S(2)}) collective-permute-start(f32[8,64,128]{2,1,0:T(8,128)S(1)} %get-tuple-element.95), channel_id=1, source_target_pairs={{0,8},{8,0},{16,24},{24,16},{1,9},{9,1},{17,25},{25,17},{2,10},{10... | collective-permute-start | bytes 786440 | tf_op jit(solution)/shard_map/ppermute | solution.py:594
  44.5 0.7 copy-start.6
  57.2 6.0 %copy-start.3 = (f32[8,2,32,128]{3,2,1,0:T(8,128)}, f32[8,2,32,128]{3,2,1,0:T(8,128)S(1)}, u32[]{:S(2)}) copy-start(f32[8,2,32,128]{3,2,1,0:T(8,128)S(1)} %all-to-all-done.1) | copy-start | bytes 786436
  57.2 17.8 %all-to-all-start.2 = ((f32[8,2,32,128]{3,2,1,0:T(8,128)}), f32[8,2,32,128]{3,2,1,0:T(8,128)S(1)}, u32[]{:S(2)}, u32[]{:S(2)}) async-start(f32[8,2,32,128]{3,2,1,0:T(8,128)} %bitcast.29), calls=%async_computation.2 | async-start | bytes 524288 | tf_op jit(solution)/shard_map/all_to_all | solution.py:641
  75.0 1.8 %collective-permute-start.4 = (f32[8,64,128]{2,1,0:T(8,128)}, f32[8,64,128]{2,1,0:T(8,128)S(1)}, u32[]{:S(2)}, u32[]{:S(2)}) collective-permute-start(f32[8,64,128]{2,1,0:T(8,128)} %get-tuple-element.79), channel_id=1, source_target_pairs={{0,8},{8,0},{16,24},{24,16},{1,9},{9,1},{17,25},{25,17},{2,10},{10... | collective-permute-start | bytes 786440 | tf_op jit(solution)/shard_map/ppermute | solution.py:594
  77.9 10.2 %collective-permute-start.5 = (f32[8,64,128]{2,1,0:T(8,128)S(1)}, f32[8,64,128]{2,1,0:T(8,128)S(1)}, u32[]{:S(2)}, u32[]{:S(2)}) collective-permute-start(f32[8,64,128]{2,1,0:T(8,128)S(1)} %multiply_add_fusion.1), channel_id=1, source_target_pairs={{16,0},{24,8},{17,1},{25,9},{18,2},{26,10},{19,3},{27,11},{20,4},{... | collective-permute-start | bytes 786440 | tf_op jit(solution)/shard_map/ppermute | solution.py:621
  79.9 15.2 %all-to-all-start.3 = ((f32[8,2,32,128]{3,2,1,0:T(8,128)}), f32[8,2,32,128]{3,2,1,0:T(8,128)S(1)}, u32[]{:S(2)}, u32[]{:S(2)}) async-start(f32[8,2,32,128]{3,2,1,0:T(8,128)} %shard_map.142), calls=%async_computation.3 | async-start | bytes 524288 | tf_op jit(solution)/shard_map/all_to_all | solution.py:657
  88.9 6.2 %collective-permute-start.6 = (f32[8,64,128]{2,1,0:T(8,128)S(1)}, f32[8,64,128]{2,1,0:T(8,128)S(1)}, u32[]{:S(2)}, u32[]{:S(2)}) collective-permute-start(f32[8,64,128]{2,1,0:T(8,128)S(1)} %get-tuple-element.93), channel_id=1, source_target_pairs={{0,8},{8,0},{16,24},{24,16},{1,9},{9,1},{17,25},{25,17},{2,10},{10... | collective-permute-start | bytes 786440 | tf_op jit(solution)/shard_map/ppermute | solution.py:594
  95.1 0.7 copy-start.2
  95.1 0.8 copy-start.5
  120.3 1.4 %collective-permute-start.7 = (f32[16,128]{1,0:T(8,128)}, f32[16,128]{1,0:T(8,128)S(1)}, u32[]{:S(2)}, u32[]{:S(2)}) collective-permute-start(f32[16,128]{1,0:T(8,128)} %get-tuple-element.92), channel_id=1, source_target_pairs={{0,8},{8,0},{16,24},{24,16},{1,9},{9,1},{17,25},{25,17},{2,10},{10... | collective-permute-start | bytes 24584 | tf_op jit(solution)/shard_map/ppermute | solution.py:664
  122.5 4.0 %collective-permute-start.8 = (f32[16,128]{1,0:T(8,128)S(1)}, f32[16,128]{1,0:T(8,128)S(1)}, u32[]{:S(2)}, u32[]{:S(2)}) collective-permute-start(f32[16,128]{1,0:T(8,128)S(1)} %add.36), channel_id=1, source_target_pairs={{0,16},{8,24},{16,0},{24,8},{1,17},{9,25},{17,1},{25,9},{2,18},{10... | collective-permute-start | bytes 24584 | tf_op jit(solution)/shard_map/ppermute | solution.py:664
  127.1 10.5 %all-to-all-start.4 = ((f32[8,16,128]{2,1,0:T(8,128)}), f32[8,16,128]{2,1,0:T(8,128)S(1)}, u32[]{:S(2)}, u32[]{:S(2)}) async-start(f32[8,16,128]{2,1,0:T(8,128)} %broadcast_in_dim.2), calls=%async_computation.4 | async-start | bytes 131072 | tf_op jit(solution)/shard_map/all_to_all | solution.py:666

commit v5 on v4

--- a/solution.py
+++ b/solution.py
@@ -171,6 +171,8 @@
               sum_cols, sum_rows, sent, turned, leaving):
         sum_cols[...] = jnp.zeros_like(sum_cols)
         leaving[...] = jnp.zeros_like(leaving)
+        for i in range(BI):
+            pack_rates(i, decay_log, rates, rates_v, rates_s)
 
     def lead(self, i, step, grad, read, decay_log, place, left, right,
              step_p, grad_p, rates, seg, read_p, rates_v, rates_s, own_rates, before_cols,
@@ -182,7 +184,6 @@
             grad_p[i * BJ + j] = gather_plane(grad, i, j)
             row_total = s if row_total is None else row_total + s
         gather_states(read, i, turned, read_p)
-        pack_rates(i, decay_log, rates, rates_v, rates_s)
         before_cols[i] = lane_dot_exact(row_total, left[...])
         places = lane_places(False, True)
         for q in range(STEPS):
@@ -659,11 +660,12 @@
 
 
 def total_of(x, rows, cols):
-    by = 1
-    while by < rows:
-        x = x + lax.ppermute(x, "row", [(k, k ^ by) for k in range(rows)])
-        by *= 2
-    parts = lax.all_to_all(jnp.broadcast_to(x[None], (cols,) + x.shape), "col", 0, 0)
+    terms = [x] + [
+        lax.ppermute(x, "row", [(k, k ^ by) for k in range(rows)]) for by in range(1, rows)
+    ]
+    while len(terms) > 1:
+        terms = [a + b for a, b in zip(terms[::2], terms[1::2])]
+    parts = lax.all_to_all(jnp.broadcast_to(terms[0][None], (cols,) + x.shape), "col", 0, 0)
     return jnp.sum(parts, 0)
 
 

time: 139 us -> 139 us (level)
    ppermute x2 -> x3, waiting for transfers between devices: 3 us -> 1.81 us  [total_of(): lax.ppermute(x, 'row', [(k, k ^ by) for k in range(rows)])]
  transfers between devices with their start and end apart: 14 -> 15, of which waited for: 9 -> 9; matrix products, arithmetic and copies ran while one was open for 3% -> 3% of each run, Pallas kernels for 28% -> 28%
where the time goes in v5:
time: 139 us; the launch traced here: 138 us
  Pallas kernels  73.7 us (53%)
  starting transfers between devices  38.2 us (27%)
  waiting for transfers between devices  17 us (12%)
  other arithmetic  5.93 us (4%)
  local copies, waits for them, and re-layouts  2.13 us (2%)
    pallas_call x6, Pallas kernels, run(): pl.pallas_call(kernel, out_shape=[jax.ShapeDtypeStruct(s, F32) for s, _ i...  72.2 us
    all_to_all x2, starting transfers between devices, col_gather(): return lax.all_to_all(sent, 'col', 0, 0)  13.4 us
    all_to_all x2, starting transfers between devices, col_return(): back = lax.all_to_all(carries, 'col', 0, 0)  12 us
    all_to_all x2, waiting for transfers between devices, col_return(): back = lax.all_to_all(carries, 'col', 0, 0)  5.99 us
    ppermute x2, starting transfers between devices, shift(): lax.ppermute(x, 'row', [(k, k + by) for k in range(size) if 0 <= k + by <...  4.74 us
    all_to_all x1, starting transfers between devices, total_of(): lax.all_to_all(jnp.broadcast_to(terms[0][None], (cols,) + x.shape), 'col'...  4.63 us
    ppermute x5, waiting for transfers between devices, swap_cores(): return lax.ppermute(x, 'row', [(k, k ^ 1) for k in range(size)])  4.49 us
  transfers between devices with their start and end apart: 15, of which 9 were waited for; matrix products, arithmetic and copies ran while one was open for 3% of the time, Pallas kernels for 28%

profile of v5, /device:TPU:0, one launch (start us, length us, event | category | flops | bytes accessed | tf_op | source)
XLA Modules:
  0.0 137.8 jit_solution(6075838744044162708)
XLA Ops:
  0.6 10.5 %shard_map.137 = (f32[16,128,128]{2,1,0:T(8,128)}, f32[16,128,128]{2,1,0:T(8,128)}, f32[16,128,128]{2,1,0:T(8,128)}, f32[16,4,128,128]{3,2,1,0:T(8,128)}, f32[16...) custom-call(f32[8,4,64,128]{3,2,1,0:T(8,128)} %bitcast.25, ...), custom_call_target="tpu_custom_call" | custom-call | bytes 16500000 | tf_op jit(solution)/shard_map/pallas_call | solution.py:579
  11.1 7.4 %all-to-all-start = ((f32[8,3,32,128]{3,2,1,0:T(8,128)}), f32[8,3,32,128]{3,2,1,0:T(8,128)S(1)}, u32[]{:S(2)}, u32[]{:S(2)}) async-start(f32[8,3,32,128]{3,2,1,0:T(8,128)} %get-tuple-element.50), calls=%async_computation | async-start | bytes 786432 | tf_op jit(solution)/shard_map/all_to_all | solution.py:642
  18.5 9.2 %shard_map.138 = (f32[16,128,128]{2,1,0:T(8,128)}, f32[16,4,128,128]{3,2,1,0:T(8,128)}, f32[16,16,128]{2,1,0:T(8,128)}, f32[4,128,128]{2,1,0:T(8,128)}, f32[8,64,128]{2,1,0:T(8,128)}, /*index=5*/f32[8,64,128]{2,1,0:T(8,128)}) custom-call(f32[8,4,64,128]{3,2,1,0:T(8,128)} %bitcast.27, f32[16,128,128]{2,1,0:T(8,128)} %get-tuple-element.51.refs_1_.refs_0_, ...), custom_call_target="tpu_custom_call" | custom-call | bytes 16500000 | tf_op jit(solution)/shard_map/pallas_call | solution.py:579
  27.7 0.1 collective-permute-start
  27.8 0.5 collective-permute-start.1
  28.3 1.1 collective-permute-done.1
  29.4 0.1 collective-permute-done
  29.5 1.0 multiply_add_fusion.3
  30.6 0.0 all-to-all-done.held.sums
  30.6 3.4 %collective-permute-start.2 = (f32[8,64,128]{2,1,0:T(8,128)S(1)}, f32[8,64,128]{2,1,0:T(8,128)S(1)}, u32[]{:S(2)}, u32[]{:S(2)}) collective-permute-start(f32[8,64,128]{2,1,0:T(8,128)S(1)} %multiply_add_fusion.3), channel_id=1, source_target_pairs={{0,16},{8,24},{1,17},{9,25},{2,18},{10,26},{3,19},{11,27},{4,20},{... | collective-permute-start | bytes 786440 | tf_op jit(solution)/shard_map/ppermute | solution.py:622
  34.0 0.7 shard_map.139
  34.8 6.0 %all-to-all-start.1 = ((f32[8,2,32,128]{3,2,1,0:T(8,128)}), f32[8,2,32,128]{3,2,1,0:T(8,128)S(1)}, u32[]{:S(2)}, u32[]{:S(2)}) async-start(f32[8,2,32,128]{3,2,1,0:T(8,128)} %shard_map.139), calls=%async_computation.1 | async-start | bytes 524288 | tf_op jit(solution)/shard_map/all_to_all | solution.py:658
  40.8 0.0 collective-permute-done.2
  40.8 1.8 %fusion = (f32[8,64,128]{2,1,0:T(8,128)S(1)}, f32[8,64,128]{2,1,0:T(8,128)}) fusion(f32[8,64,128]{2,1,0:T(8,128)S(1)} %collective-permute-done.2, f32[16,64,128]{2,1,0:T(8,128)S(1)} %copy-done.1, s32[]{:T(128)S(6)} %select_n.82, f32[64,128]{1,0:T(8,128)S(1)} %get-tuple-element.99, pred[]{:T(512)S(6)} %eq.14, f32[8,64,128]{2,1,0:T(8,128)} %get-tuple-element.59, ...), kind=kLoop, calls=%fused_computation.4 | loop fusion | flops 458752 | bytes 1605637 | tf_op jit(solution)/shard_map/jit(_where)/select_n | solution.py:637
  42.5 0.0 collective-permute-start.3
  42.5 1.5 %collective-permute-done.3.refs_5_ = f32[8,64,128]{2,1,0:T(8,128)S(1)} collective-permute-done((f32[8,64,128]{2,1,0:T(8,128)S(1)}, f32[8,64,128]{2,1,0:T(8,128)S(1)}, u32[]{:S(2)}, u32[]{:S(2)}) %collective-permute-start.3) | collective-permute-done | bytes 262176 | tf_op jit(solution)/shard_map/ppermute | solution.py:595
  44.1 0.7 copy-done.6
  44.8 11.9 %shard_map.140 = (f32[16,4,128,128]{3,2,1,0:T(8,128)}, f32[16,4,128,128]{3,2,1,0:T(8,128)}, f32[16,32,128]{2,1,0:T(8,128)}) custom-call(f32[16,128,128]{2,1,0:T(8,128)} %get-tuple-element.51.refs_1_.refs_0_, f32[16,128,128]{2,1,0:T(8,128)} %get-tuple-element.55.refs_1_, f32[16,128,128]{2,1,0:T(8,128)} %get-tuple-element.52.refs_2_.refs_3_, ...), custom_call_target="tpu_custom_call" | custom-call | bytes 33000000 | tf_op jit(solution)/shard_map/pallas_call | solution.py:579
  56.7 0.0 all-to-all-done.1
  56.7 6.0 %all-to-all-start.2 = ((f32[8,2,32,128]{3,2,1,0:T(8,128)}), f32[8,2,32,128]{3,2,1,0:T(8,128)S(1)}, u32[]{:S(2)}, u32[]{:S(2)}) async-start(f32[8,2,32,128]{3,2,1,0:T(8,128)} %bitcast.29), calls=%async_computation.2 | async-start | bytes 524288 | tf_op jit(solution)/shard_map/all_to_all | solution.py:642
  62.7 11.8 %shard_map.141 = (f32[16,4,128,128]{3,2,1,0:T(8,128)}, f32[16,4,128,128]{3,2,1,0:T(8,128)}, f32[8,64,128]{2,1,0:T(8,128)}, f32[8,64,128]{2,1,0:T(8,128)}) custom-call(f32[16,128,128]{2,1,0:T(8,128)} %get-tuple-element.51.refs_1_.refs_0_, f32[16,128,128]{2,1,0:T(8,128)} %get-tuple-element.56.refs_1_.refs_2_, ...), custom_call_target="tpu_custom_call" | custom-call | bytes 33000000 | tf_op jit(solution)/shard_map/pallas_call | solution.py:579
  74.6 0.0 all-to-all-done.2.held
  74.6 0.1 collective-permute-start.4
  74.7 1.7 %collective-permute-done.4 = f32[8,64,128]{2,1,0:T(8,128)S(1)} collective-permute-done((f32[8,64,128]{2,1,0:T(8,128)}, f32[8,64,128]{2,1,0:T(8,128)S(1)}, u32[]{:S(2)}, u32[]{:S(2)}) %collective-permute-start.4) | collective-permute-done | bytes 262176 | tf_op jit(solution)/shard_map/ppermute | solution.py:595
  76.4 1.0 multiply_add_fusion.1
  77.4 1.3 collective-permute-start.5
  78.7 0.7 shard_map.142
  79.5 6.0 %all-to-all-start.3 = ((f32[8,2,32,128]{3,2,1,0:T(8,128)}), f32[8,2,32,128]{3,2,1,0:T(8,128)S(1)}, u32[]{:S(2)}, u32[]{:S(2)}) async-start(f32[8,2,32,128]{3,2,1,0:T(8,128)} %shard_map.142), calls=%async_computation.3 | async-start | bytes 524288 | tf_op jit(solution)/shard_map/all_to_all | solution.py:658
  85.5 2.2 %collective-permute-done.5 = f32[8,64,128]{2,1,0:T(8,128)S(1)} collective-permute-done((f32[8,64,128]{2,1,0:T(8,128)S(1)}, f32[8,64,128]{2,1,0:T(8,128)S(1)}, u32[]{:S(2)}, u32[]{:S(2)}) %collective-permute-start.5) | collective-permute-done | bytes 262176 | tf_op jit(solution)/shard_map/ppermute | solution.py:622
  87.7 0.8 fusion.2
  88.5 0.3 collective-permute-start.6
  88.7 6.0 %all-to-all-done.3 = f32[8,2,32,128]{3,2,1,0:T(8,128)S(1)} async-done(((f32[8,2,32,128]{3,2,1,0:T(8,128)}), f32[8,2,32,128]{3,2,1,0:T(8,128)S(1)}, u32[]{:S(2)}, u32[]{:S(2)}) %all-to-all-start.3) | async-done | bytes 262176 | tf_op jit(solution)/shard_map/all_to_all | solution.py:658
  94.7 0.0 collective-permute-done.6.refs_10_
  94.7 0.7 copy-done.2
  95.4 0.1 copy-done.5
  95.5 24.4 %shard_map.143 = (f32[16,128,128]{2,1,0:T(8,128)}, f32[16,128,128]{2,1,0:T(8,128)}, f32[16,128,128]{2,1,0:T(8,128)}, f32[16,128,128]{2,1,0:T(8,128)}, f32[16,128]{1,0:T(8,128)}) custom-call(f32[16,128,128]{2,1,0:T(8,128)} %get-tuple-element.51.refs_1_.refs_0_, f32[16,128,128]{2,1,0:T(8,128)} %get-tuple-element.55.refs_1_, ...), custom_call_target="tpu_custom_call" | custom-call | bytes 82500000 | tf_op jit(solution)/shard_map/pallas_call | solution.py:579
  119.9 0.1 collective-permute-start.9
  120.0 2.4 %collective-permute-start.8 = (f32[16,128]{1,0:T(8,128)}, f32[16,128]{1,0:T(8,128)S(1)}, u32[]{:S(2)}, u32[]{:S(2)}) collective-permute-start(f32[16,128]{1,0:T(8,128)} %get-tuple-element.92), channel_id=1, source_target_pairs={{0,16},{8,24},{16,0},{24,8},{1,17},{9,25},{17,1},{25,9},{2,18},{10... | collective-permute-start | bytes 24584 | tf_op jit(solution)/shard_map/ppermute | solution.py:664
  122.4 0.0 collective-permute-start.7
  122.5 0.8 collective-permute-done.9
  123.3 1.0 collective-permute-done.8
  124.3 0.0 collective-permute-done.7
  124.3 0.7 add_add_fusion
  125.0 0.6 broadcast_in_dim.2
  125.6 4.6 %all-to-all-start.4 = ((f32[8,16,128]{2,1,0:T(8,128)}), f32[8,16,128]{2,1,0:T(8,128)S(1)}, u32[]{:S(2)}, u32[]{:S(2)}) async-start(f32[8,16,128]{2,1,0:T(8,128)} %broadcast_in_dim.2), calls=%async_computation.4 | async-start | bytes 131072 | tf_op jit(solution)/shard_map/all_to_all | solution.py:668
  130.2 4.4 %shard_map.144 = (f32[8,4,64,128]{3,2,1,0:T(8,128)}, f32[8,4,64,128]{3,2,1,0:T(8,128)}, f32[8,4,16,64]{3,2,1,0:T(8,128)}, f32[8,4,16,64]{3,2,1,0:T(8,128)}) custom-call(f32[16,128,128]{2,1,0:T(8,128)} %get-tuple-element.84.refs_0_, f32[16,128,128]{2,1,0:T(8,128)} %get-tuple-element.85.refs_1_, f32[16,128,128]{2,1,0:T(8,128)} %get-tuple-element.86.refs_2_, ...), custom_call_target="tpu_custom_call" | custom-call | bytes 16500000 | tf_op jit(solution)/shard_map/pallas_call | solution.py:579
  134.6 2.5 %all-to-all-done.4 = f32[8,16,128]{2,1,0:T(8,128)S(1)} async-done(((f32[8,16,128]{2,1,0:T(8,128)}), f32[8,16,128]{2,1,0:T(8,128)S(1)}, u32[]{:S(2)}, u32[]{:S(2)}) %all-to-all-start.4) | async-done | bytes 65568 | tf_op jit(solution)/shard_map/all_to_all | solution.py:668
  137.1 0.6 reduce_sum.9
  (12 shorter events, 0.0 us)
Async XLA Ops:
  11.1 16.7 %copy-start.4 = (f32[64,128]{1,0:T(8,128)S(1)}, f32[64,128]{1,0:T(8,128)}, u32[]{:S(2)}) copy-start(f32[64,128]{1,0:T(8,128)} %get-tuple-element.54.refs_5_.refs_16_) | copy-start | bytes 98308
  11.1 18.4 %copy-start.1 = (f32[16,64,128]{2,1,0:T(8,128)S(1)}, f32[16,64,128]{2,1,0:T(8,128)}, u32[]{:S(2)}) copy-start(f32[16,64,128]{2,1,0:T(8,128)} %get-tuple-element.53.refs_4_.refs_13_) | copy-start | bytes 1572868
  11.1 22.9 %copy-start = (f32[2,32,128]{2,1,0:T(8,128)S(1)}, f32[2,32,128]{2,1,0:T(8,128)}, u32[]{:S(2)}) copy-start(f32[2,32,128]{2,1,0:T(8,128)} %get-tuple-element.62.rates) | copy-start | bytes 98308
  11.1 19.4 %all-to-all-start = ((f32[8,3,32,128]{3,2,1,0:T(8,128)}), f32[8,3,32,128]{3,2,1,0:T(8,128)S(1)}, u32[]{:S(2)}, u32[]{:S(2)}) async-start(f32[8,3,32,128]{3,2,1,0:T(8,128)} %get-tuple-element.50), calls=%async_computation | async-start | bytes 786432 | tf_op jit(solution)/shard_map/all_to_all | solution.py:642
  27.7 1.8 %collective-permute-start = (f32[8,64,128]{2,1,0:T(8,128)}, f32[8,64,128]{2,1,0:T(8,128)S(1)}, u32[]{:S(2)}, u32[]{:S(2)}) collective-permute-start(f32[8,64,128]{2,1,0:T(8,128)} %get-tuple-element.58), channel_id=1, source_target_pairs={{0,8},{8,0},{16,24},{24,16},{1,9},{9,1},{17,25},{25,17},{2,10},{10... | collective-permute-start | bytes 786440 | tf_op jit(solution)/shard_map/ppermute | solution.py:595
  27.8 1.6 %collective-permute-start.1 = (f32[64,128]{1,0:T(8,128)S(1)}, f32[64,128]{1,0:T(8,128)S(1)}, u32[]{:S(2)}, u32[]{:S(2)}) collective-permute-start(f32[64,128]{1,0:T(8,128)S(1)} %copy-done.4), channel_id=1, source_target_pairs={{0,8},{8,0},{16,24},{24,16},{1,9},{9,1},{17,25},{25,17},{2,10},{10... | collective-permute-start | bytes 98312 | tf_op jit(solution)/shard_map/ppermute | solution.py:595
  30.6 10.2 %collective-permute-start.2 = (f32[8,64,128]{2,1,0:T(8,128)S(1)}, f32[8,64,128]{2,1,0:T(8,128)S(1)}, u32[]{:S(2)}, u32[]{:S(2)}) collective-permute-start(f32[8,64,128]{2,1,0:T(8,128)S(1)} %multiply_add_fusion.3), channel_id=1, source_target_pairs={{0,16},{8,24},{1,17},{9,25},{2,18},{10,26},{3,19},{11,27},{4,20},{... | collective-permute-start | bytes 786440 | tf_op jit(solution)/shard_map/ppermute | solution.py:622
  34.8 21.9 %all-to-all-start.1 = ((f32[8,2,32,128]{3,2,1,0:T(8,128)}), f32[8,2,32,128]{3,2,1,0:T(8,128)S(1)}, u32[]{:S(2)}, u32[]{:S(2)}) async-start(f32[8,2,32,128]{3,2,1,0:T(8,128)} %shard_map.139), calls=%async_computation.1 | async-start | bytes 524288 | tf_op jit(solution)/shard_map/all_to_all | solution.py:658
  42.5 1.5 %collective-permute-start.3 = (f32[8,64,128]{2,1,0:T(8,128)S(1)}, f32[8,64,128]{2,1,0:T(8,128)S(1)}, u32[]{:S(2)}, u32[]{:S(2)}) collective-permute-start(f32[8,64,128]{2,1,0:T(8,128)S(1)} %get-tuple-element.95), channel_id=1, source_target_pairs={{0,8},{8,0},{16,24},{24,16},{1,9},{9,1},{17,25},{25,17},{2,10},{10... | collective-permute-start | bytes 786440 | tf_op jit(solution)/shard_map/ppermute | solution.py:595
  44.1 0.7 copy-start.6
  56.7 6.0 %copy-start.3 = (f32[8,2,32,128]{3,2,1,0:T(8,128)}, f32[8,2,32,128]{3,2,1,0:T(8,128)S(1)}, u32[]{:S(2)}) copy-start(f32[8,2,32,128]{3,2,1,0:T(8,128)S(1)} %all-to-all-done.1) | copy-start | bytes 786436
  56.7 17.9 %all-to-all-start.2 = ((f32[8,2,32,128]{3,2,1,0:T(8,128)}), f32[8,2,32,128]{3,2,1,0:T(8,128)S(1)}, u32[]{:S(2)}, u32[]{:S(2)}) async-start(f32[8,2,32,128]{3,2,1,0:T(8,128)} %bitcast.29), calls=%async_computation.2 | async-start | bytes 524288 | tf_op jit(solution)/shard_map/all_to_all | solution.py:642
  74.6 1.8 %collective-permute-start.4 = (f32[8,64,128]{2,1,0:T(8,128)}, f32[8,64,128]{2,1,0:T(8,128)S(1)}, u32[]{:S(2)}, u32[]{:S(2)}) collective-permute-start(f32[8,64,128]{2,1,0:T(8,128)} %get-tuple-element.79), channel_id=1, source_target_pairs={{0,8},{8,0},{16,24},{24,16},{1,9},{9,1},{17,25},{25,17},{2,10},{10... | collective-permute-start | bytes 786440 | tf_op jit(solution)/shard_map/ppermute | solution.py:595
  77.4 10.2 %collective-permute-start.5 = (f32[8,64,128]{2,1,0:T(8,128)S(1)}, f32[8,64,128]{2,1,0:T(8,128)S(1)}, u32[]{:S(2)}, u32[]{:S(2)}) collective-permute-start(f32[8,64,128]{2,1,0:T(8,128)S(1)} %multiply_add_fusion.1), channel_id=1, source_target_pairs={{16,0},{24,8},{17,1},{25,9},{18,2},{26,10},{19,3},{27,11},{20,4},{... | collective-permute-start | bytes 786440 | tf_op jit(solution)/shard_map/ppermute | solution.py:622
  79.5 15.2 %all-to-all-start.3 = ((f32[8,2,32,128]{3,2,1,0:T(8,128)}), f32[8,2,32,128]{3,2,1,0:T(8,128)S(1)}, u32[]{:S(2)}, u32[]{:S(2)}) async-start(f32[8,2,32,128]{3,2,1,0:T(8,128)} %shard_map.142), calls=%async_computation.3 | async-start | bytes 524288 | tf_op jit(solution)/shard_map/all_to_all | solution.py:658
  88.5 6.3 %collective-permute-start.6 = (f32[8,64,128]{2,1,0:T(8,128)S(1)}, f32[8,64,128]{2,1,0:T(8,128)S(1)}, u32[]{:S(2)}, u32[]{:S(2)}) collective-permute-start(f32[8,64,128]{2,1,0:T(8,128)S(1)} %get-tuple-element.93), channel_id=1, source_target_pairs={{0,8},{8,0},{16,24},{24,16},{1,9},{9,1},{17,25},{25,17},{2,10},{10... | collective-permute-start | bytes 786440 | tf_op jit(solution)/shard_map/ppermute | solution.py:595
  94.7 0.7 copy-start.2
  94.7 0.8 copy-start.5
  119.9 3.4 %collective-permute-start.9 = (f32[16,128]{1,0:T(8,128)}, f32[16,128]{1,0:T(8,128)S(1)}, u32[]{:S(2)}, u32[]{:S(2)}) collective-permute-start(f32[16,128]{1,0:T(8,128)} %get-tuple-element.92), channel_id=1, source_target_pairs={{0,24},{8,16},{16,8},{24,0},{1,25},{9,17},{17,9},{25,1},{2,26},{10... | collective-permute-start | bytes 24584 | tf_op jit(solution)/shard_map/ppermute | solution.py:664
  120.0 4.3 %collective-permute-start.8 = (f32[16,128]{1,0:T(8,128)}, f32[16,128]{1,0:T(8,128)S(1)}, u32[]{:S(2)}, u32[]{:S(2)}) collective-permute-start(f32[16,128]{1,0:T(8,128)} %get-tuple-element.92), channel_id=1, source_target_pairs={{0,16},{8,24},{16,0},{24,8},{1,17},{9,25},{17,1},{25,9},{2,18},{10... | collective-permute-start | bytes 24584 | tf_op jit(solution)/shard_map/ppermute | solution.py:664
  122.4 1.9 %collective-permute-start.7 = (f32[16,128]{1,0:T(8,128)}, f32[16,128]{1,0:T(8,128)S(1)}, u32[]{:S(2)}, u32[]{:S(2)}) collective-permute-start(f32[16,128]{1,0:T(8,128)} %get-tuple-element.92), channel_id=1, source_target_pairs={{0,8},{8,0},{16,24},{24,16},{1,9},{9,1},{17,25},{25,17},{2,10},{10... | collective-permute-start | bytes 24584 | tf_op jit(solution)/shard_map/ppermute | solution.py:664
  125.6 11.5 %all-to-all-start.4 = ((f32[8,16,128]{2,1,0:T(8,128)}), f32[8,16,128]{2,1,0:T(8,128)S(1)}, u32[]{:S(2)}, u32[]{:S(2)}) async-start(f32[8,16,128]{2,1,0:T(8,128)} %broadcast_in_dim.2), calls=%async_computation.4 | async-start | bytes 131072 | tf_op jit(solution)/shard_map/all_to_all | solution.py:668

commit v6 on v5

--- a/solution.py
+++ b/solution.py
@@ -319,6 +319,9 @@
                     seg[n, i, d] = state[k] * jnp.exp2(-r[k] * after)
 
         each_group(b, states, 8, group)
+
+    def after(self, b, step_p, source_p, rates, seg_rows, keep, got, write_p, rates_s, before_rows,
+             before_cols, sum_cols, core, left, start_rows, seg, leaving, entering):
         send(b, seg, left, leaving, False)
 
     def last(self, step_p, source_p, rates, seg_rows, keep, got, write_p, rates_s, before_rows,
@@ -369,6 +372,10 @@
                     seg[n, j, d] = passed_v[k][j] * jnp.exp2(r[k] * before)
 
         each_group(b, states, 8, group)
+
+    def after(self, b, step_p, grad_p, rates, seg_cols, entering, read_p, rates_s, before_rows,
+             before_cols, sum_cols, core, below, start_cols, seg, keep, give,
+             scaled, leaving):
         send(b, seg, below, leaving, True)
 
     def last(self, step_p, grad_p, rates, seg_cols, entering, read_p, rates_s, before_rows,
@@ -542,7 +549,12 @@
                 for copy in into[which]:
                     copy(k).wait()
                 getattr(stage, name)(k, *views, *extra)
-                for copy in out_of[which]:
+                early = 1 if hasattr(stage, "after") else 0
+                for copy in out_of[which][:early]:
+                    copy(k).start()
+                if early:
+                    stage.after(k, *views, *extra)
+                for copy in out_of[which][early:]:
                     copy(k).start()
                 return carry
 

time: 139 us -> 139 us (level)
  no operation moved by 1% of the time
where the time goes in v6:
time: 139 us; the launch traced here: 138 us
  Pallas kernels  73.7 us (53%)
  starting transfers between devices  38.2 us (27%)
  waiting for transfers between devices  17 us (12%)
  other arithmetic  5.93 us (4%)
  local copies, waits for them, and re-layouts  2.13 us (2%)
    pallas_call x6, Pallas kernels, run(): pl.pallas_call(kernel, out_shape=[jax.ShapeDtypeStruct(s, F32) for s, _ i...  72.2 us
    all_to_all x2, starting transfers between devices, col_gather(): return lax.all_to_all(sent, 'col', 0, 0)  13.4 us
    all_to_all x2, starting transfers between devices, col_return(): back = lax.all_to_all(carries, 'col', 0, 0)  12 us
    all_to_all x2, waiting for transfers between devices, col_return(): back = lax.all_to_all(carries, 'col', 0, 0)  5.99 us
    ppermute x2, starting transfers between devices, shift(): lax.ppermute(x, 'row', [(k, k + by) for k in range(size) if 0 <= k + by <...  4.74 us
    all_to_all x1, starting transfers between devices, total_of(): lax.all_to_all(jnp.broadcast_to(terms[0][None], (cols,) + x.shape), 'col'...  4.63 us
    ppermute x5, waiting for transfers between devices, swap_cores(): return lax.ppermute(x, 'row', [(k, k ^ 1) for k in range(size)])  4.49 us
  transfers between devices with their start and end apart: 15, of which 9 were waited for; matrix products, arithmetic and copies ran while one was open for 3% of the time, Pallas kernels for 28%

profile of v6, /device:TPU:0, one launch (start us, length us, event | category | flops | bytes accessed | tf_op | source)
XLA Modules:
  0.0 137.8 jit_solution(6075838744044162708)
XLA Ops:
  0.6 10.5 %shard_map.137 = (f32[16,128,128]{2,1,0:T(8,128)}, f32[16,128,128]{2,1,0:T(8,128)}, f32[16,128,128]{2,1,0:T(8,128)}, f32[16,4,128,128]{3,2,1,0:T(8,128)}, f32[16...) custom-call(f32[8,4,64,128]{3,2,1,0:T(8,128)} %bitcast.25, ...), custom_call_target="tpu_custom_call" | custom-call | bytes 16500000 | tf_op jit(solution)/shard_map/pallas_call | solution.py:591
  11.1 7.4 %all-to-all-start = ((f32[8,3,32,128]{3,2,1,0:T(8,128)}), f32[8,3,32,128]{3,2,1,0:T(8,128)S(1)}, u32[]{:S(2)}, u32[]{:S(2)}) async-start(f32[8,3,32,128]{3,2,1,0:T(8,128)} %get-tuple-element.50), calls=%async_computation | async-start | bytes 786432 | tf_op jit(solution)/shard_map/all_to_all | solution.py:654
  18.5 9.2 %shard_map.138 = (f32[16,128,128]{2,1,0:T(8,128)}, f32[16,4,128,128]{3,2,1,0:T(8,128)}, f32[16,16,128]{2,1,0:T(8,128)}, f32[4,128,128]{2,1,0:T(8,128)}, f32[8,64,128]{2,1,0:T(8,128)}, /*index=5*/f32[8,64,128]{2,1,0:T(8,128)}) custom-call(f32[8,4,64,128]{3,2,1,0:T(8,128)} %bitcast.27, f32[16,128,128]{2,1,0:T(8,128)} %get-tuple-element.51.refs_1_.refs_0_, ...), custom_call_target="tpu_custom_call" | custom-call | bytes 16500000 | tf_op jit(solution)/shard_map/pallas_call | solution.py:591
  27.7 0.1 collective-permute-start
  27.8 0.5 collective-permute-start.1
  28.3 1.1 collective-permute-done.1
  29.4 0.1 collective-permute-done
  29.5 1.0 multiply_add_fusion.3
  30.6 0.0 all-to-all-done.held.sums
  30.6 3.4 %collective-permute-start.2 = (f32[8,64,128]{2,1,0:T(8,128)S(1)}, f32[8,64,128]{2,1,0:T(8,128)S(1)}, u32[]{:S(2)}, u32[]{:S(2)}) collective-permute-start(f32[8,64,128]{2,1,0:T(8,128)S(1)} %multiply_add_fusion.3), channel_id=1, source_target_pairs={{0,16},{8,24},{1,17},{9,25},{2,18},{10,26},{3,19},{11,27},{4,20},{... | collective-permute-start | bytes 786440 | tf_op jit(solution)/shard_map/ppermute | solution.py:634
  34.0 0.7 shard_map.139
  34.8 6.0 %all-to-all-start.1 = ((f32[8,2,32,128]{3,2,1,0:T(8,128)}), f32[8,2,32,128]{3,2,1,0:T(8,128)S(1)}, u32[]{:S(2)}, u32[]{:S(2)}) async-start(f32[8,2,32,128]{3,2,1,0:T(8,128)} %shard_map.139), calls=%async_computation.1 | async-start | bytes 524288 | tf_op jit(solution)/shard_map/all_to_all | solution.py:670
  40.8 0.0 collective-permute-done.2
  40.8 1.8 %fusion = (f32[8,64,128]{2,1,0:T(8,128)S(1)}, f32[8,64,128]{2,1,0:T(8,128)}) fusion(f32[8,64,128]{2,1,0:T(8,128)S(1)} %collective-permute-done.2, f32[16,64,128]{2,1,0:T(8,128)S(1)} %copy-done.1, s32[]{:T(128)S(6)} %select_n.82, f32[64,128]{1,0:T(8,128)S(1)} %get-tuple-element.99, pred[]{:T(512)S(6)} %eq.14, f32[8,64,128]{2,1,0:T(8,128)} %get-tuple-element.59, ...), kind=kLoop, calls=%fused_computation.4 | loop fusion | flops 458752 | bytes 1605637 | tf_op jit(solution)/shard_map/jit(_where)/select_n | solution.py:649
  42.5 0.0 collective-permute-start.3
  42.5 1.5 %collective-permute-done.3.refs_5_ = f32[8,64,128]{2,1,0:T(8,128)S(1)} collective-permute-done((f32[8,64,128]{2,1,0:T(8,128)S(1)}, f32[8,64,128]{2,1,0:T(8,128)S(1)}, u32[]{:S(2)}, u32[]{:S(2)}) %collective-permute-start.3) | collective-permute-done | bytes 262176 | tf_op jit(solution)/shard_map/ppermute | solution.py:607
  44.1 0.7 copy-done.6
  44.8 11.9 %shard_map.140 = (f32[16,4,128,128]{3,2,1,0:T(8,128)}, f32[16,4,128,128]{3,2,1,0:T(8,128)}, f32[16,32,128]{2,1,0:T(8,128)}) custom-call(f32[16,128,128]{2,1,0:T(8,128)} %get-tuple-element.51.refs_1_.refs_0_, f32[16,128,128]{2,1,0:T(8,128)} %get-tuple-element.55.refs_1_, f32[16,128,128]{2,1,0:T(8,128)} %get-tuple-element.52.refs_2_.refs_3_, ...), custom_call_target="tpu_custom_call" | custom-call | bytes 33000000 | tf_op jit(solution)/shard_map/pallas_call | solution.py:591
  56.7 0.0 all-to-all-done.1
  56.7 6.0 %all-to-all-start.2 = ((f32[8,2,32,128]{3,2,1,0:T(8,128)}), f32[8,2,32,128]{3,2,1,0:T(8,128)S(1)}, u32[]{:S(2)}, u32[]{:S(2)}) async-start(f32[8,2,32,128]{3,2,1,0:T(8,128)} %bitcast.29), calls=%async_computation.2 | async-start | bytes 524288 | tf_op jit(solution)/shard_map/all_to_all | solution.py:654
  62.7 11.8 %shard_map.141 = (f32[16,4,128,128]{3,2,1,0:T(8,128)}, f32[16,4,128,128]{3,2,1,0:T(8,128)}, f32[8,64,128]{2,1,0:T(8,128)}, f32[8,64,128]{2,1,0:T(8,128)}) custom-call(f32[16,128,128]{2,1,0:T(8,128)} %get-tuple-element.51.refs_1_.refs_0_, f32[16,128,128]{2,1,0:T(8,128)} %get-tuple-element.56.refs_1_.refs_2_, ...), custom_call_target="tpu_custom_call" | custom-call | bytes 33000000 | tf_op jit(solution)/shard_map/pallas_call | solution.py:591
  74.6 0.0 all-to-all-done.2.held
  74.6 0.1 collective-permute-start.4
  74.7 1.7 %collective-permute-done.4 = f32[8,64,128]{2,1,0:T(8,128)S(1)} collective-permute-done((f32[8,64,128]{2,1,0:T(8,128)}, f32[8,64,128]{2,1,0:T(8,128)S(1)}, u32[]{:S(2)}, u32[]{:S(2)}) %collective-permute-start.4) | collective-permute-done | bytes 262176 | tf_op jit(solution)/shard_map/ppermute | solution.py:607
  76.4 1.0 multiply_add_fusion.1
  77.4 1.3 collective-permute-start.5
  78.7 0.7 shard_map.142
  79.5 6.0 %all-to-all-start.3 = ((f32[8,2,32,128]{3,2,1,0:T(8,128)}), f32[8,2,32,128]{3,2,1,0:T(8,128)S(1)}, u32[]{:S(2)}, u32[]{:S(2)}) async-start(f32[8,2,32,128]{3,2,1,0:T(8,128)} %shard_map.142), calls=%async_computation.3 | async-start | bytes 524288 | tf_op jit(solution)/shard_map/all_to_all | solution.py:670
  85.5 2.2 %collective-permute-done.5 = f32[8,64,128]{2,1,0:T(8,128)S(1)} collective-permute-done((f32[8,64,128]{2,1,0:T(8,128)S(1)}, f32[8,64,128]{2,1,0:T(8,128)S(1)}, u32[]{:S(2)}, u32[]{:S(2)}) %collective-permute-start.5) | collective-permute-done | bytes 262176 | tf_op jit(solution)/shard_map/ppermute | solution.py:634
  87.7 0.8 fusion.2
  88.5 0.3 collective-permute-start.6
  88.7 6.0 %all-to-all-done.3 = f32[8,2,32,128]{3,2,1,0:T(8,128)S(1)} async-done(((f32[8,2,32,128]{3,2,1,0:T(8,128)}), f32[8,2,32,128]{3,2,1,0:T(8,128)S(1)}, u32[]{:S(2)}, u32[]{:S(2)}) %all-to-all-start.3) | async-done | bytes 262176 | tf_op jit(solution)/shard_map/all_to_all | solution.py:670
  94.7 0.0 collective-permute-done.6.refs_10_
  94.7 0.7 copy-done.2
  95.4 0.1 copy-done.5
  95.5 24.4 %shard_map.143 = (f32[16,128,128]{2,1,0:T(8,128)}, f32[16,128,128]{2,1,0:T(8,128)}, f32[16,128,128]{2,1,0:T(8,128)}, f32[16,128,128]{2,1,0:T(8,128)}, f32[16,128]{1,0:T(8,128)}) custom-call(f32[16,128,128]{2,1,0:T(8,128)} %get-tuple-element.51.refs_1_.refs_0_, f32[16,128,128]{2,1,0:T(8,128)} %get-tuple-element.55.refs_1_, ...), custom_call_target="tpu_custom_call" | custom-call | bytes 82500000 | tf_op jit(solution)/shard_map/pallas_call | solution.py:591
  119.9 0.1 collective-permute-start.9
  120.0 2.4 %collective-permute-start.8 = (f32[16,128]{1,0:T(8,128)}, f32[16,128]{1,0:T(8,128)S(1)}, u32[]{:S(2)}, u32[]{:S(2)}) collective-permute-start(f32[16,128]{1,0:T(8,128)} %get-tuple-element.92), channel_id=1, source_target_pairs={{0,16},{8,24},{16,0},{24,8},{1,17},{9,25},{17,1},{25,9},{2,18},{10... | collective-permute-start | bytes 24584 | tf_op jit(solution)/shard_map/ppermute | solution.py:676
  122.4 0.0 collective-permute-start.7
  122.5 0.8 collective-permute-done.9
  123.3 1.0 collective-permute-done.8
  124.3 0.0 collective-permute-done.7
  124.3 0.7 add_add_fusion
  125.0 0.6 broadcast_in_dim.2
  125.6 4.6 %all-to-all-start.4 = ((f32[8,16,128]{2,1,0:T(8,128)}), f32[8,16,128]{2,1,0:T(8,128)S(1)}, u32[]{:S(2)}, u32[]{:S(2)}) async-start(f32[8,16,128]{2,1,0:T(8,128)} %broadcast_in_dim.2), calls=%async_computation.4 | async-start | bytes 131072 | tf_op jit(solution)/shard_map/all_to_all | solution.py:680
  130.2 4.4 %shard_map.144 = (f32[8,4,64,128]{3,2,1,0:T(8,128)}, f32[8,4,64,128]{3,2,1,0:T(8,128)}, f32[8,4,16,64]{3,2,1,0:T(8,128)}, f32[8,4,16,64]{3,2,1,0:T(8,128)}) custom-call(f32[16,128,128]{2,1,0:T(8,128)} %get-tuple-element.84.refs_0_, f32[16,128,128]{2,1,0:T(8,128)} %get-tuple-element.85.refs_1_, f32[16,128,128]{2,1,0:T(8,128)} %get-tuple-element.86.refs_2_, ...), custom_call_target="tpu_custom_call" | custom-call | bytes 16500000 | tf_op jit(solution)/shard_map/pallas_call | solution.py:591
  134.6 2.5 %all-to-all-done.4 = f32[8,16,128]{2,1,0:T(8,128)S(1)} async-done(((f32[8,16,128]{2,1,0:T(8,128)}), f32[8,16,128]{2,1,0:T(8,128)S(1)}, u32[]{:S(2)}, u32[]{:S(2)}) %all-to-all-start.4) | async-done | bytes 65568 | tf_op jit(solution)/shard_map/all_to_all | solution.py:680
  137.1 0.6 reduce_sum.9
  (12 shorter events, 0.0 us)
Async XLA Ops:
  11.1 16.7 %copy-start.4 = (f32[64,128]{1,0:T(8,128)S(1)}, f32[64,128]{1,0:T(8,128)}, u32[]{:S(2)}) copy-start(f32[64,128]{1,0:T(8,128)} %get-tuple-element.54.refs_5_.refs_16_) | copy-start | bytes 98308
  11.1 18.4 %copy-start.1 = (f32[16,64,128]{2,1,0:T(8,128)S(1)}, f32[16,64,128]{2,1,0:T(8,128)}, u32[]{:S(2)}) copy-start(f32[16,64,128]{2,1,0:T(8,128)} %get-tuple-element.53.refs_4_.refs_13_) | copy-start | bytes 1572868
  11.1 22.9 %copy-start = (f32[2,32,128]{2,1,0:T(8,128)S(1)}, f32[2,32,128]{2,1,0:T(8,128)}, u32[]{:S(2)}) copy-start(f32[2,32,128]{2,1,0:T(8,128)} %get-tuple-element.62.rates) | copy-start | bytes 98308
  11.1 19.4 %all-to-all-start = ((f32[8,3,32,128]{3,2,1,0:T(8,128)}), f32[8,3,32,128]{3,2,1,0:T(8,128)S(1)}, u32[]{:S(2)}, u32[]{:S(2)}) async-start(f32[8,3,32,128]{3,2,1,0:T(8,128)} %get-tuple-element.50), calls=%async_computation | async-start | bytes 786432 | tf_op jit(solution)/shard_map/all_to_all | solution.py:654
  27.7 1.8 %collective-permute-start = (f32[8,64,128]{2,1,0:T(8,128)}, f32[8,64,128]{2,1,0:T(8,128)S(1)}, u32[]{:S(2)}, u32[]{:S(2)}) collective-permute-start(f32[8,64,128]{2,1,0:T(8,128)} %get-tuple-element.58), channel_id=1, source_target_pairs={{0,8},{8,0},{16,24},{24,16},{1,9},{9,1},{17,25},{25,17},{2,10},{10... | collective-permute-start | bytes 786440 | tf_op jit(solution)/shard_map/ppermute | solution.py:607
  27.8 1.6 %collective-permute-start.1 = (f32[64,128]{1,0:T(8,128)S(1)}, f32[64,128]{1,0:T(8,128)S(1)}, u32[]{:S(2)}, u32[]{:S(2)}) collective-permute-start(f32[64,128]{1,0:T(8,128)S(1)} %copy-done.4), channel_id=1, source_target_pairs={{0,8},{8,0},{16,24},{24,16},{1,9},{9,1},{17,25},{25,17},{2,10},{10... | collective-permute-start | bytes 98312 | tf_op jit(solution)/shard_map/ppermute | solution.py:607
  30.6 10.2 %collective-permute-start.2 = (f32[8,64,128]{2,1,0:T(8,128)S(1)}, f32[8,64,128]{2,1,0:T(8,128)S(1)}, u32[]{:S(2)}, u32[]{:S(2)}) collective-permute-start(f32[8,64,128]{2,1,0:T(8,128)S(1)} %multiply_add_fusion.3), channel_id=1, source_target_pairs={{0,16},{8,24},{1,17},{9,25},{2,18},{10,26},{3,19},{11,27},{4,20},{... | collective-permute-start | bytes 786440 | tf_op jit(solution)/shard_map/ppermute | solution.py:634
  34.8 21.9 %all-to-all-start.1 = ((f32[8,2,32,128]{3,2,1,0:T(8,128)}), f32[8,2,32,128]{3,2,1,0:T(8,128)S(1)}, u32[]{:S(2)}, u32[]{:S(2)}) async-start(f32[8,2,32,128]{3,2,1,0:T(8,128)} %shard_map.139), calls=%async_computation.1 | async-start | bytes 524288 | tf_op jit(solution)/shard_map/all_to_all | solution.py:670
  42.5 1.5 %collective-permute-start.3 = (f32[8,64,128]{2,1,0:T(8,128)S(1)}, f32[8,64,128]{2,1,0:T(8,128)S(1)}, u32[]{:S(2)}, u32[]{:S(2)}) collective-permute-start(f32[8,64,128]{2,1,0:T(8,128)S(1)} %get-tuple-element.95), channel_id=1, source_target_pairs={{0,8},{8,0},{16,24},{24,16},{1,9},{9,1},{17,25},{25,17},{2,10},{10... | collective-permute-start | bytes 786440 | tf_op jit(solution)/shard_map/ppermute | solution.py:607
  44.1 0.7 copy-start.6
  56.7 6.0 %copy-start.3 = (f32[8,2,32,128]{3,2,1,0:T(8,128)}, f32[8,2,32,128]{3,2,1,0:T(8,128)S(1)}, u32[]{:S(2)}) copy-start(f32[8,2,32,128]{3,2,1,0:T(8,128)S(1)} %all-to-all-done.1) | copy-start | bytes 786436
  56.7 17.9 %all-to-all-start.2 = ((f32[8,2,32,128]{3,2,1,0:T(8,128)}), f32[8,2,32,128]{3,2,1,0:T(8,128)S(1)}, u32[]{:S(2)}, u32[]{:S(2)}) async-start(f32[8,2,32,128]{3,2,1,0:T(8,128)} %bitcast.29), calls=%async_computation.2 | async-start | bytes 524288 | tf_op jit(solution)/shard_map/all_to_all | solution.py:654
  74.6 1.8 %collective-permute-start.4 = (f32[8,64,128]{2,1,0:T(8,128)}, f32[8,64,128]{2,1,0:T(8,128)S(1)}, u32[]{:S(2)}, u32[]{:S(2)}) collective-permute-start(f32[8,64,128]{2,1,0:T(8,128)} %get-tuple-element.79), channel_id=1, source_target_pairs={{0,8},{8,0},{16,24},{24,16},{1,9},{9,1},{17,25},{25,17},{2,10},{10... | collective-permute-start | bytes 786440 | tf_op jit(solution)/shard_map/ppermute | solution.py:607
  77.4 10.2 %collective-permute-start.5 = (f32[8,64,128]{2,1,0:T(8,128)S(1)}, f32[8,64,128]{2,1,0:T(8,128)S(1)}, u32[]{:S(2)}, u32[]{:S(2)}) collective-permute-start(f32[8,64,128]{2,1,0:T(8,128)S(1)} %multiply_add_fusion.1), channel_id=1, source_target_pairs={{16,0},{24,8},{17,1},{25,9},{18,2},{26,10},{19,3},{27,11},{20,4},{... | collective-permute-start | bytes 786440 | tf_op jit(solution)/shard_map/ppermute | solution.py:634
  79.5 15.2 %all-to-all-start.3 = ((f32[8,2,32,128]{3,2,1,0:T(8,128)}), f32[8,2,32,128]{3,2,1,0:T(8,128)S(1)}, u32[]{:S(2)}, u32[]{:S(2)}) async-start(f32[8,2,32,128]{3,2,1,0:T(8,128)} %shard_map.142), calls=%async_computation.3 | async-start | bytes 524288 | tf_op jit(solution)/shard_map/all_to_all | solution.py:670
  88.5 6.3 %collective-permute-start.6 = (f32[8,64,128]{2,1,0:T(8,128)S(1)}, f32[8,64,128]{2,1,0:T(8,128)S(1)}, u32[]{:S(2)}, u32[]{:S(2)}) collective-permute-start(f32[8,64,128]{2,1,0:T(8,128)S(1)} %get-tuple-element.93), channel_id=1, source_target_pairs={{0,8},{8,0},{16,24},{24,16},{1,9},{9,1},{17,25},{25,17},{2,10},{10... | collective-permute-start | bytes 786440 | tf_op jit(solution)/shard_map/ppermute | solution.py:607
  94.7 0.7 copy-start.2
  94.7 0.8 copy-start.5
  119.9 3.4 %collective-permute-start.9 = (f32[16,128]{1,0:T(8,128)}, f32[16,128]{1,0:T(8,128)S(1)}, u32[]{:S(2)}, u32[]{:S(2)}) collective-permute-start(f32[16,128]{1,0:T(8,128)} %get-tuple-element.92), channel_id=1, source_target_pairs={{0,24},{8,16},{16,8},{24,0},{1,25},{9,17},{17,9},{25,1},{2,26},{10... | collective-permute-start | bytes 24584 | tf_op jit(solution)/shard_map/ppermute | solution.py:676
  120.0 4.3 %collective-permute-start.8 = (f32[16,128]{1,0:T(8,128)}, f32[16,128]{1,0:T(8,128)S(1)}, u32[]{:S(2)}, u32[]{:S(2)}) collective-permute-start(f32[16,128]{1,0:T(8,128)} %get-tuple-element.92), channel_id=1, source_target_pairs={{0,16},{8,24},{16,0},{24,8},{1,17},{9,25},{17,1},{25,9},{2,18},{10... | collective-permute-start | bytes 24584 | tf_op jit(solution)/shard_map/ppermute | solution.py:676
  122.4 1.9 %collective-permute-start.7 = (f32[16,128]{1,0:T(8,128)}, f32[16,128]{1,0:T(8,128)S(1)}, u32[]{:S(2)}, u32[]{:S(2)}) collective-permute-start(f32[16,128]{1,0:T(8,128)} %get-tuple-element.92), channel_id=1, source_target_pairs={{0,8},{8,0},{16,24},{24,16},{1,9},{9,1},{17,25},{25,17},{2,10},{10... | collective-permute-start | bytes 24584 | tf_op jit(solution)/shard_map/ppermute | solution.py:676
  125.6 11.5 %all-to-all-start.4 = ((f32[8,16,128]{2,1,0:T(8,128)}), f32[8,16,128]{2,1,0:T(8,128)S(1)}, u32[]{:S(2)}, u32[]{:S(2)}) async-start(f32[8,16,128]{2,1,0:T(8,128)} %broadcast_in_dim.2), calls=%async_computation.4 | async-start | bytes 131072 | tf_op jit(solution)/shard_map/all_to_all | solution.py:680
